TPU v7x, 32 devices: a whole 2x2x4 slice. The times are simulated.
32 devices in a mesh: rep: 2 (over x), dp: 4 (over z), tp: 4 (over y, core).
Axes of the slice: x: 2, y: 2, z: 4, core: 2. Of those that a mesh axis runs over, the one named last changes fastest.
Arguments:
- attention_output: bfloat16 [4, 1024, 8192], P(None, ('rep', 'dp'), 'tp'), parts along dimension 1, may hold values from -6 to 6
- output_projection_weight: bfloat16 [8192, 8192], P('tp'), may hold values from -0.09375 to 0.09375
- shrink_matrix_store: bfloat16 [256, 16, 8192], P('dp', None, 'tp'), may hold values from -0.0625 to 0.0625
- expand_matrix_store: bfloat16 [256, 16, 8192], P('dp', None, 'tp'), may hold values from -1.5 to 1.5
- segment_adapter: int32 [4, 64], P(None, ('rep', 'dp')), parts along dimension 1, may hold values from 0 to 255, as said below
- segment_live_rows: int32 [4, 64], P(None, ('rep', 'dp')), parts along dimension 1, may hold values from 1 to 16, as said below
- adapter_store_index: int32 [512], P('rep'), parts along dimension 0, may hold values from 0 to 255, as said below
Outputs:
- projected: bfloat16 [4, 1024, 8192], P(None, ('rep', 'dp'), 'tp'), parts along dimension 1
There are 2 independent parts, one for each index of `rep`. A program takes and returns all parts, laid end to end along the dimension named above; an argument that names none is the same for every part. Nothing has to cross between parts.
Inputs may be any that keep to these rules, and one draw needn't show every extreme that they name: `segment_adapter`: adapter stored at position p lies on index p // 64 of dp. Over all 4 steps, the segments of one index of dp name adapters of which at most 16 lie on any one index of dp, and exactly 16 lie on one of them. `segment_live_rows`: every step of every index of dp has a segment with all 16 rows live. `adapter_store_index`: A permutation: each store position holds one adapter.
All inputs are finite; a program needn't handle non-finite values.
Results may differ from a plain program's by a relative error of at most 0.0095.
Values may be sent and summed in bfloat16 or wider, within the bound.
No kernel may reach another device: no remote copies, remote signals or barrier semaphores. Data moves between devices by JAX's collectives and lax.ppermute only.
A program may use at most 192 MiB of HBM per device.

v0:
```python
import functools

import jax
import jax.numpy as jnp
from jax import lax
from jax.experimental import pallas as pl
from jax.experimental.pallas import tpu as pltpu
from jax.sharding import PartitionSpec as P

NEAR = 208
OWN = 72
SHARED = 64
ROUND = 64
META = 128
RELAY = -1
VMEM = 48 * 2**20
FREE = pl.CostEstimate(flops=0, bytes_accessed=0, transcendentals=0)


def group_of(shape):
    return lax.broadcasted_iota(jnp.int32, shape, 1) // 16


def row_of(shape):
    return lax.broadcasted_iota(jnp.int32, shape, 0) % 8


def fold(v):
    for shift in (64, 32, 16):
        v = v + pltpu.roll(v, shift, axis=1)
    return v


def score_kernel(dists, *refs):
    m = len(dists)
    got, known, a_ref = refs[:m], refs[m:-m - 3], refs[-m - 3]
    out_ref, slots, acc = refs[-m - 2], refs[-m - 1:-1], refs[-1]
    g = pl.program_id(0)
    per, width = a_ref.shape[0] // 16, a_ref.shape[1]

    @pl.when(g == 0)
    def _():
        acc[...] = jnp.zeros_like(acc)
        for i, dist in enumerate(dists):
            if dist is None:
                slots[i][...] = known[0][...]
            else:
                meta = got[i][:, width:].astype(jnp.float32).astype(jnp.int32)
                if dist == RELAY:
                    dist = (2 + lax.broadcasted_iota(jnp.int32, (meta.shape[0], 1), 0) // SHARED) ^ 1
                slots[i][...] = jnp.where(meta[:, 1:2] == dist, meta[:, 0:1] - 1, -1)

    off = 0
    for i in range(m):
        n = got[i].shape[0]
        s = lax.dot_general(
            got[i][:, :width], a_ref[...], (((1,), (1,)), ((), ())), preferred_element_type=jnp.float32
        )
        s = jnp.where(group_of(s.shape) + g * per == slots[i][...], s, 0.0)
        v = s[:, :128]
        for c in range(128, s.shape[1], 128):
            v = v + s[:, c:c + 128]
        acc[off:off + n, :] += v
        off += n

    @pl.when(g == pl.num_programs(0) - 1)
    def _():
        off = 0
        for i in range(m):
            n = got[i].shape[0]
            v = fold(acc[off:off + n, :])
            v = jnp.where(group_of(v.shape) == row_of(v.shape), v, 0.0)
            out_ref[off // 8:(off + n) // 8, :] = jnp.sum(v.reshape(n // 8, 8, 128), axis=1)
            off += n


def whole(shape):
    return pl.BlockSpec(shape, lambda g: (0, 0))


def scores(dists, got, known, store):
    sizes = [v.shape[0] for v in got]
    total, width = sum(sizes), store.shape[1]
    blk = 256
    out = pl.pallas_call(
        functools.partial(score_kernel, tuple(dists)),
        grid=(store.shape[0] // blk,),
        in_specs=[whole(v.shape) for v in got + known] + [pl.BlockSpec((blk, width), lambda g: (g, 0))],
        out_specs=[whole((total // 8, 128))] + [whole((n, 1)) for n in sizes],
        out_shape=[jax.ShapeDtypeStruct((total // 8, 128), jnp.float32)]
        + [jax.ShapeDtypeStruct((n, 1), jnp.int32) for n in sizes],
        scratch_shapes=[pltpu.VMEM((total, 128), jnp.float32)],
        compiler_params=pltpu.CompilerParams(vmem_limit_bytes=VMEM),
        cost_estimate=FREE,
        name="scores",
    )(*got, *known, store)
    return out[0], list(out[1:])


def spread_out(slots, packed, depth, spread):
    off = 0
    for i in range(len(slots)):
        n = slots[i].shape[0]
        v = packed[off // 8:(off + n) // 8, :]
        v = jnp.broadcast_to(v[:, None, :], (n // 8, 8, 128)).reshape(n, 128)
        group = group_of(v.shape)
        v = fold(jnp.where(group == row_of(v.shape), v, 0.0))
        for c in range(depth // 128):
            hit = group + c * 8 == slots[i][...]
            spread[i][:, c * 128:(c + 1) * 128] = jnp.where(hit, v, 0.0).astype(jnp.bfloat16)
        off += n


def delta_kernel(m, *refs):
    slots, packed, b_ref, outs, spread = refs[:m], refs[m], refs[m + 1], refs[m + 2:-m], refs[-m:]

    @pl.when(pl.program_id(0) == 0)
    def _():
        spread_out(slots, packed, b_ref.shape[0], spread)

    for i in range(m):
        outs[i][...] = jnp.dot(spread[i][...], b_ref[...], preferred_element_type=jnp.float32).astype(jnp.bfloat16)


def direct_kernel(n_dp, me_ref, *refs):
    m = n_dp - 1
    slots, packed, b_ref, outs, spread = refs[:m], refs[m], refs[m + 1], refs[m + 2:-m], refs[-m:]
    me = me_ref[0]

    @pl.when(pl.program_id(0) == 0)
    def _():
        spread_out(slots, packed, b_ref.shape[0], spread)

    block = outs[-1]
    block[me] = jnp.zeros(block.shape[1:], block.dtype)
    for i in range(m):
        v = jnp.dot(spread[i][...], b_ref[...], preferred_element_type=jnp.float32)
        if i < m - 1:
            outs[i][...] = v[:SHARED].astype(jnp.bfloat16)
            block[me ^ (i + 2)] = v[SHARED:].astype(jnp.bfloat16)
        else:
            block[me ^ 1] = v[:OWN].astype(jnp.bfloat16)
            outs[i][...] = v[OWN:].astype(jnp.bfloat16)


def deltas(slots, packed, store, me=None, n_dp=None):
    depth, width = store.shape
    cols = width // 4
    part = lambda n: pl.BlockSpec((n, cols), lambda g: (0, g))
    ins = [whole(v.shape) for v in slots] + [whole(packed.shape), part(depth)]
    if me is None:
        kernel, first, args = functools.partial(delta_kernel, len(slots)), [], []
        sizes, shapes = [v.shape[0] for v in slots], []
        outs = [part(n) for n in sizes]
    else:
        kernel, first, args = functools.partial(direct_kernel, n_dp), [pl.BlockSpec(memory_space=pltpu.SMEM)], [me]
        sizes, shapes = [SHARED] * (n_dp - 2) + [NEAR - OWN], [(n_dp, OWN, width)]
        outs = [part(n) for n in sizes] + [pl.BlockSpec((n_dp, OWN, cols), lambda g: (0, 0, g))]
    shapes = [(n, width) for n in sizes] + shapes
    return list(pl.pallas_call(
        kernel,
        grid=(width // cols,),
        in_specs=first + ins,
        out_specs=outs,
        out_shape=[jax.ShapeDtypeStruct(v, jnp.bfloat16) for v in shapes],
        scratch_shapes=[pltpu.VMEM((v.shape[0], depth), jnp.bfloat16) for v in slots],
        compiler_params=pltpu.CompilerParams(vmem_limit_bytes=VMEM),
        cost_estimate=FREE,
        name="deltas",
    )(*args, *slots, packed, store))


def finish_kernel(m, n_dp, me_ref, row_ref, *refs):
    codes, block_codes = refs[:m], refs[m:m + n_dp - 1]
    back, block, adds, out_ref = refs[m + n_dp - 1:2 * m + n_dp - 1], refs[2 * m + n_dp - 1], refs[2 * m + n_dp:-1], refs[-1]
    total = adds[0][...].astype(jnp.float32)
    for v in adds[1:]:
        total += v[...].astype(jnp.float32)
    codes = [c[...] for c in codes + block_codes]
    back = [b[...] for b in back] + [block[me_ref[0] ^ (1 + i)] for i in range(n_dp - 1)]
    for code, b in zip(codes, back):
        put = jnp.where(row_ref[...] == code, 1.0, 0.0).astype(jnp.bfloat16)
        total += jnp.dot(put, b, preferred_element_type=jnp.float32)
    out_ref[...] = total.astype(out_ref.dtype)


def finish(me, row_code, codes, block_codes, back, block, adds):
    rows, width = adds[0].shape
    cols = width // 4
    n_dp = block.shape[0]
    part = lambda v: pl.BlockSpec((v.shape[0], cols), lambda g: (0, g))
    return pl.pallas_call(
        functools.partial(finish_kernel, len(codes), n_dp),
        grid=(width // cols,),
        in_specs=[pl.BlockSpec(memory_space=pltpu.SMEM), whole(row_code.shape)]
        + [whole(v.shape) for v in codes + block_codes] + [part(v) for v in back]
        + [pl.BlockSpec((n_dp, OWN, cols), lambda g: (0, 0, g))] + [part(v) for v in adds],
        out_specs=pl.BlockSpec((rows, cols), lambda g: (0, g)),
        out_shape=jax.ShapeDtypeStruct((rows, width), jnp.bfloat16),
        compiler_params=pltpu.CompilerParams(vmem_limit_bytes=VMEM),
        name="finish",
    )(me, row_code, *codes, *block_codes, *back, block, *adds)


def column(row):
    n = row.shape[1]
    eye = lax.broadcasted_iota(jnp.int32, (n, n), 0) == lax.broadcasted_iota(jnp.int32, (n, n), 1)
    return jnp.sum(jnp.where(eye, jnp.broadcast_to(row, (n, n)), 0), axis=1, keepdims=True)


def row(col):
    n = col.shape[0]
    eye = lax.broadcasted_iota(jnp.int32, (n, n), 0) == lax.broadcasted_iota(jnp.int32, (n, n), 1)
    return jnp.sum(jnp.where(eye, jnp.broadcast_to(col, (n, n)), 0), axis=0, keepdims=True)


def segments(pos, alive, device, shift):
    n = pos.shape[1]
    dist = (pos >> shift) ^ device
    i = lax.broadcasted_iota(jnp.int32, (n, n), 0)
    j = lax.broadcasted_iota(jnp.int32, (n, n), 1)
    before = (column(dist) == dist) & (i < j)
    start = jnp.sum(jnp.where(before, column(alive), 0), axis=0, keepdims=True)
    return dist, start


def total(dist, alive, j):
    return jnp.sum(jnp.where(dist == j, alive, 0), axis=1, keepdims=True)


def over_of(dist, alive, j):
    return jnp.maximum(total(dist, alive, j - j % 2) - OWN, 0)


def iota_of(n, axis):
    return lax.broadcasted_iota(jnp.int32, (n, 1) if axis == 0 else (1, n), axis)


def near_code(big, axis):
    return big + iota_of(NEAR, axis)


def own_code(big, j, axis):
    return j * big + iota_of(OWN, axis)


def shared_code(big, j, over, axis):
    f = iota_of(SHARED, axis) + (j % 2) * SHARED
    even = j - j % 2
    return OWN + jnp.where(f < over, even * big + f, (even + 1) * big + f - over)


def far_code(big, j, over, axis):
    f = iota_of(SHARED + OWN, axis)
    g = f + (j % 2) * SHARED
    even = j - j % 2
    code = OWN + jnp.where(g < over, even * big + g, (even + 1) * big + g - over)
    return jnp.where(f < SHARED, code, j * big + f - SHARED)


def pack_kernel(n_dp, seg_len, shift, me_ref, ids_ref, lives_ref, index_ref, x_ref,
                table_ref, row_ref, self_ref, meta_ref, *outs):
    me = me_ref[0]
    count, (rows, width) = ids_ref.shape[1], x_ref.shape
    big = 2 * rows
    lives = lives_ref[...]
    hit = column(ids_ref[...]) == lax.broadcasted_iota(jnp.int32, (count, index_ref.shape[1]), 1)
    pos = row(jnp.sum(jnp.where(hit, index_ref[...], 0), axis=1, keepdims=True))
    table_ref[0:1, :] = pos
    table_ref[1:2, :] = lives
    dist, start = segments(pos, lives, me, shift)
    code = dist * big + start
    slot = pos & ((1 << shift) - 1)

    def spread(value, axis):
        shape = (count, rows) if axis == 1 else (rows, count)
        r = lax.broadcasted_iota(jnp.int32, shape, axis)
        seg = lax.broadcasted_iota(jnp.int32, shape, 1 - axis)
        v = column(value) if axis == 1 else value
        return jnp.sum(jnp.where(r // seg_len == seg, v, 0), axis=1 - axis, keepdims=True)

    def rows_code(axis):
        lane = iota_of(rows, axis) % seg_len
        return jnp.where(lane < spread(lives, axis), spread(code, axis) + lane, -1)

    by_row, by_lane = rows_code(0), rows_code(1)
    row_slot, row_dist = spread(slot, 0), spread(dist, 0)
    row_ref[...] = by_row
    self_ref[...] = jnp.where((by_row >= 0) & (row_dist == 0), row_slot, -1)
    lane = lax.broadcasted_iota(jnp.int32, (rows, META), 1)
    meta = jnp.where(lane == 0, row_slot + 1, jnp.where(lane == 1, row_dist, 0))
    meta = meta.astype(jnp.float32).astype(jnp.bfloat16)
    meta_ref[...] = meta

    left = total(dist, lives, 1) - NEAR
    for j in range(2, n_dp):
        held = OWN + 2 * SHARED if j % 2 == 0 else OWN + jnp.maximum(2 * SHARED - over_of(dist, lives, j), 0)
        left = jnp.maximum(left, total(dist, lives, j) - held)
    rounds = ((jnp.maximum(left, 0) + ROUND - 1) // ROUND).astype(jnp.float32)
    told = jnp.where(lax.broadcasted_iota(jnp.int32, (1, META), 1) == 2, rounds, 0.0)

    far = range(2, n_dp)
    codes = [far_code(big, j, over_of(dist, lives, j), 0) for j in far] + [near_code(big, 0)]
    m = len(codes)
    for c, out in zip(codes, outs[:m]):
        pick = jnp.where(c == by_lane, 1.0, 0.0).astype(jnp.bfloat16)
        out[:, :width] = jnp.dot(pick, x_ref[...], preferred_element_type=jnp.float32).astype(jnp.bfloat16)
        out[:, width:] = (jnp.dot(pick, meta, preferred_element_type=jnp.float32) + told).astype(jnp.bfloat16)
    lanes = [shared_code(big, j, over_of(dist, lives, j), 1) for j in far]
    lanes += [big + OWN + iota_of(NEAR - OWN, 1)]
    lanes += [own_code(big, j, 1) for j in range(1, n_dp)]
    for c, out in zip(lanes, outs[m:]):
        out[...] = c


def vmem(count):
    return [pl.BlockSpec(memory_space=pltpu.VMEM) for _ in range(count)]


def packs(me, ids, lives, index, x, n_dp, seg_len, shift):
    count, (rows, width) = ids.shape[1], x.shape
    sizes = [SHARED + OWN] * (n_dp - 2) + [NEAR]
    parts = [SHARED] * (n_dp - 2) + [NEAR - OWN] + [OWN] * (n_dp - 1)
    shapes = [((2, count), jnp.int32), ((rows, 1), jnp.int32), ((rows, 1), jnp.int32)]
    shapes += [((rows, META), jnp.bfloat16)]
    shapes += [((n, width + META), jnp.bfloat16) for n in sizes] + [((1, n), jnp.int32) for n in parts]
    return pl.pallas_call(
        functools.partial(pack_kernel, n_dp, seg_len, shift),
        in_specs=[pl.BlockSpec(memory_space=pltpu.SMEM)] + vmem(4),
        out_specs=vmem(len(shapes)),
        out_shape=[jax.ShapeDtypeStruct(*v) for v in shapes],
        compiler_params=pltpu.CompilerParams(vmem_limit_bytes=VMEM),
        cost_estimate=FREE,
        name="pack",
    )(me, ids, lives, index, x)


def share_kernel(at_ref, x_ref, w_ref, out_ref):
    out_ref[...] = jnp.dot(x_ref[...], w_ref[...], preferred_element_type=jnp.float32).astype(jnp.bfloat16)


def share(at, x, weight, cols):
    rows, depth = x.shape
    tile = min(512, cols)
    return pl.pallas_call(
        share_kernel,
        grid_spec=pltpu.PrefetchScalarGridSpec(
            num_scalar_prefetch=1,
            grid=(cols // tile,),
            in_specs=[
                pl.BlockSpec((rows, depth), lambda g, at: (0, 0)),
                pl.BlockSpec((depth, tile), lambda g, at: (0, at[0] * (cols // tile) + g)),
            ],
            out_specs=pl.BlockSpec((rows, tile), lambda g, at: (0, g)),
        ),
        out_shape=jax.ShapeDtypeStruct((rows, cols), jnp.bfloat16),
        compiler_params=pltpu.CompilerParams(vmem_limit_bytes=VMEM),
        cost_estimate=FREE,
        name="share",
    )(at, x, weight)


def per_device(
    attention_output,
    output_projection_weight,
    shrink_matrix_store,
    expand_matrix_store,
    segment_adapter,
    segment_live_rows,
    adapter_store_index,
):
    steps, rows_dev, width = attention_output.shape
    seg_count = segment_adapter.shape[1]
    seg_len = rows_dev // seg_count
    store, rank, _ = shrink_matrix_store.shape
    n_dp, n_tp = lax.axis_size("dp"), lax.axis_size("tp")
    me = lax.axis_index("dp").reshape(1)
    rows = steps * rows_dev
    count = steps * seg_count
    shift = store.bit_length() - 1
    big = 2 * rows
    far = range(2, n_dp)

    x = attention_output.reshape(rows, width)
    shrink_store = shrink_matrix_store.reshape(store * rank, width)
    expand_store = expand_matrix_store.reshape(store * rank, width)
    weight = output_projection_weight

    def swap(v, axis, k):
        n = lax.axis_size(axis)
        return lax.ppermute(v, axis, [(i, i ^ k) for i in range(n)])

    def butterfly(v, axis, op):
        k = 1
        while k < lax.axis_size(axis):
            v = op(v, swap(v, axis, k))
            k *= 2
        return v

    def answer(dists, got, known=()):
        scored, slots = scores(dists, got, list(known), shrink_store)
        return slots, butterfly(scored, "tp", jnp.add)

    def after(v, *others):
        return lax.optimization_barrier((v, others))[0]

    packed = list(packs(
        me,
        segment_adapter.reshape(1, count),
        segment_live_rows.reshape(1, count),
        adapter_store_index.reshape(1, -1),
        x, n_dp, seg_len, shift,
    ))
    table, row_code, self_slots, meta = packed[:4]
    m = len(far)
    out_far, out_near = packed[4:4 + m], packed[4 + m]
    codes, block_codes = packed[5 + m:6 + 2 * m], packed[6 + 2 * m:]

    in_far = [swap(v, "dp", j) for v, j in zip(out_far, far)]
    in_near = swap(out_near, "dp", 1)

    found, self_part = answer([None], [after(x, table)], [self_slots])
    (self_delta,) = deltas(found, self_part, expand_store)

    at = after(lax.axis_index("tp").reshape(1), table)
    cols = weight.shape[1] // n_tp
    shares = {k: share(at ^ k, x, weight, cols) for k in reversed(range(n_tp))}
    (in_far, in_near, shares), _ = lax.optimization_barrier(((in_far, in_near, shares), self_delta))

    in_relay = swap(jnp.concatenate([v[:SHARED] for v in in_far]), "dp", 1)
    found, part = answer(list(far) + [1], in_far + [in_near])
    direct = deltas(found, part, expand_store, me, n_dp)
    block = lax.all_to_all(direct[-1], "dp", split_axis=0, concat_axis=0, tiled=True)

    adds = {k: [shares[k]] for k in shares}
    for k in range(1, n_tp, 2):
        adds[k ^ 1].append(swap(adds.pop(k)[0], "tp", 1))
    told = [v[0, width + 2] for v in in_far + [in_near, out_near]]
    rounds = functools.reduce(jnp.maximum, told).astype(jnp.int32).reshape(1, 1)
    rounds = butterfly(rounds, "rep", jnp.maximum)

    found, part = answer([RELAY], [after(in_relay, direct)])
    part, adds, rounds = lax.optimization_barrier((part, adds, rounds))
    rounds = rounds[0, 0]
    (relayed,) = deltas(found, part, expand_store)
    relayed = swap(relayed, "dp", 1)
    bit = 2
    while bit < n_tp:
        for k in sorted((k for k in adds if k & bit), reverse=True):
            v = functools.reduce(jnp.add, [u.astype(jnp.float32) for u in adds.pop(k)])
            adds[k ^ bit].append(swap(v.astype(jnp.bfloat16), "tp", bit))
        bit *= 2
    near, _ = lax.optimization_barrier((direct[m], relayed))
    back = [swap(direct[i] + relayed[i * SHARED:(i + 1) * SHARED], "dp", j) for i, j in enumerate(far)]
    back.append(swap(near, "dp", 1))
    adds = adds[0] + [self_delta]

    def rest():
        pos, alive = table[0], table[1]
        dist = (pos >> shift) ^ me[0]
        held = [None, jnp.int32(NEAR)]
        for j in range(2, n_dp, 2):
            extra = jnp.maximum(jnp.sum(jnp.where(dist == j, alive, 0)) - OWN, 0)
            held += [jnp.int32(OWN + 2 * SHARED), OWN + jnp.maximum(2 * SHARED - extra, 0)]
        x_meta = jnp.concatenate([x, meta], axis=1)

        def body(i, extra):
            code = [j * big + held[j] + i * ROUND + jnp.arange(ROUND, dtype=jnp.int32) for j in range(1, n_dp)]
            got = []
            for j, c in zip(range(1, n_dp), code):
                pick = (c[:, None] == row_code.reshape(1, rows)).astype(jnp.bfloat16)
                v = jnp.dot(pick, x_meta, preferred_element_type=jnp.float32).astype(jnp.bfloat16)
                got.append(swap(v, "dp", j))
            found, part = answer(list(range(1, n_dp)), got)
            for j, c, v in zip(range(1, n_dp), code, deltas(found, part, expand_store)):
                put = (row_code == c[None, :]).astype(jnp.bfloat16)
                extra = extra + jnp.dot(put, swap(v, "dp", j), preferred_element_type=jnp.float32)
            return extra

        extra = lax.fori_loop(0, rounds, body, jnp.zeros((rows, width), jnp.float32))
        return finish(me, row_code, codes, block_codes, back, block, adds + [extra])

    out = lax.cond(rounds > 0, rest, lambda: finish(me, row_code, codes, block_codes, back, block, adds))
    return out.reshape(steps, rows_dev, width)


def solution(mesh):
    return jax.shard_map(
        per_device,
        mesh=mesh,
        in_specs=(
            P(None, ("rep", "dp"), "tp"),
            P("tp", None),
            P("dp", None, "tp"),
            P("dp", None, "tp"),
            P(None, ("rep", "dp")),
            P(None, ("rep", "dp")),
            P("rep"),
        ),
        out_specs=P(None, ("rep", "dp"), "tp"),
        check_vma=False,
    )
```

profile of v0, /device:TPU:0, one launch (start us, length us, event | category | flops | bytes accessed | tf_op | source)
XLA Modules:
  0.0 170.1 jit_solution(3977014069382481817)
XLA Ops:
  2.2 4.1 %pack.1 = (s32[2,32]{1,0:T(2,128)}, s32[512,1]{1,0:T(8,128)S(1)}, s32[512,1]{1,0:T(8,128)S(1)}, bf16[512,128]{1,0:T(8,128)(2,1)}, bf16[136,2176]{1,0:T(8,128)(2,...) custom-call(s32[1]{0:T(128)} %bitcast.3.me_ref, ...), custom_call_target="tpu_custom_call" | custom-call | tf_op jit(solution)/shard_map/pack/pallas_call | solution.py:327
  6.4 3.0 %collective-permute-start.10 = (bf16[208,2176]{1,0:T(8,128)(2,1)S(1)}, bf16[208,2176]{1,0:T(8,128)(2,1)S(1)}, u32[]{:S(2)}, u32[]{:S(2)}) collective-permute-start(bf16[208,2176]{1,0:T(8,128)(2,1)S(1)} %get-tuple-element.272), channel_id=1, source_target_pairs={{0,4},{4,0},{8,12},{12,8},{1,5},{5,1},{9,13},{13,9},{2,6},{6,2},{1... | collective-permute-start | bytes 2715656 | tf_op jit(solution)/shard_map/ppermute | solution.py:391
  9.4 2.6 %collective-permute-start.8 = (bf16[136,2176]{1,0:T(8,128)(2,1)}, bf16[136,2176]{1,0:T(8,128)(2,1)S(1)}, u32[]{:S(2)}, u32[]{:S(2)}) collective-permute-start(bf16[136,2176]{1,0:T(8,128)(2,1)} %get-tuple-element.270), channel_id=1, source_target_pairs={{0,8},{4,12},{8,0},{12,4},{1,9},{5,13},{9,1},{13,5},{2,10},{6,14},... | collective-permute-start | bytes 1775624 | tf_op jit(solution)/shard_map/ppermute | solution.py:391
  12.0 5.2 %scores.6 = (f32[64,128]{1,0:T(8,128)S(1)}, s32[512,1]{1,0:T(8,128)S(1)}) custom-call(bf16[512,2048]{1,0:T(8,128)(2,1)S(1)} %bitcast.42, s32[512,1]{1,0:T(8,128)S(1)} %get-tuple-element.276.refs_1_, bf16[1024,2048]{1,0:T(8,128)(2,1)} %bitcast.31), custom_call_target="tpu_custom_call" | custom-call | tf_op jit(solution)/shard_map/scores/pallas_call | solution.py:85
  17.2 1.2 collective-permute-done.11
  18.4 1.7 %collective-permute-start.12 = (f32[64,128]{1,0:T(8,128)S(1)}, f32[64,128]{1,0:T(8,128)}, u32[]{:S(2)}, u32[]{:S(2)}) collective-permute-start(f32[64,128]{1,0:T(8,128)S(1)} %add.133), channel_id=1, source_target_pairs={{0,2},{1,3},{2,0},{3,1},{4,6},{5,7},{6,4},{7,5},{8,10},{9,11},{10,... | collective-permute-start | bytes 98312 | tf_op jit(solution)/shard_map/ppermute | solution.py:391
  20.2 9.0 %share.4 = bf16[512,2048]{1,0:T(8,128)(2,1)} custom-call(s32[1]{0:T(128)} %bitcast.6.at_ref, bf16[512,2048]{1,0:T(8,128)(2,1)} %bitcast.40, bf16[2048,8192]{1,0:T(8,128)(2,1)} %w_ref.7), custom_call_target="tpu_custom_call" | custom-call | tf_op jit(solution)/shard_map/share/pallas_call | solution.py:345
  29.2 7.1 %share.5 = bf16[512,2048]{1,0:T(8,128)(2,1)S(1)} custom-call(s32[1]{0:T(128)S(6)} %xor.16.at_ref, bf16[512,2048]{1,0:T(8,128)(2,1)S(1)} %bitcast.43, bf16[2048,8192]{1,0:T(8,128)(2,1)} %w_ref.7), custom_call_target="tpu_custom_call" | custom-call | tf_op jit(solution)/shard_map/share/pallas_call | solution.py:345
  36.3 7.1 %share.6 = bf16[512,2048]{1,0:T(8,128)(2,1)S(1)} custom-call(s32[1]{0:T(128)S(6)} %xor.17.at_ref, bf16[512,2048]{1,0:T(8,128)(2,1)S(1)} %bitcast.44, bf16[2048,8192]{1,0:T(8,128)(2,1)} %w_ref.7), custom_call_target="tpu_custom_call" | custom-call | tf_op jit(solution)/shard_map/share/pallas_call | solution.py:345
  43.5 7.1 %share.7 = bf16[512,2048]{1,0:T(8,128)(2,1)S(1)} custom-call(s32[1]{0:T(128)S(6)} %xor.18.at_ref, bf16[512,2048]{1,0:T(8,128)(2,1)S(1)} %bitcast.45, bf16[2048,8192]{1,0:T(8,128)(2,1)} %w_ref.7), custom_call_target="tpu_custom_call" | custom-call | tf_op jit(solution)/shard_map/share/pallas_call | solution.py:345
  51.4 6.7 %deltas.6 = bf16[512,2048]{1,0:T(8,128)(2,1)} custom-call(s32[512,1]{1,0:T(8,128)S(1)} %get-tuple-element.277.refs_0_, f32[64,128]{1,0:T(8,128)S(1)} %add.134.refs_1_, bf16[1024,2048]{1,0:T(8,128)(2,1)} %bitcast.35), custom_call_target="tpu_custom_call" | custom-call | tf_op jit(solution)/shard_map/deltas/pallas_call | solution.py:160
  58.8 5.9 %collective-permute-start.13 = (bf16[128,2176]{1,0:T(8,128)(2,1)S(1)}, bf16[128,2176]{1,0:T(8,128)(2,1)S(1)}, u32[]{:S(2)}, u32[]{:S(2)}) collective-permute-start(bf16[128,2176]{1,0:T(8,128)(2,1)S(1)} %pad_maximum_fusion.1), channel_id=1, source_target_pairs={{0,4},{4,0},{8,12},{12,8},{1,5},{5,1},{9,13},{13,9},{2,6},{6,2},{1... | collective-permute-start | bytes 1671176 | tf_op jit(solution)/shard_map/ppermute | solution.py:391
  64.7 5.3 %scores.7 = (f32[60,128]{1,0:T(8,128)S(1)}, s32[136,1]{1,0:T(8,128)S(1)}, s32[136,1]{1,0:T(8,128)S(1)}, s32[208,1]{1,0:T(8,128)S(1)}) custom-call(bf16[136,2176]{1,0:T(8,128)(2,1)S(1)} %collective-permute-done.8.refs_0_, bf16[136,2176]{1,0:T(8,128)(2,1)S(1)} %collective-permute-done.9.refs_1_, bf16[208,2176]{1,0:T(8,128)(2,1)S(1)} %collective-permute-done.10.refs_2_, ...), custom_call_target="tpu_custom_call" | custom-call | tf_op jit(solution)/shard_map/scores/pallas_call | solution.py:85
  70.1 1.2 collective-permute-done.14
  71.3 1.5 collective-permute-start.15
  72.8 2.4 %collective-permute-done.15 = f32[60,128]{1,0:T(8,128)S(1)} collective-permute-done((f32[60,128]{1,0:T(8,128)S(1)}, f32[60,128]{1,0:T(8,128)S(1)}, u32[]{:S(2)}, u32[]{:S(2)}) %collective-permute-start.15) | collective-permute-done | bytes 30752 | tf_op jit(solution)/shard_map/ppermute | solution.py:391
  75.2 6.6 %deltas.7 = (bf16[64,2048]{1,0:T(8,128)(2,1)S(1)}, bf16[64,2048]{1,0:T(8,128)(2,1)S(1)}, bf16[136,2048]{1,0:T(8,128)(2,1)S(1)}, bf16[4,72,2048]{2,1,0:T(8,128)(2,1)}) custom-call(s32[1]{0:T(128)} %bitcast.3.me_ref, s32[136,1]{1,0:T(8,128)S(1)} %get-tuple-element.282.refs_0_, s32[136,1]{1,0:T(8,128)S(1)} %get-tuple-element.283.refs_1_, ...), custom_call_target="tpu_custom_call" | custom-call | tf_op jit(solution)/shard_map/deltas/pallas_call | solution.py:160
  81.8 2.4 %scores.8 = (f32[16,128]{1,0:T(8,128)S(1)}, s32[128,1]{1,0:T(8,128)S(1)}) custom-call(bf16[128,2176]{1,0:T(8,128)(2,1)S(1)} %collective-permute-done.13.refs_0_, bf16[1024,2048]{1,0:T(8,128)(2,1)S(1)} %bitcast.34), custom_call_target="tpu_custom_call" | custom-call | tf_op jit(solution)/shard_map/scores/pallas_call | solution.py:85
  85.4 1.5 collective-permute-start.17
  87.0 1.3 slice.35
  92.7 2.9 %collective-permute-start.20 = (s32[1,1]{1,0:T(1,128)}, s32[1,1]{1,0:T(1,128)}, u32[]{:S(2)}, u32[]{:S(2)}) collective-permute-start(s32[1,1]{1,0:T(1,128)} %convert_element_type.37), channel_id=1, source_target_pairs={{0,16},{16,0},{1,17},{17,1},{2,18},{18,2},{3,19},{19,3},{4,20},{20... | collective-permute-start | bytes 20 | tf_op jit(solution)/shard_map/ppermute | solution.py:391
  97.0 3.9 %add_convert_fusion = bf16[512,2048]{1,0:T(8,128)(2,1)} fusion(bf16[512,2048]{1,0:T(8,128)(2,1)} %collective-permute-done.19, bf16[512,2048]{1,0:T(8,128)(2,1)S(1)} %share.6), kind=kLoop, calls=%fused_computation.31 | loop fusion | flops 4194304 | bytes 6291456 | tf_op jit(solution)/shard_map/convert_element_type | solution.py:451
  101.3 3.7 %all-to-all-start = ((bf16[4,72,2048]{2,1,0:T(8,128)(2,1)}), bf16[4,72,2048]{2,1,0:T(8,128)(2,1)S(1)}, u32[]{:S(2)}, u32[]{:S(2)}) async-start(bf16[4,72,2048]{2,1,0:T(8,128)(2,1)} %get-tuple-element.289), calls=%async_computation | async-start | bytes 2359296 | tf_op jit(solution)/shard_map/all_to_all | solution.py:433
  105.1 3.9 %deltas.8 = bf16[128,2048]{1,0:T(8,128)(2,1)S(1)} custom-call(s32[128,1]{1,0:T(8,128)S(1)} %get-tuple-element.304.refs_0_, f32[16,128]{1,0:T(8,128)S(1)} %add.138.refs_1_, bf16[1024,2048]{1,0:T(8,128)(2,1)} %bitcast.37), custom_call_target="tpu_custom_call" | custom-call | tf_op jit(solution)/shard_map/deltas/pallas_call | solution.py:160
  109.0 2.1 %collective-permute-start.21 = (bf16[128,2048]{1,0:T(8,128)(2,1)S(1)}, bf16[128,2048]{1,0:T(8,128)(2,1)S(1)}, u32[]{:S(2)}, u32[]{:S(2)}) collective-permute-start(bf16[128,2048]{1,0:T(8,128)(2,1)S(1)} %deltas.8), channel_id=1, source_target_pairs={{0,4},{4,0},{8,12},{12,8},{1,5},{5,1},{9,13},{13,9},{2,6},{6,2},{1... | collective-permute-start | bytes 1572872 | tf_op jit(solution)/shard_map/ppermute | solution.py:391
  111.1 25.4 %collective-permute-done.21 = bf16[128,2048]{1,0:T(8,128)(2,1)S(1)} collective-permute-done((bf16[128,2048]{1,0:T(8,128)(2,1)S(1)}, bf16[128,2048]{1,0:T(8,128)(2,1)S(1)}, u32[]{:S(2)}, u32[]{:S(2)}) %collective-permute-start.21) | collective-permute-done | bytes 524320 | tf_op jit(solution)/shard_map/ppermute | solution.py:391
  137.7 3.4 %collective-permute-start.23 = (bf16[64,2048]{1,0:T(8,128)(2,1)}, bf16[64,2048]{1,0:T(8,128)(2,1)S(1)}, u32[]{:S(2)}, u32[]{:S(2)}) collective-permute-start(bf16[64,2048]{1,0:T(8,128)(2,1)} %get-tuple-element.337), channel_id=1, source_target_pairs={{0,12},{4,8},{8,4},{12,0},{1,13},{5,9},{9,5},{13,1},{2,14},{6,10},... | collective-permute-start | bytes 786440 | tf_op jit(solution)/shard_map/ppermute | solution.py:391
  141.1 17.9 %collective-permute-done.23 = bf16[64,2048]{1,0:T(8,128)(2,1)S(1)} collective-permute-done((bf16[64,2048]{1,0:T(8,128)(2,1)}, bf16[64,2048]{1,0:T(8,128)(2,1)S(1)}, u32[]{:S(2)}, u32[]{:S(2)}) %collective-permute-start.23) | collective-permute-done | bytes 262176 | tf_op jit(solution)/shard_map/ppermute | solution.py:391
  159.0 2.8 %collective-permute-done.22 = bf16[64,2048]{1,0:T(8,128)(2,1)S(1)} collective-permute-done((bf16[64,2048]{1,0:T(8,128)(2,1)S(1)}, bf16[64,2048]{1,0:T(8,128)(2,1)S(1)}, u32[]{:S(2)}, u32[]{:S(2)}) %collective-permute-start.22) | collective-permute-done | bytes 262176 | tf_op jit(solution)/shard_map/ppermute | solution.py:391
  161.9 6.9 %conditional.1 = (bf16[4,128,2048]{2,1,0:T(8,128)(2,1)S(1)}) conditional(s32[]{:T(128)} %convert_element_type.38, (s32[1]{0:T(128)}, s32[512,1]{1,0:T(8,128)S(1)}, s32[1,64]{1,0:T(1,128)S(1)}, s32[1,64]{1,0:T(1,128)S(1)}, s32[1,136]{1,0:T(1,128)S(1)}, /*index=5*/s32[1,72]{1,0:T(1,128)S(1)}, s32[1,72]{1,0:T(1,128)S(1)}, s32[1,72]{1,0:T(1,128)S(1)}, ...), branch_computations={%region_0.0_spmd, %region_1.5_spmd} | conditional | flops 838695296 | bytes 105958760 | solution.py:483
  161.9 6.8 %finish.2 = bf16[512,2048]{1,0:T(8,128)(2,1)S(1)} custom-call(s32[1]{0:T(128)} %get-tuple-element.171.me_ref, s32[512,1]{1,0:T(8,128)S(1)} %get-tuple-element.172.row_ref, s32[1,64]{1,0:T(1,128)S(1)} %get-tuple-element.173.refs_0_, s32[1,64]{1,0:T(1,128)S(1)} %get-tuple-element.174.refs_1_, s32[1,136]{1,0:T(1,128)S(1)} %get-tuple-element.175.refs_2_, ...), custom_call_target="tpu_custom_call" | custom-call | tf_op jit(solution)/shard_map/cond/branch_0_fun/finish/pallas_call | solution.py:192
  168.8 1.3 copy-done.10
  (62 shorter events, 9.4 us)
Async XLA Ops:
  1.5 0.7 copy-start
  2.2 9.8 %copy-start.6 = (bf16[4,128,2048]{2,1,0:T(8,128)(2,1)S(1)}, bf16[4,128,2048]{2,1,0:T(8,128)(2,1)}, u32[]{:S(2)}) copy-start(bf16[4,128,2048]{2,1,0:T(8,128)(2,1)} %param.11) | copy-start | bytes 6291460
  6.4 10.8 %copy-start.1 = (bf16[208,2176]{1,0:T(8,128)(2,1)}, bf16[208,2176]{1,0:T(8,128)(2,1)S(1)}, u32[]{:S(2)}) copy-start(bf16[208,2176]{1,0:T(8,128)(2,1)S(1)} %get-tuple-element.272) | copy-start | bytes 2715652
  6.4 51.8 %collective-permute-start.10 = (bf16[208,2176]{1,0:T(8,128)(2,1)S(1)}, bf16[208,2176]{1,0:T(8,128)(2,1)S(1)}, u32[]{:S(2)}, u32[]{:S(2)}) collective-permute-start(bf16[208,2176]{1,0:T(8,128)(2,1)S(1)} %get-tuple-element.272), channel_id=1, source_target_pairs={{0,4},{4,0},{8,12},{12,8},{1,5},{5,1},{9,13},{13,9},{2,6},{6,2},{1... | collective-permute-start | bytes 2715656 | tf_op jit(solution)/shard_map/ppermute | solution.py:391
  9.4 48.7 %collective-permute-start.8 = (bf16[136,2176]{1,0:T(8,128)(2,1)}, bf16[136,2176]{1,0:T(8,128)(2,1)S(1)}, u32[]{:S(2)}, u32[]{:S(2)}) collective-permute-start(bf16[136,2176]{1,0:T(8,128)(2,1)} %get-tuple-element.270), channel_id=1, source_target_pairs={{0,8},{4,12},{8,0},{12,4},{1,9},{5,13},{9,1},{13,5},{2,10},{6,14},... | collective-permute-start | bytes 1775624 | tf_op jit(solution)/shard_map/ppermute | solution.py:391
  12.0 46.1 %collective-permute-start.9 = (bf16[136,2176]{1,0:T(8,128)(2,1)}, bf16[136,2176]{1,0:T(8,128)(2,1)S(1)}, u32[]{:S(2)}, u32[]{:S(2)}) collective-permute-start(bf16[136,2176]{1,0:T(8,128)(2,1)} %get-tuple-element.271), channel_id=1, source_target_pairs={{0,12},{4,8},{8,4},{12,0},{1,13},{5,9},{9,5},{13,1},{2,14},{6,10},... | collective-permute-start | bytes 1775624 | tf_op jit(solution)/shard_map/ppermute | solution.py:391
  17.2 1.3 collective-permute-start.11
  18.4 32.2 %collective-permute-start.12 = (f32[64,128]{1,0:T(8,128)S(1)}, f32[64,128]{1,0:T(8,128)}, u32[]{:S(2)}, u32[]{:S(2)}) collective-permute-start(f32[64,128]{1,0:T(8,128)S(1)} %add.133), channel_id=1, source_target_pairs={{0,2},{1,3},{2,0},{3,1},{4,6},{5,7},{6,4},{7,5},{8,10},{9,11},{10,... | collective-permute-start | bytes 98312 | tf_op jit(solution)/shard_map/ppermute | solution.py:391
  20.2 9.0 %copy-start.7 = (bf16[4,128,2048]{2,1,0:T(8,128)(2,1)S(1)}, bf16[4,128,2048]{2,1,0:T(8,128)(2,1)}, u32[]{:S(2)}) copy-start(bf16[4,128,2048]{2,1,0:T(8,128)(2,1)} %param.11) | copy-start | bytes 6291460
  51.4 13.3 %copy-start.2 = (bf16[64,16,2048]{2,1,0:T(8,128)(2,1)S(1)}, bf16[64,16,2048]{2,1,0:T(8,128)(2,1)}, u32[]{:S(2)}) copy-start(bf16[64,16,2048]{2,1,0:T(8,128)(2,1)} %param.13) | copy-start | bytes 12582916
  58.1 38.8 %collective-permute-start.18 = (bf16[512,2048]{1,0:T(8,128)(2,1)S(1)}, bf16[512,2048]{1,0:T(8,128)(2,1)}, u32[]{:S(2)}, u32[]{:S(2)}) collective-permute-start(bf16[512,2048]{1,0:T(8,128)(2,1)S(1)} %share.5), channel_id=1, source_target_pairs={{0,1},{1,0},{2,3},{3,2},{4,5},{5,4},{6,7},{7,6},{8,9},{9,8},{10,11... | collective-permute-start | bytes 6291464 | tf_op jit(solution)/shard_map/ppermute | solution.py:391
  58.2 38.7 %collective-permute-start.19 = (bf16[512,2048]{1,0:T(8,128)(2,1)S(1)}, bf16[512,2048]{1,0:T(8,128)(2,1)}, u32[]{:S(2)}, u32[]{:S(2)}) collective-permute-start(bf16[512,2048]{1,0:T(8,128)(2,1)S(1)} %share.7), channel_id=1, source_target_pairs={{0,1},{1,0},{2,3},{3,2},{4,5},{5,4},{6,7},{7,6},{8,9},{9,8},{10,11... | collective-permute-start | bytes 6291464 | tf_op jit(solution)/shard_map/ppermute | solution.py:391
  58.8 23.0 %collective-permute-start.13 = (bf16[128,2176]{1,0:T(8,128)(2,1)S(1)}, bf16[128,2176]{1,0:T(8,128)(2,1)S(1)}, u32[]{:S(2)}, u32[]{:S(2)}) collective-permute-start(bf16[128,2176]{1,0:T(8,128)(2,1)S(1)} %pad_maximum_fusion.1), channel_id=1, source_target_pairs={{0,4},{4,0},{8,12},{12,8},{1,5},{5,1},{9,13},{13,9},{2,6},{6,2},{1... | collective-permute-start | bytes 1671176 | tf_op jit(solution)/shard_map/ppermute | solution.py:391
  70.0 1.3 collective-permute-start.14
  71.3 3.9 %collective-permute-start.15 = (f32[60,128]{1,0:T(8,128)S(1)}, f32[60,128]{1,0:T(8,128)S(1)}, u32[]{:S(2)}, u32[]{:S(2)}) collective-permute-start(f32[60,128]{1,0:T(8,128)S(1)} %add.135), channel_id=1, source_target_pairs={{0,2},{1,3},{2,0},{3,1},{4,6},{5,7},{6,4},{7,5},{8,10},{9,11},{10,... | collective-permute-start | bytes 92168 | tf_op jit(solution)/shard_map/ppermute | solution.py:391
  84.2 1.2 collective-permute-start.16
  85.4 11.5 %collective-permute-start.17 = (f32[16,128]{1,0:T(8,128)S(1)}, f32[16,128]{1,0:T(8,128)S(1)}, u32[]{:S(2)}, u32[]{:S(2)}) collective-permute-start(f32[16,128]{1,0:T(8,128)S(1)} %add.137), channel_id=1, source_target_pairs={{0,2},{1,3},{2,0},{3,1},{4,6},{5,7},{6,4},{7,5},{8,10},{9,11},{10,... | collective-permute-start | bytes 24584 | tf_op jit(solution)/shard_map/ppermute | solution.py:391
  92.7 3.6 %collective-permute-start.20 = (s32[1,1]{1,0:T(1,128)}, s32[1,1]{1,0:T(1,128)}, u32[]{:S(2)}, u32[]{:S(2)}) collective-permute-start(s32[1,1]{1,0:T(1,128)} %convert_element_type.37), channel_id=1, source_target_pairs={{0,16},{16,0},{1,17},{17,1},{2,18},{18,2},{3,19},{19,3},{4,20},{20... | collective-permute-start | bytes 20 | tf_op jit(solution)/shard_map/ppermute | solution.py:391
  100.8 61.0 %collective-permute-start.25 = (bf16[512,2048]{1,0:T(8,128)(2,1)}, bf16[512,2048]{1,0:T(8,128)(2,1)}, u32[]{:S(2)}, u32[]{:S(2)}) collective-permute-start(bf16[512,2048]{1,0:T(8,128)(2,1)} %add_convert_fusion), channel_id=1, source_target_pairs={{0,2},{1,3},{2,0},{3,1},{4,6},{5,7},{6,4},{7,5},{8,10},{9,11},{10,... | collective-permute-start | bytes 6291464 | tf_op jit(solution)/shard_map/ppermute | solution.py:391
  101.3 39.8 %all-to-all-start = ((bf16[4,72,2048]{2,1,0:T(8,128)(2,1)}), bf16[4,72,2048]{2,1,0:T(8,128)(2,1)S(1)}, u32[]{:S(2)}, u32[]{:S(2)}) async-start(bf16[4,72,2048]{2,1,0:T(8,128)(2,1)} %get-tuple-element.289), calls=%async_computation | async-start | bytes 2359296 | tf_op jit(solution)/shard_map/all_to_all | solution.py:433
  105.1 56.8 %copy-start.13 = (s32[1,136]{1,0:T(1,128)S(1)}, s32[1,136]{1,0:T(1,128)}, u32[]{:S(2)}) copy-start(s32[1,136]{1,0:T(1,128)} %get-tuple-element.300) | copy-start | bytes 1636
  105.1 56.8 %copy-start.14 = (s32[1,64]{1,0:T(1,128)S(1)}, s32[1,64]{1,0:T(1,128)}, u32[]{:S(2)}) copy-start(s32[1,64]{1,0:T(1,128)} %get-tuple-element.298) | copy-start | bytes 772
  105.1 56.8 %copy-start.15 = (s32[1,64]{1,0:T(1,128)S(1)}, s32[1,64]{1,0:T(1,128)}, u32[]{:S(2)}) copy-start(s32[1,64]{1,0:T(1,128)} %get-tuple-element.299) | copy-start | bytes 772
  105.1 56.8 %copy-start.16 = (s32[1,72]{1,0:T(1,128)S(1)}, s32[1,72]{1,0:T(1,128)}, u32[]{:S(2)}) copy-start(s32[1,72]{1,0:T(1,128)} %get-tuple-element.301) | copy-start | bytes 868
  105.1 56.8 %copy-start.17 = (s32[1,72]{1,0:T(1,128)S(1)}, s32[1,72]{1,0:T(1,128)}, u32[]{:S(2)}) copy-start(s32[1,72]{1,0:T(1,128)} %get-tuple-element.302) | copy-start | bytes 868
  105.1 56.8 %copy-start.18 = (s32[1,72]{1,0:T(1,128)S(1)}, s32[1,72]{1,0:T(1,128)}, u32[]{:S(2)}) copy-start(s32[1,72]{1,0:T(1,128)} %get-tuple-element.303) | copy-start | bytes 868
  105.1 56.8 %copy-start.19 = (s32[2,32]{1,0:T(2,128)S(1)}, s32[2,32]{1,0:T(2,128)}, u32[]{:S(2)}) copy-start(s32[2,32]{1,0:T(2,128)} %get-tuple-element.273) | copy-start | bytes 772
  109.0 27.4 %collective-permute-start.21 = (bf16[128,2048]{1,0:T(8,128)(2,1)S(1)}, bf16[128,2048]{1,0:T(8,128)(2,1)S(1)}, u32[]{:S(2)}, u32[]{:S(2)}) collective-permute-start(bf16[128,2048]{1,0:T(8,128)(2,1)S(1)} %deltas.8), channel_id=1, source_target_pairs={{0,4},{4,0},{8,12},{12,8},{1,5},{5,1},{9,13},{13,9},{2,6},{6,2},{1... | collective-permute-start | bytes 1572872 | tf_op jit(solution)/shard_map/ppermute | solution.py:391
  136.4 25.4 %collective-permute-start.24 = (bf16[136,2048]{1,0:T(8,128)(2,1)S(1)}, bf16[136,2048]{1,0:T(8,128)(2,1)}, u32[]{:S(2)}, u32[]{:S(2)}) collective-permute-start(bf16[136,2048]{1,0:T(8,128)(2,1)S(1)} %get-tuple-element.306), channel_id=1, source_target_pairs={{0,4},{4,0},{8,12},{12,8},{1,5},{5,1},{9,13},{13,9},{2,6},{6,2},{1... | collective-permute-start | bytes 1671176 | tf_op jit(solution)/shard_map/ppermute | solution.py:391
  137.7 21.3 %collective-permute-start.23 = (bf16[64,2048]{1,0:T(8,128)(2,1)}, bf16[64,2048]{1,0:T(8,128)(2,1)S(1)}, u32[]{:S(2)}, u32[]{:S(2)}) collective-permute-start(bf16[64,2048]{1,0:T(8,128)(2,1)} %get-tuple-element.337), channel_id=1, source_target_pairs={{0,12},{4,8},{8,4},{12,0},{1,13},{5,9},{9,5},{13,1},{2,14},{6,10},... | collective-permute-start | bytes 786440 | tf_op jit(solution)/shard_map/ppermute | solution.py:391
  141.1 20.7 %collective-permute-start.22 = (bf16[64,2048]{1,0:T(8,128)(2,1)S(1)}, bf16[64,2048]{1,0:T(8,128)(2,1)S(1)}, u32[]{:S(2)}, u32[]{:S(2)}) collective-permute-start(bf16[64,2048]{1,0:T(8,128)(2,1)S(1)} %get-tuple-element.338), channel_id=1, source_target_pairs={{0,8},{4,12},{8,0},{12,4},{1,9},{5,13},{9,1},{13,5},{2,10},{6,14},... | collective-permute-start | bytes 786440 | tf_op jit(solution)/shard_map/ppermute | solution.py:391
  168.8 1.3 copy-start.10
where the time goes:
time: 171 us; the launch traced here: 170 us
  Pallas kernels  71.4 us (42%)
  waiting for transfers between devices  52.8 us (31%)
  starting transfers between devices  30.2 us (18%)
  local copies, waits for them, and re-layouts  6.78 us (4%)
  other arithmetic  5.44 us (3%)
  between operations  3.51 us (2%)
    ppermute x18, waiting for transfers between devices, swap(): return lax.ppermute(v, axis, [(i, i ^ k) for i in range(n)])  52.8 us
    pallas_call x4, Pallas kernels, share(): pl.pallas_call(share_kernel, grid_spec=pltpu.PrefetchScalarGridSpec(num_s...  30.4 us
    ppermute x18, starting transfers between devices, swap(): return lax.ppermute(v, axis, [(i, i ^ k) for i in range(n)])  26.4 us
    pallas_call x3, Pallas kernels, deltas(): pl.pallas_call(kernel, grid=(width // cols,), in_specs=first + ins, out_s...  17.1 us
    pallas_call x3, Pallas kernels, scores(): pl.pallas_call(functools.partial(score_kernel, tuple(dists)), grid=(store...  12.9 us
    pallas_call x1, Pallas kernels, finish(): pl.pallas_call(functools.partial(finish_kernel, len(codes), n_dp), grid=(...  6.85 us
    pallas_call x1, Pallas kernels, packs(): pl.pallas_call(functools.partial(pack_kernel, n_dp, seg_len, shift), in_s...  4.15 us
    convert_element_type x1, other arithmetic, per_device(): adds[k ^ bit].append(swap(v.astype(jnp.bfloat16), 'tp', bit))  3.86 us
  transfers between devices with their start and end apart: 19, of which 8 were waited for; matrix products, arithmetic and copies ran while one was open for 3% of the time, Pallas kernels for 36%

commit v1 on v0

--- a/solution.py
+++ b/solution.py
@@ -31,30 +31,36 @@
     return v
 
 
-def score_kernel(dists, *refs):
+def score_kernel(dists, block, *refs):
+    me_ref, known_ref, refs = refs[0], refs[1], refs[2:]
     m = len(dists)
-    got, known, a_ref = refs[:m], refs[m:-m - 3], refs[-m - 3]
-    out_ref, slots, acc = refs[-m - 2], refs[-m - 1:-1], refs[-1]
+    got, a_ref, refs = refs[:1 if block else m], refs[1 if block else m], refs[(2 if block else m + 1):]
+    out_ref, told_ref, slots, acc = refs[0], refs[1], refs[2:-1], refs[-1]
     g = pl.program_id(0)
     per, width = a_ref.shape[0] // 16, a_ref.shape[1]
+
+    def view(i, low, high):
+        return got[0][me_ref[0] ^ (i + 1), :, low:high] if block else got[i][:, low:high]
 
     @pl.when(g == 0)
     def _():
         acc[...] = jnp.zeros_like(acc)
+        told_ref[...] = known_ref[0:1, 0:1]
         for i, dist in enumerate(dists):
             if dist is None:
-                slots[i][...] = known[0][...]
-            else:
-                meta = got[i][:, width:].astype(jnp.float32).astype(jnp.int32)
-                if dist == RELAY:
-                    dist = (2 + lax.broadcasted_iota(jnp.int32, (meta.shape[0], 1), 0) // SHARED) ^ 1
-                slots[i][...] = jnp.where(meta[:, 1:2] == dist, meta[:, 0:1] - 1, -1)
+                slots[i][...] = known_ref[...]
+                continue
+            meta = view(i, width, width + META).astype(jnp.float32).astype(jnp.int32)
+            if dist == RELAY:
+                dist = (2 + lax.broadcasted_iota(jnp.int32, (meta.shape[0], 1), 0) // SHARED) ^ 1
+            slots[i][...] = jnp.where(meta[:, 1:2] == dist, meta[:, 0:1] - 1, -1)
+            told_ref[...] = jnp.maximum(told_ref[...], meta[0:1, 2:3])
 
     off = 0
     for i in range(m):
-        n = got[i].shape[0]
+        n = slots[i].shape[0]
         s = lax.dot_general(
-            got[i][:, :width], a_ref[...], (((1,), (1,)), ((), ())), preferred_element_type=jnp.float32
+            view(i, 0, width), a_ref[...], (((1,), (1,)), ((), ())), preferred_element_type=jnp.float32
         )
         s = jnp.where(group_of(s.shape) + g * per == slots[i][...], s, 0.0)
         v = s[:, :128]
@@ -67,7 +73,7 @@
     def _():
         off = 0
         for i in range(m):
-            n = got[i].shape[0]
+            n = slots[i].shape[0]
             v = fold(acc[off:off + n, :])
             v = jnp.where(group_of(v.shape) == row_of(v.shape), v, 0.0)
             out_ref[off // 8:(off + n) // 8, :] = jnp.sum(v.reshape(n // 8, 8, 128), axis=1)
@@ -75,26 +81,28 @@
 
 
 def whole(shape):
-    return pl.BlockSpec(shape, lambda g: (0, 0))
-
-
-def scores(dists, got, known, store):
-    sizes = [v.shape[0] for v in got]
+    return pl.BlockSpec(shape, lambda g: (0,) * len(shape))
+
+
+def scores(me, known, dists, got, store):
+    block = got[0].ndim == 3
+    sizes = [got[0].shape[1]] * len(dists) if block else [v.shape[0] for v in got]
     total, width = sum(sizes), store.shape[1]
     blk = 256
     out = pl.pallas_call(
-        functools.partial(score_kernel, tuple(dists)),
+        functools.partial(score_kernel, tuple(dists), block),
         grid=(store.shape[0] // blk,),
-        in_specs=[whole(v.shape) for v in got + known] + [pl.BlockSpec((blk, width), lambda g: (g, 0))],
-        out_specs=[whole((total // 8, 128))] + [whole((n, 1)) for n in sizes],
-        out_shape=[jax.ShapeDtypeStruct((total // 8, 128), jnp.float32)]
+        in_specs=[pl.BlockSpec(memory_space=pltpu.SMEM), whole(known.shape)]
+        + [whole(v.shape) for v in got] + [pl.BlockSpec((blk, width), lambda g: (g, 0))],
+        out_specs=[whole((total // 8, 128)), whole((1, 1))] + [whole((n, 1)) for n in sizes],
+        out_shape=[jax.ShapeDtypeStruct((total // 8, 128), jnp.float32), jax.ShapeDtypeStruct((1, 1), jnp.int32)]
         + [jax.ShapeDtypeStruct((n, 1), jnp.int32) for n in sizes],
         scratch_shapes=[pltpu.VMEM((total, 128), jnp.float32)],
         compiler_params=pltpu.CompilerParams(vmem_limit_bytes=VMEM),
         cost_estimate=FREE,
         name="scores",
-    )(*got, *known, store)
-    return out[0], list(out[1:])
+    )(me, known, *got, store)
+    return out[0], out[1], list(out[2:])
 
 
 def spread_out(slots, packed, depth, spread):
@@ -122,52 +130,44 @@
         outs[i][...] = jnp.dot(spread[i][...], b_ref[...], preferred_element_type=jnp.float32).astype(jnp.bfloat16)
 
 
-def direct_kernel(n_dp, me_ref, *refs):
-    m = n_dp - 1
-    slots, packed, b_ref, outs, spread = refs[:m], refs[m], refs[m + 1], refs[m + 2:-m], refs[-m:]
+def direct_kernel(m, me_ref, *refs):
+    slots, packed, b_ref, block, spread = refs[:m], refs[m], refs[m + 1], refs[m + 2], refs[m + 3:]
     me = me_ref[0]
 
     @pl.when(pl.program_id(0) == 0)
     def _():
         spread_out(slots, packed, b_ref.shape[0], spread)
 
-    block = outs[-1]
     block[me] = jnp.zeros(block.shape[1:], block.dtype)
     for i in range(m):
         v = jnp.dot(spread[i][...], b_ref[...], preferred_element_type=jnp.float32)
-        if i < m - 1:
-            outs[i][...] = v[:SHARED].astype(jnp.bfloat16)
-            block[me ^ (i + 2)] = v[SHARED:].astype(jnp.bfloat16)
-        else:
-            block[me ^ 1] = v[:OWN].astype(jnp.bfloat16)
-            outs[i][...] = v[OWN:].astype(jnp.bfloat16)
-
-
-def deltas(slots, packed, store, me=None, n_dp=None):
+        block[me ^ (i + 1)] = v.astype(jnp.bfloat16)
+
+
+def deltas(slots, packed, store, me=None):
     depth, width = store.shape
     cols = width // 4
+    m, sizes = len(slots), [v.shape[0] for v in slots]
     part = lambda n: pl.BlockSpec((n, cols), lambda g: (0, g))
     ins = [whole(v.shape) for v in slots] + [whole(packed.shape), part(depth)]
+    args = [*slots, packed, store]
     if me is None:
-        kernel, first, args = functools.partial(delta_kernel, len(slots)), [], []
-        sizes, shapes = [v.shape[0] for v in slots], []
-        outs = [part(n) for n in sizes]
+        kernel, outs, shapes = delta_kernel, [part(n) for n in sizes], [(n, width) for n in sizes]
     else:
-        kernel, first, args = functools.partial(direct_kernel, n_dp), [pl.BlockSpec(memory_space=pltpu.SMEM)], [me]
-        sizes, shapes = [SHARED] * (n_dp - 2) + [NEAR - OWN], [(n_dp, OWN, width)]
-        outs = [part(n) for n in sizes] + [pl.BlockSpec((n_dp, OWN, cols), lambda g: (0, 0, g))]
-    shapes = [(n, width) for n in sizes] + shapes
+        kernel, ins, args = direct_kernel, [pl.BlockSpec(memory_space=pltpu.SMEM)] + ins, [me] + args
+        outs = [pl.BlockSpec((m + 1, OWN, cols), lambda g: (0, 0, g))]
+        shapes = [(m + 1, OWN, width)]
     return list(pl.pallas_call(
-        kernel,
+        functools.partial(kernel, m),
         grid=(width // cols,),
-        in_specs=first + ins,
+        in_specs=ins,
         out_specs=outs,
         out_shape=[jax.ShapeDtypeStruct(v, jnp.bfloat16) for v in shapes],
-        scratch_shapes=[pltpu.VMEM((v.shape[0], depth), jnp.bfloat16) for v in slots],
+        scratch_shapes=[pltpu.VMEM((n, depth), jnp.bfloat16) for n in sizes],
         compiler_params=pltpu.CompilerParams(vmem_limit_bytes=VMEM),
         cost_estimate=FREE,
         name="deltas",
-    )(*args, *slots, packed, store))
+    )(*args))
 
 
 def finish_kernel(m, n_dp, me_ref, row_ref, *refs):
@@ -237,7 +237,7 @@
 
 
 def near_code(big, axis):
-    return big + iota_of(NEAR, axis)
+    return big + OWN + iota_of(NEAR - OWN, axis)
 
 
 def own_code(big, j, axis):
@@ -250,21 +250,23 @@
     return OWN + jnp.where(f < over, even * big + f, (even + 1) * big + f - over)
 
 
-def far_code(big, j, over, axis):
-    f = iota_of(SHARED + OWN, axis)
-    g = f + (j % 2) * SHARED
-    even = j - j % 2
-    code = OWN + jnp.where(g < over, even * big + g, (even + 1) * big + g - over)
-    return jnp.where(f < SHARED, code, j * big + f - SHARED)
+def flat_column(v):
+    a, b = v.shape
+    i = lax.broadcasted_iota(jnp.int32, (a * b, b), 0)
+    j = lax.broadcasted_iota(jnp.int32, (a * b, b), 1)
+    out = jnp.zeros((a * b, b), jnp.int32)
+    for k in range(a):
+        out += jnp.where(i - j == k * b, v[k:k + 1, :], 0)
+    return jnp.sum(out, axis=1, keepdims=True)
 
 
 def pack_kernel(n_dp, seg_len, shift, me_ref, ids_ref, lives_ref, index_ref, x_ref,
-                table_ref, row_ref, self_ref, meta_ref, *outs):
+                table_ref, row_ref, self_ref, meta_ref, rounds_ref, block, *outs):
     me = me_ref[0]
-    count, (rows, width) = ids_ref.shape[1], x_ref.shape
+    count, (rows, width) = ids_ref.shape[0] * ids_ref.shape[1], x_ref.shape
     big = 2 * rows
-    lives = lives_ref[...]
-    hit = column(ids_ref[...]) == lax.broadcasted_iota(jnp.int32, (count, index_ref.shape[1]), 1)
+    lives = row(flat_column(lives_ref[...]))
+    hit = flat_column(ids_ref[...]) == lax.broadcasted_iota(jnp.int32, (count, index_ref.shape[1]), 1)
     pos = row(jnp.sum(jnp.where(hit, index_ref[...], 0), axis=1, keepdims=True))
     table_ref[0:1, :] = pos
     table_ref[1:2, :] = lives
@@ -296,18 +298,26 @@
     for j in range(2, n_dp):
         held = OWN + 2 * SHARED if j % 2 == 0 else OWN + jnp.maximum(2 * SHARED - over_of(dist, lives, j), 0)
         left = jnp.maximum(left, total(dist, lives, j) - held)
-    rounds = ((jnp.maximum(left, 0) + ROUND - 1) // ROUND).astype(jnp.float32)
-    told = jnp.where(lax.broadcasted_iota(jnp.int32, (1, META), 1) == 2, rounds, 0.0)
+    rounds = (jnp.maximum(left, 0) + ROUND - 1) // ROUND
+    rounds_ref[...] = rounds
+    told = jnp.where(lax.broadcasted_iota(jnp.int32, (1, META), 1) == 2, rounds.astype(jnp.float32), 0.0)
+
+    def chosen(c):
+        pick = jnp.where(c == by_lane, 1.0, 0.0).astype(jnp.bfloat16)
+        v = jnp.dot(pick, x_ref[...], preferred_element_type=jnp.float32).astype(jnp.bfloat16)
+        return v, (jnp.dot(pick, meta, preferred_element_type=jnp.float32) + told).astype(jnp.bfloat16)
 
     far = range(2, n_dp)
-    codes = [far_code(big, j, over_of(dist, lives, j), 0) for j in far] + [near_code(big, 0)]
+    block[me] = jnp.zeros(block.shape[1:], block.dtype)
+    for j in range(1, n_dp):
+        v, u = chosen(own_code(big, j, 0))
+        block[me ^ j, :, :width] = v
+        block[me ^ j, :, width:] = u
+    codes = [shared_code(big, j, over_of(dist, lives, j), 0) for j in far] + [near_code(big, 0)]
     m = len(codes)
     for c, out in zip(codes, outs[:m]):
-        pick = jnp.where(c == by_lane, 1.0, 0.0).astype(jnp.bfloat16)
-        out[:, :width] = jnp.dot(pick, x_ref[...], preferred_element_type=jnp.float32).astype(jnp.bfloat16)
-        out[:, width:] = (jnp.dot(pick, meta, preferred_element_type=jnp.float32) + told).astype(jnp.bfloat16)
-    lanes = [shared_code(big, j, over_of(dist, lives, j), 1) for j in far]
-    lanes += [big + OWN + iota_of(NEAR - OWN, 1)]
+        out[:, :width], out[:, width:] = chosen(c)
+    lanes = [shared_code(big, j, over_of(dist, lives, j), 1) for j in far] + [near_code(big, 1)]
     lanes += [own_code(big, j, 1) for j in range(1, n_dp)]
     for c, out in zip(lanes, outs[m:]):
         out[...] = c
@@ -318,12 +328,12 @@
 
 
 def packs(me, ids, lives, index, x, n_dp, seg_len, shift):
-    count, (rows, width) = ids.shape[1], x.shape
-    sizes = [SHARED + OWN] * (n_dp - 2) + [NEAR]
-    parts = [SHARED] * (n_dp - 2) + [NEAR - OWN] + [OWN] * (n_dp - 1)
+    count, (rows, width) = ids.shape[0] * ids.shape[1], x.shape
+    sizes = [SHARED] * (n_dp - 2) + [NEAR - OWN]
     shapes = [((2, count), jnp.int32), ((rows, 1), jnp.int32), ((rows, 1), jnp.int32)]
-    shapes += [((rows, META), jnp.bfloat16)]
-    shapes += [((n, width + META), jnp.bfloat16) for n in sizes] + [((1, n), jnp.int32) for n in parts]
+    shapes += [((rows, META), jnp.bfloat16), ((1, 1), jnp.int32), ((n_dp, OWN, width + META), jnp.bfloat16)]
+    shapes += [((n, width + META), jnp.bfloat16) for n in sizes]
+    shapes += [((1, n), jnp.int32) for n in sizes + [OWN] * (n_dp - 1)]
     return pl.pallas_call(
         functools.partial(pack_kernel, n_dp, seg_len, shift),
         in_specs=[pl.BlockSpec(memory_space=pltpu.SMEM)] + vmem(4),
@@ -397,90 +407,101 @@
             k *= 2
         return v
 
-    def answer(dists, got, known=()):
-        scored, slots = scores(dists, got, list(known), shrink_store)
-        return slots, butterfly(scored, "tp", jnp.add)
+    def answer(dists, got, known):
+        scored, told, slots = scores(me, known, dists, got, shrink_store)
+        return slots, told, butterfly(scored, "tp", jnp.add)
+
+    def total_of(parts):
+        if len(parts) == 1:
+            return parts[0]
+        return functools.reduce(jnp.add, [v.astype(jnp.float32) for v in parts]).astype(jnp.bfloat16)
+
+    def a2a(v):
+        return lax.all_to_all(v, "dp", split_axis=0, concat_axis=0, tiled=True)
 
     def after(v, *others):
         return lax.optimization_barrier((v, others))[0]
 
     packed = list(packs(
-        me,
-        segment_adapter.reshape(1, count),
-        segment_live_rows.reshape(1, count),
-        adapter_store_index.reshape(1, -1),
-        x, n_dp, seg_len, shift,
+        me, segment_adapter, segment_live_rows, adapter_store_index.reshape(1, -1), x, n_dp, seg_len, shift
     ))
-    table, row_code, self_slots, meta = packed[:4]
+    table, row_code, self_slots, meta, rounds, block = packed[:6]
     m = len(far)
-    out_far, out_near = packed[4:4 + m], packed[4 + m]
-    codes, block_codes = packed[5 + m:6 + 2 * m], packed[6 + 2 * m:]
-
-    in_far = [swap(v, "dp", j) for v, j in zip(out_far, far)]
+    out_shared, out_near, codes = packed[6:6 + m], packed[6 + m], packed[7 + m:]
+    codes, block_codes = codes[:m + 1], codes[m + 1:]
+
+    block = a2a(block)
+    in_shared = [swap(v, "dp", j) for v, j in zip(out_shared, far)]
     in_near = swap(out_near, "dp", 1)
 
-    found, self_part = answer([None], [after(x, table)], [self_slots])
-    (self_delta,) = deltas(found, self_part, expand_store)
-
-    at = after(lax.axis_index("tp").reshape(1), table)
+    self_found, _, self_part = answer([None], [after(x, table)], self_slots)
+
+    at = after(lax.axis_index("tp").reshape(1), self_part)
     cols = weight.shape[1] // n_tp
-    shares = {k: share(at ^ k, x, weight, cols) for k in reversed(range(n_tp))}
-    (in_far, in_near, shares), _ = lax.optimization_barrier(((in_far, in_near, shares), self_delta))
-
-    in_relay = swap(jnp.concatenate([v[:SHARED] for v in in_far]), "dp", 1)
-    found, part = answer(list(far) + [1], in_far + [in_near])
-    direct = deltas(found, part, expand_store, me, n_dp)
-    block = lax.all_to_all(direct[-1], "dp", split_axis=0, concat_axis=0, tiled=True)
+    early = [k for k in reversed(range(n_tp)) if k >= n_tp // 2]
+    shares = {k: share(at ^ k, x, weight, cols) for k in early}
+
+    block, shares = lax.optimization_barrier((block, shares))
+    found, rounds, part = answer(list(range(1, n_dp)), [block], rounds)
+    (block,) = deltas(found, part, expand_store, me)
+    at = after(at, block)
+    block = a2a(block)
+    for k in reversed(range(n_tp)):
+        if k not in early and k:
+            shares[k] = share(at ^ k, x, weight, cols)
+
+    in_shared, shares = lax.optimization_barrier((in_shared, shares))
+    in_relay = jnp.concatenate(in_shared)
+    at = after(at, in_relay)
+    in_relay = swap(in_relay, "dp", 1)
+    shares[0] = share(at, x, weight, cols)
+    (self_delta,) = deltas(self_found, after(self_part, in_shared), expand_store)
 
     adds = {k: [shares[k]] for k in shares}
     for k in range(1, n_tp, 2):
         adds[k ^ 1].append(swap(adds.pop(k)[0], "tp", 1))
-    told = [v[0, width + 2] for v in in_far + [in_near, out_near]]
-    rounds = functools.reduce(jnp.maximum, told).astype(jnp.int32).reshape(1, 1)
-    rounds = butterfly(rounds, "rep", jnp.maximum)
-
-    found, part = answer([RELAY], [after(in_relay, direct)])
-    part, adds, rounds = lax.optimization_barrier((part, adds, rounds))
-    rounds = rounds[0, 0]
-    (relayed,) = deltas(found, part, expand_store)
-    relayed = swap(relayed, "dp", 1)
+    for k in range(2, n_tp, 2):
+        adds[k] = [total_of(adds[k])]
+
+    got, self_delta, adds = lax.optimization_barrier((in_shared + [in_near, in_relay], self_delta, adds))
+    found, _, part = answer(list(far) + [1, RELAY], got, rounds)
+    part, adds, block = lax.optimization_barrier((part, adds, block))
+    late = deltas(found, part, expand_store)
+    relayed = swap(late[-1], "dp", 1)
     bit = 2
     while bit < n_tp:
         for k in sorted((k for k in adds if k & bit), reverse=True):
-            v = functools.reduce(jnp.add, [u.astype(jnp.float32) for u in adds.pop(k)])
-            adds[k ^ bit].append(swap(v.astype(jnp.bfloat16), "tp", bit))
+            adds[k ^ bit].append(swap(total_of(adds.pop(k)), "tp", bit))
         bit *= 2
-    near, _ = lax.optimization_barrier((direct[m], relayed))
-    back = [swap(direct[i] + relayed[i * SHARED:(i + 1) * SHARED], "dp", j) for i, j in enumerate(far)]
-    back.append(swap(near, "dp", 1))
+    back = [swap(late[i] + relayed[i * SHARED:(i + 1) * SHARED], "dp", j) for i, j in enumerate(far)]
+    back.append(swap(late[m], "dp", 1))
     adds = adds[0] + [self_delta]
-
-    def rest():
-        pos, alive = table[0], table[1]
+    rounds = butterfly(rounds, "rep", jnp.maximum)[0, 0]
+
+    def late_round(i, out):
+        tab, rows_in, rows_meta, places = lax.optimization_barrier((table, x, meta, row_code, i))[:4]
+        pos, alive = tab[0], tab[1]
         dist = (pos >> shift) ^ me[0]
         held = [None, jnp.int32(NEAR)]
         for j in range(2, n_dp, 2):
             extra = jnp.maximum(jnp.sum(jnp.where(dist == j, alive, 0)) - OWN, 0)
             held += [jnp.int32(OWN + 2 * SHARED), OWN + jnp.maximum(2 * SHARED - extra, 0)]
-        x_meta = jnp.concatenate([x, meta], axis=1)
-
-        def body(i, extra):
-            code = [j * big + held[j] + i * ROUND + jnp.arange(ROUND, dtype=jnp.int32) for j in range(1, n_dp)]
-            got = []
-            for j, c in zip(range(1, n_dp), code):
-                pick = (c[:, None] == row_code.reshape(1, rows)).astype(jnp.bfloat16)
-                v = jnp.dot(pick, x_meta, preferred_element_type=jnp.float32).astype(jnp.bfloat16)
-                got.append(swap(v, "dp", j))
-            found, part = answer(list(range(1, n_dp)), got)
-            for j, c, v in zip(range(1, n_dp), code, deltas(found, part, expand_store)):
-                put = (row_code == c[None, :]).astype(jnp.bfloat16)
-                extra = extra + jnp.dot(put, swap(v, "dp", j), preferred_element_type=jnp.float32)
-            return extra
-
-        extra = lax.fori_loop(0, rounds, body, jnp.zeros((rows, width), jnp.float32))
-        return finish(me, row_code, codes, block_codes, back, block, adds + [extra])
-
-    out = lax.cond(rounds > 0, rest, lambda: finish(me, row_code, codes, block_codes, back, block, adds))
+        x_meta = jnp.concatenate([rows_in, rows_meta], axis=1)
+        code = [j * big + held[j] + i * ROUND + jnp.arange(ROUND, dtype=jnp.int32) for j in range(1, n_dp)]
+        got = []
+        for j, c in zip(range(1, n_dp), code):
+            pick = (c[:, None] == places.reshape(1, rows)).astype(jnp.bfloat16)
+            v = jnp.dot(pick, x_meta, preferred_element_type=jnp.float32).astype(jnp.bfloat16)
+            got.append(swap(v, "dp", j))
+        found, _, part = answer(list(range(1, n_dp)), got, rounds.reshape(1, 1))
+        total = out.astype(jnp.float32)
+        for j, c, v in zip(range(1, n_dp), code, deltas(found, part, expand_store)):
+            put = (places == c[None, :]).astype(jnp.bfloat16)
+            total = total + jnp.dot(put, swap(v, "dp", j), preferred_element_type=jnp.float32)
+        return total.astype(jnp.bfloat16)
+
+    out = finish(me, row_code, codes, block_codes, back, block, adds)
+    out = lax.fori_loop(0, rounds, late_round, out)
     return out.reshape(steps, rows_dev, width)
 
 

time: 171 us -> 211 us (1.23)
  waiting for transfers between devices: 52.8 us -> 73.7 us
  local copies, waits for them, and re-layouts: 6.78 us -> 17.6 us
  Pallas kernels: 71.4 us -> 81.8 us
    unnamed x26 -> x61, local copies, waits for them, and re-layouts: 2.04 us -> 15.9 us
    ppermute x18, waiting for transfers between devices: 52.8 us -> 63.3 us  [swap(): return lax.ppermute(v, axis, [(i, i ^ k) for i in range(n)])]
    all_to_all x1 -> x2, waiting for transfers between devices: 0.01 us -> 10.4 us  [a2a(): return lax.all_to_all(v, 'dp', split_axis=0, concat_axis=0, tiled=True)]
    pallas_call x6, Pallas kernels: 30 us -> 37.3 us  [the longest x3 22.5 us: scores(): pl.pallas_call(functools.partial(score_kernel, tuple(dists), block), grid...]
    ppermute x18, starting transfers between devices: 26.4 us -> 19.6 us  [swap(): return lax.ppermute(v, axis, [(i, i ^ k) for i in range(n)])]
    all_to_all x1 -> x2, starting transfers between devices: 3.75 us -> 10 us  [a2a(): return lax.all_to_all(v, 'dp', split_axis=0, concat_axis=0, tiled=True)]
    slice x6 -> x0, local copies, waits for them, and re-layouts: 3.22 us -> none  [the longest x4 3.18 us: per_device(): told = [v[0, width + 2] for v in in_far + [in_near, out_near]]]
  transfers between devices with their start and end apart: 19 -> 20, of which waited for: 8 -> 13; matrix products, arithmetic and copies ran while one was open for 3% -> 4% of each run, Pallas kernels for 36% -> 33%
where the time goes in v1:
time: 211 us; the launch traced here: 210 us
  Pallas kernels  81.8 us (39%)
  waiting for transfers between devices  73.7 us (35%)
  starting transfers between devices  29.6 us (14%)
  local copies, waits for them, and re-layouts  17.6 us (8%)
  other arithmetic  5.99 us (3%)
    ppermute x18, waiting for transfers between devices, swap(): return lax.ppermute(v, axis, [(i, i ^ k) for i in range(n)])  63.3 us
    pallas_call x4, Pallas kernels, share(): pl.pallas_call(share_kernel, grid_spec=pltpu.PrefetchScalarGridSpec(num_s...  32.1 us
    pallas_call x3, Pallas kernels, scores(): pl.pallas_call(functools.partial(score_kernel, tuple(dists), block), grid...  22.5 us
    ppermute x18, starting transfers between devices, swap(): return lax.ppermute(v, axis, [(i, i ^ k) for i in range(n)])  19.6 us
    unnamed x61, local copies, waits for them, and re-layouts  15.9 us
    pallas_call x3, Pallas kernels, deltas(): pl.pallas_call(functools.partial(kernel, m), grid=(width // cols,), in_sp...  14.8 us
    all_to_all x2, waiting for transfers between devices, a2a(): return lax.all_to_all(v, 'dp', split_axis=0, concat_axis=0, tiled=True)  10.4 us
    all_to_all x2, starting transfers between devices, a2a(): return lax.all_to_all(v, 'dp', split_axis=0, concat_axis=0, tiled=True)  10 us
  transfers between devices with their start and end apart: 20, of which 13 were waited for; matrix products, arithmetic and copies ran while one was open for 4% of the time, Pallas kernels for 33%

profile of v1, /device:TPU:0, one launch (start us, length us, event | category | flops | bytes accessed | tf_op | source)
XLA Modules:
  0.0 210.2 jit_solution(933283084330221476)
XLA Ops:
  2.0 4.9 %pack.1 = (s32[2,32]{1,0:T(2,128)}, s32[512,1]{1,0:T(8,128)S(1)}, s32[512,1]{1,0:T(8,128)S(1)}, bf16[512,128]{1,0:T(8,128)(2,1)}, s32[1,1]{1,0:T(1,128)}, /*inde...) custom-call(s32[1]{0:T(128)} %bitcast.1.me_ref.refs_0_, ...), custom_call_target="tpu_custom_call" | custom-call | tf_op jit(solution)/shard_map/pack/pallas_call | solution.py:337
  9.6 6.3 %all-to-all-start = ((bf16[4,72,2176]{2,1,0:T(8,128)(2,1)}), bf16[4,72,2176]{2,1,0:T(8,128)(2,1)S(1)}, u32[]{:S(2)}, u32[]{:S(2)}) async-start(bf16[4,72,2176]{2,1,0:T(8,128)(2,1)} %get-tuple-element.230), calls=%async_computation | async-start | bytes 2506752 | tf_op jit(solution)/shard_map/all_to_all | solution.py:420
  15.9 2.9 %collective-permute-start.10 = (bf16[64,2176]{1,0:T(8,128)(2,1)}, bf16[64,2176]{1,0:T(8,128)(2,1)}, u32[]{:S(2)}, u32[]{:S(2)}) collective-permute-start(bf16[64,2176]{1,0:T(8,128)(2,1)} %get-tuple-element.238), channel_id=1, source_target_pairs={{0,8},{4,12},{8,0},{12,4},{1,9},{5,13},{9,1},{13,5},{2,10},{6,14},... | collective-permute-start | bytes 835592 | tf_op jit(solution)/shard_map/ppermute | solution.py:401
  20.3 6.4 %scores.7 = (f32[64,128]{1,0:T(8,128)S(1)}, s32[1,1]{1,0:T(1,128)}, s32[512,1]{1,0:T(8,128)S(1)}) custom-call(s32[1]{0:T(128)} %bitcast.1.me_ref.refs_0_, s32[512,1]{1,0:T(8,128)S(1)} %get-tuple-element.231.refs_1_, bf16[512,2048]{1,0:T(8,128)(2,1)} %bitcast.39, bf16[1024,2048]{1,0:T(8,128)(2,1)} %bitcast.34), custom_call_target="tpu_custom_call" | custom-call | tf_op jit(solution)/shard_map/scores/pallas_call | solution.py:92
  28.6 1.5 collective-permute-start.9
  30.1 2.4 %collective-permute-done.9 = f32[64,128]{1,0:T(8,128)S(1)} collective-permute-done((f32[64,128]{1,0:T(8,128)S(1)}, f32[64,128]{1,0:T(8,128)S(1)}, u32[]{:S(2)}, u32[]{:S(2)}) %collective-permute-start.9) | collective-permute-done | bytes 32800 | tf_op jit(solution)/shard_map/ppermute | solution.py:401
  32.5 7.9 %share.4 = bf16[512,2048]{1,0:T(8,128)(2,1)S(1)} custom-call(s32[1]{0:T(128)S(6)} %xor.22.at_ref, bf16[512,2048]{1,0:T(8,128)(2,1)} %bitcast.40, bf16[2048,8192]{1,0:T(8,128)(2,1)} %w_ref.7), custom_call_target="tpu_custom_call" | custom-call | tf_op jit(solution)/shard_map/share/pallas_call | solution.py:355
  40.5 8.1 %share.5 = bf16[512,2048]{1,0:T(8,128)(2,1)} custom-call(s32[1]{0:T(128)S(6)} %xor.23.at_ref, bf16[512,2048]{1,0:T(8,128)(2,1)S(1)} %bitcast.43, bf16[2048,8192]{1,0:T(8,128)(2,1)} %w_ref.7), custom_call_target="tpu_custom_call" | custom-call | tf_op jit(solution)/shard_map/share/pallas_call | solution.py:355
  48.6 10.4 %all-to-all-done.refs_2_ = bf16[4,72,2176]{2,1,0:T(8,128)(2,1)S(1)} async-done(((bf16[4,72,2176]{2,1,0:T(8,128)(2,1)}), bf16[4,72,2176]{2,1,0:T(8,128)(2,1)S(1)}, u32[]{:S(2)}, u32[]{:S(2)}) %all-to-all-start) | async-done | bytes 1253408 | tf_op jit(solution)/shard_map/all_to_all | solution.py:420
  59.0 7.6 %scores.8 = (f32[27,128]{1,0:T(8,128)S(1)}, s32[1,1]{1,0:T(1,128)}, s32[72,1]{1,0:T(8,128)S(1)}, s32[72,1]{1,0:T(8,128)S(1)}, s32[72,1]{1,0:T(8,128)S(1)}) custom-call(s32[1]{0:T(128)} %bitcast.1.me_ref.refs_0_, s32[1,1]{1,0:T(1,128)} %get-tuple-element.229.refs_1_, bf16[4,72,2176]{2,1,0:T(8,128)(2,1)S(1)} %all-to-all-done.refs_2_, bf16[1024,2048]{1,0:T(8,128)(2,1)} %bitcast.35), custom_call_target="tpu_custom_call" | custom-call | tf_op jit(solution)/shard_map/scores/pallas_call | solution.py:92
  67.8 1.5 collective-permute-start.13
  69.3 2.2 %collective-permute-done.13 = f32[27,128]{1,0:T(8,128)S(1)} collective-permute-done((f32[27,128]{1,0:T(8,128)S(1)}, f32[27,128]{1,0:T(8,128)S(1)}, u32[]{:S(2)}, u32[]{:S(2)}) %collective-permute-start.13) | collective-permute-done | bytes 13856 | tf_op jit(solution)/shard_map/ppermute | solution.py:401
  71.6 3.8 %deltas.7 = bf16[4,72,2048]{2,1,0:T(8,128)(2,1)S(1)} custom-call(s32[1]{0:T(128)} %bitcast.1.me_ref.refs_0_, s32[72,1]{1,0:T(8,128)S(1)} %get-tuple-element.240.refs_0_, s32[72,1]{1,0:T(8,128)S(1)} %get-tuple-element.241.refs_1_, s32[72,1]{1,0:T(8,128)S(1)} %get-tuple-element.242.refs_2_, f32[27,128]{1,0:T(8,128)S(1)} %add.156.refs_3_, ...), custom_call_target="tpu_custom_call" | custom-call | tf_op jit(solution)/shard_map/deltas/pallas_call | solution.py:160
  76.4 8.2 %share.6 = bf16[512,2048]{1,0:T(8,128)(2,1)} custom-call(s32[1]{0:T(128)S(6)} %xor.24.at_ref, bf16[512,2048]{1,0:T(8,128)(2,1)S(1)} %bitcast.44, bf16[2048,8192]{1,0:T(8,128)(2,1)} %w_ref.7), custom_call_target="tpu_custom_call" | custom-call | tf_op jit(solution)/shard_map/share/pallas_call | solution.py:355
  85.1 3.7 %all-to-all-start.1 = ((bf16[4,72,2048]{2,1,0:T(8,128)(2,1)}), bf16[4,72,2048]{2,1,0:T(8,128)(2,1)S(1)}, u32[]{:S(2)}, u32[]{:S(2)}) async-start(bf16[4,72,2048]{2,1,0:T(8,128)(2,1)} %copy-done.3), calls=%async_computation.1 | async-start | bytes 2359296 | tf_op jit(solution)/shard_map/all_to_all | solution.py:420
  88.9 1.8 collective-permute-start.14
  93.0 7.9 %share.7.refs_10_ = bf16[512,2048]{1,0:T(8,128)(2,1)S(1)} custom-call(s32[1]{0:T(128)} %bitcast.4.at_ref, bf16[512,2048]{1,0:T(8,128)(2,1)} %bitcast.41, bf16[2048,8192]{1,0:T(8,128)(2,1)} %w_ref.7), custom_call_target="tpu_custom_call" | custom-call | tf_op jit(solution)/shard_map/share/pallas_call | solution.py:355
  102.2 4.1 %deltas.8.refs_13_ = bf16[512,2048]{1,0:T(8,128)(2,1)S(1)} custom-call(s32[512,1]{1,0:T(8,128)S(1)} %copy-done.7, f32[64,128]{1,0:T(8,128)S(1)} %add.154.refs_1_, bf16[1024,2048]{1,0:T(8,128)(2,1)S(1)} %bitcast.33), custom_call_target="tpu_custom_call" | custom-call | tf_op jit(solution)/shard_map/deltas/pallas_call | solution.py:160
  106.4 4.5 %add_convert_fusion.1 = bf16[512,2048]{1,0:T(8,128)(2,1)} fusion(bf16[512,2048]{1,0:T(8,128)(2,1)} %collective-permute-done.17, bf16[512,2048]{1,0:T(8,128)(2,1)S(1)} %share.4), kind=kLoop, calls=%fused_computation.32 | loop fusion | flops 4194304 | bytes 6291456 | tf_op jit(solution)/shard_map/convert_element_type | solution.py:417
  110.9 13.1 %collective-permute-done.14.refs_4_ = bf16[136,2176]{1,0:T(8,128)(2,1)S(1)} collective-permute-done((bf16[136,2176]{1,0:T(8,128)(2,1)}, bf16[136,2176]{1,0:T(8,128)(2,1)S(1)}, u32[]{:S(2)}, u32[]{:S(2)}) %collective-permute-start.14) | collective-permute-done | bytes 591904 | tf_op jit(solution)/shard_map/ppermute | solution.py:401
  124.0 11.1 %collective-permute-done.15.refs_5_ = bf16[128,2176]{1,0:T(8,128)(2,1)S(1)} collective-permute-done((bf16[128,2176]{1,0:T(8,128)(2,1)S(1)}, bf16[128,2176]{1,0:T(8,128)(2,1)S(1)}, u32[]{:S(2)}, u32[]{:S(2)}) %collective-permute-start.15) | collective-permute-done | bytes 557088 | tf_op jit(solution)/shard_map/ppermute | solution.py:401
  135.1 8.6 %scores.9 = (f32[49,128]{1,0:T(8,128)S(1)}, s32[1,1]{1,0:T(1,128)}, s32[64,1]{1,0:T(8,128)S(1)}, s32[64,1]{1,0:T(8,128)S(1)}, s32[136,1]{1,0:T(8,128)S(1)}, /*index=5*/s32[128,1]{1,0:T(8,128)S(1)}) custom-call(s32[1]{0:T(128)} %bitcast.1.me_ref.refs_0_, s32[1,1]{1,0:T(1,128)} %get-tuple-element.237.refs_1_, ...), custom_call_target="tpu_custom_call" | custom-call | tf_op jit(solution)/shard_map/scores/pallas_call | solution.py:92
  146.7 1.5 collective-permute-start.19
  148.2 2.4 %collective-permute-done.19 = f32[49,128]{1,0:T(8,128)S(1)} collective-permute-done((f32[49,128]{1,0:T(8,128)S(1)}, f32[49,128]{1,0:T(8,128)S(1)}, u32[]{:S(2)}, u32[]{:S(2)}) %collective-permute-start.19) | collective-permute-done | bytes 25120 | tf_op jit(solution)/shard_map/ppermute | solution.py:401
  151.2 1.5 collective-permute-start.24
  156.7 6.9 %deltas.9 = (bf16[64,2048]{1,0:T(8,128)(2,1)S(1)}, bf16[64,2048]{1,0:T(8,128)(2,1)S(1)}, bf16[136,2048]{1,0:T(8,128)(2,1)}, bf16[128,2048]{1,0:T(8,128)(2,1)S(1)}) custom-call(s32[64,1]{1,0:T(8,128)S(1)} %copy-done.14, s32[64,1]{1,0:T(8,128)S(1)} %copy-done.16, s32[136,1]{1,0:T(8,128)S(1)} %copy-done.10, s32[128,1]{1,0:T(8,128)S(1)} %copy-done.12, ...), custom_call_target="tpu_custom_call" | custom-call | tf_op jit(solution)/shard_map/deltas/pallas_call | solution.py:160
  165.6 12.8 %collective-permute-done.20 = bf16[128,2048]{1,0:T(8,128)(2,1)S(1)} collective-permute-done((bf16[128,2048]{1,0:T(8,128)(2,1)S(1)}, bf16[128,2048]{1,0:T(8,128)(2,1)S(1)}, u32[]{:S(2)}, u32[]{:S(2)}) %collective-permute-start.20) | collective-permute-done | bytes 524320 | tf_op jit(solution)/shard_map/ppermute | solution.py:401
  179.3 2.4 %collective-permute-start.21 = (bf16[64,2048]{1,0:T(8,128)(2,1)}, bf16[64,2048]{1,0:T(8,128)(2,1)}, u32[]{:S(2)}, u32[]{:S(2)}) collective-permute-start(bf16[64,2048]{1,0:T(8,128)(2,1)} %get-tuple-element.317), channel_id=1, source_target_pairs={{0,8},{4,12},{8,0},{12,4},{1,9},{5,13},{9,1},{13,5},{2,10},{6,14},... | collective-permute-start | bytes 786440 | tf_op jit(solution)/shard_map/ppermute | solution.py:401
  184.4 2.1 collective-permute-done.25
  187.7 6.5 %collective-permute-done.23.refs_8_ = bf16[136,2048]{1,0:T(8,128)(2,1)} collective-permute-done((bf16[136,2048]{1,0:T(8,128)(2,1)}, bf16[136,2048]{1,0:T(8,128)(2,1)}, u32[]{:S(2)}, u32[]{:S(2)}) %collective-permute-start.23) | collective-permute-done | bytes 557088 | tf_op jit(solution)/shard_map/ppermute | solution.py:401
  194.2 7.1 %collective-permute-done.22.refs_7_ = bf16[64,2048]{1,0:T(8,128)(2,1)} collective-permute-done((bf16[64,2048]{1,0:T(8,128)(2,1)}, bf16[64,2048]{1,0:T(8,128)(2,1)}, u32[]{:S(2)}, u32[]{:S(2)}) %collective-permute-start.22) | collective-permute-done | bytes 262176 | tf_op jit(solution)/shard_map/ppermute | solution.py:401
  202.7 7.5 %finish.1 = bf16[512,2048]{1,0:T(8,128)(2,1)} custom-call(s32[1]{0:T(128)} %bitcast.1.me_ref.refs_0_, s32[512,1]{1,0:T(8,128)S(1)} %copy-done.5, s32[1,64]{1,0:T(1,128)S(1)} %get-tuple-element.223.refs_0_, s32[1,64]{1,0:T(1,128)S(1)} %get-tuple-element.224.refs_1_, s32[1,136]{1,0:T(1,128)S(1)} %get-tuple-element.225.refs_2_, ...), custom_call_target="tpu_custom_call" | custom-call | tf_op jit(solution)/shard_map/finish/pallas_call | solution.py:192
  (92 shorter events, 29.0 us)
Async XLA Ops:
  9.6 49.4 %all-to-all-start = ((bf16[4,72,2176]{2,1,0:T(8,128)(2,1)}), bf16[4,72,2176]{2,1,0:T(8,128)(2,1)S(1)}, u32[]{:S(2)}, u32[]{:S(2)}) async-start(bf16[4,72,2176]{2,1,0:T(8,128)(2,1)} %get-tuple-element.230), calls=%async_computation | async-start | bytes 2506752 | tf_op jit(solution)/shard_map/all_to_all | solution.py:420
  15.9 68.6 %collective-permute-start.10 = (bf16[64,2176]{1,0:T(8,128)(2,1)}, bf16[64,2176]{1,0:T(8,128)(2,1)}, u32[]{:S(2)}, u32[]{:S(2)}) collective-permute-start(bf16[64,2176]{1,0:T(8,128)(2,1)} %get-tuple-element.238), channel_id=1, source_target_pairs={{0,8},{4,12},{8,0},{12,4},{1,9},{5,13},{9,1},{13,5},{2,10},{6,14},... | collective-permute-start | bytes 835592 | tf_op jit(solution)/shard_map/ppermute | solution.py:401
  18.9 65.7 %collective-permute-start.11 = (bf16[64,2176]{1,0:T(8,128)(2,1)}, bf16[64,2176]{1,0:T(8,128)(2,1)}, u32[]{:S(2)}, u32[]{:S(2)}) collective-permute-start(bf16[64,2176]{1,0:T(8,128)(2,1)} %get-tuple-element.239), channel_id=1, source_target_pairs={{0,12},{4,8},{8,4},{12,0},{1,13},{5,9},{9,5},{13,1},{2,14},{6,10},... | collective-permute-start | bytes 835592 | tf_op jit(solution)/shard_map/ppermute | solution.py:401
  27.4 1.2 collective-permute-start.8
  28.6 3.9 %collective-permute-start.9 = (f32[64,128]{1,0:T(8,128)S(1)}, f32[64,128]{1,0:T(8,128)S(1)}, u32[]{:S(2)}, u32[]{:S(2)}) collective-permute-start(f32[64,128]{1,0:T(8,128)S(1)} %add.153), channel_id=1, source_target_pairs={{0,2},{1,3},{2,0},{3,1},{4,6},{5,7},{6,4},{7,5},{8,10},{9,11},{10,... | collective-permute-start | bytes 98312 | tf_op jit(solution)/shard_map/ppermute | solution.py:401
  32.5 7.9 %copy-start.29 = (bf16[4,128,2048]{2,1,0:T(8,128)(2,1)S(1)}, bf16[4,128,2048]{2,1,0:T(8,128)(2,1)}, u32[]{:S(2)}) copy-start(bf16[4,128,2048]{2,1,0:T(8,128)(2,1)} %param.9) | copy-start | bytes 6291460
  59.0 12.5 %copy-start.25 = (bf16[64,16,2048]{2,1,0:T(8,128)(2,1)S(1)}, bf16[64,16,2048]{2,1,0:T(8,128)(2,1)}, u32[]{:S(2)}) copy-start(bf16[64,16,2048]{2,1,0:T(8,128)(2,1)} %param.12) | copy-start | bytes 12582916
  66.6 1.2 collective-permute-start.12
  67.8 3.7 %collective-permute-start.13 = (f32[27,128]{1,0:T(8,128)S(1)}, f32[27,128]{1,0:T(8,128)S(1)}, u32[]{:S(2)}, u32[]{:S(2)}) collective-permute-start(f32[27,128]{1,0:T(8,128)S(1)} %add.155), channel_id=1, source_target_pairs={{0,2},{1,3},{2,0},{3,1},{4,6},{5,7},{6,4},{7,5},{8,10},{9,11},{10,... | collective-permute-start | bytes 41480 | tf_op jit(solution)/shard_map/ppermute | solution.py:401
  71.6 4.8 %copy-start.30 = (bf16[4,128,2048]{2,1,0:T(8,128)(2,1)S(1)}, bf16[4,128,2048]{2,1,0:T(8,128)(2,1)}, u32[]{:S(2)}) copy-start(bf16[4,128,2048]{2,1,0:T(8,128)(2,1)} %param.9) | copy-start | bytes 6291460
  75.3 1.0 copy-start.3
  84.6 21.8 %collective-permute-start.17 = (bf16[512,2048]{1,0:T(8,128)(2,1)}, bf16[512,2048]{1,0:T(8,128)(2,1)}, u32[]{:S(2)}, u32[]{:S(2)}) collective-permute-start(bf16[512,2048]{1,0:T(8,128)(2,1)} %share.5), channel_id=1, source_target_pairs={{0,1},{1,0},{2,3},{3,2},{4,5},{5,4},{6,7},{7,6},{8,9},{9,8},{10,11... | collective-permute-start | bytes 6291464 | tf_op jit(solution)/shard_map/ppermute | solution.py:401
  84.6 50.5 %collective-permute-start.16 = (bf16[512,2048]{1,0:T(8,128)(2,1)}, bf16[512,2048]{1,0:T(8,128)(2,1)}, u32[]{:S(2)}, u32[]{:S(2)}) collective-permute-start(bf16[512,2048]{1,0:T(8,128)(2,1)} %share.6), channel_id=1, source_target_pairs={{0,1},{1,0},{2,3},{3,2},{4,5},{5,4},{6,7},{7,6},{8,9},{9,8},{10,11... | collective-permute-start | bytes 6291464 | tf_op jit(solution)/shard_map/ppermute | solution.py:401
  85.1 66.0 %all-to-all-start.1 = ((bf16[4,72,2048]{2,1,0:T(8,128)(2,1)}), bf16[4,72,2048]{2,1,0:T(8,128)(2,1)S(1)}, u32[]{:S(2)}, u32[]{:S(2)}) async-start(bf16[4,72,2048]{2,1,0:T(8,128)(2,1)} %copy-done.3), calls=%async_computation.1 | async-start | bytes 2359296 | tf_op jit(solution)/shard_map/all_to_all | solution.py:420
  88.9 35.2 %collective-permute-start.14 = (bf16[136,2176]{1,0:T(8,128)(2,1)}, bf16[136,2176]{1,0:T(8,128)(2,1)S(1)}, u32[]{:S(2)}, u32[]{:S(2)}) collective-permute-start(bf16[136,2176]{1,0:T(8,128)(2,1)} %copy-done.24), channel_id=1, source_target_pairs={{0,4},{4,0},{8,12},{12,8},{1,5},{5,1},{9,13},{13,9},{2,6},{6,2},{1... | collective-permute-start | bytes 1775624 | tf_op jit(solution)/shard_map/ppermute | solution.py:401
  92.6 9.6 %copy-start.7 = (s32[512,1]{1,0:T(8,128)S(1)}, s32[512,1]{1,0:T(8,128)}, u32[]{:S(2)}) copy-start(s32[512,1]{1,0:T(8,128)} %copy-done.6) | copy-start | bytes 6148
  92.6 42.5 %collective-permute-start.15 = (bf16[128,2176]{1,0:T(8,128)(2,1)S(1)}, bf16[128,2176]{1,0:T(8,128)(2,1)S(1)}, u32[]{:S(2)}, u32[]{:S(2)}) collective-permute-start(bf16[128,2176]{1,0:T(8,128)(2,1)S(1)} %constant_dynamic-update-slice_fusion.2), channel_id=1, source_target_pairs={{0,4},{4,0},{8,12},{12,8},{1,5},{5,1},{9,13},{13,9},{2,6},{6,2},{1... | collective-permute-start | bytes 1671176 | tf_op jit(solution)/shard_map/ppermute | solution.py:401
  93.0 9.2 %copy-start.26 = (bf16[64,16,2048]{2,1,0:T(8,128)(2,1)S(1)}, bf16[64,16,2048]{2,1,0:T(8,128)(2,1)}, u32[]{:S(2)}) copy-start(bf16[64,16,2048]{2,1,0:T(8,128)(2,1)} %param.12) | copy-start | bytes 12582916
  100.9 1.3 copy-start
  106.4 4.5 %copy-start.2 = (bf16[512,2048]{1,0:T(8,128)(2,1)}, bf16[512,2048]{1,0:T(8,128)(2,1)S(1)}, u32[]{:S(2)}) copy-start(bf16[512,2048]{1,0:T(8,128)(2,1)S(1)} %deltas.8.refs_13_) | copy-start | bytes 6291460
  106.4 28.7 %copy-start.28 = (bf16[64,16,2048]{2,1,0:T(8,128)(2,1)S(1)}, bf16[64,16,2048]{2,1,0:T(8,128)(2,1)}, u32[]{:S(2)}) copy-start(bf16[64,16,2048]{2,1,0:T(8,128)(2,1)} %param.11) | copy-start | bytes 12582916
  145.5 5.1 %copy-start.9 = (s32[136,1]{1,0:T(8,128)}, s32[136,1]{1,0:T(8,128)S(1)}, u32[]{:S(2)}) copy-start(s32[136,1]{1,0:T(8,128)S(1)} %get-tuple-element.262.refs_2_) | copy-start | bytes 1636
  145.5 1.2 collective-permute-start.18
  146.7 3.9 %collective-permute-start.19 = (f32[49,128]{1,0:T(8,128)S(1)}, f32[49,128]{1,0:T(8,128)S(1)}, u32[]{:S(2)}, u32[]{:S(2)}) collective-permute-start(f32[49,128]{1,0:T(8,128)S(1)} %add.158), channel_id=1, source_target_pairs={{0,2},{1,3},{2,0},{3,1},{4,6},{5,7},{6,4},{7,5},{8,10},{9,11},{10,... | collective-permute-start | bytes 75272 | tf_op jit(solution)/shard_map/ppermute | solution.py:401
  151.2 50.2 %collective-permute-start.24 = (bf16[512,2048]{1,0:T(8,128)(2,1)}, bf16[512,2048]{1,0:T(8,128)(2,1)}, u32[]{:S(2)}, u32[]{:S(2)}) collective-permute-start(bf16[512,2048]{1,0:T(8,128)(2,1)} %add_convert_fusion.1), channel_id=1, source_target_pairs={{0,2},{1,3},{2,0},{3,1},{4,6},{5,7},{6,4},{7,5},{8,10},{9,11},{10,... | collective-permute-start | bytes 6291464 | tf_op jit(solution)/shard_map/ppermute | solution.py:401
  156.7 25.5 %copy-start.5 = (s32[512,1]{1,0:T(8,128)S(1)}, s32[512,1]{1,0:T(8,128)}, u32[]{:S(2)}) copy-start(s32[512,1]{1,0:T(8,128)} %copy-done.4) | copy-start | bytes 6148
  156.7 44.6 %copy-start.1 = (bf16[512,2048]{1,0:T(8,128)(2,1)S(1)}, bf16[512,2048]{1,0:T(8,128)(2,1)}, u32[]{:S(2)}) copy-start(bf16[512,2048]{1,0:T(8,128)(2,1)} %copy-done) | copy-start | bytes 6291460
  163.6 14.9 %collective-permute-start.20 = (bf16[128,2048]{1,0:T(8,128)(2,1)S(1)}, bf16[128,2048]{1,0:T(8,128)(2,1)S(1)}, u32[]{:S(2)}, u32[]{:S(2)}) collective-permute-start(bf16[128,2048]{1,0:T(8,128)(2,1)S(1)} %get-tuple-element.270), channel_id=1, source_target_pairs={{0,4},{4,0},{8,12},{12,8},{1,5},{5,1},{9,13},{13,9},{2,6},{6,2},{1... | collective-permute-start | bytes 1572872 | tf_op jit(solution)/shard_map/ppermute | solution.py:401
  164.1 30.1 %collective-permute-start.23 = (bf16[136,2048]{1,0:T(8,128)(2,1)}, bf16[136,2048]{1,0:T(8,128)(2,1)}, u32[]{:S(2)}, u32[]{:S(2)}) collective-permute-start(bf16[136,2048]{1,0:T(8,128)(2,1)} %get-tuple-element.272), channel_id=1, source_target_pairs={{0,4},{4,0},{8,12},{12,8},{1,5},{5,1},{9,13},{13,9},{2,6},{6,2},{1... | collective-permute-start | bytes 1671176 | tf_op jit(solution)/shard_map/ppermute | solution.py:401
  179.3 14.9 %collective-permute-start.21 = (bf16[64,2048]{1,0:T(8,128)(2,1)}, bf16[64,2048]{1,0:T(8,128)(2,1)}, u32[]{:S(2)}, u32[]{:S(2)}) collective-permute-start(bf16[64,2048]{1,0:T(8,128)(2,1)} %get-tuple-element.317), channel_id=1, source_target_pairs={{0,8},{4,12},{8,0},{12,4},{1,9},{5,13},{9,1},{13,5},{2,10},{6,14},... | collective-permute-start | bytes 786440 | tf_op jit(solution)/shard_map/ppermute | solution.py:401
  181.8 19.6 %collective-permute-start.22 = (bf16[64,2048]{1,0:T(8,128)(2,1)}, bf16[64,2048]{1,0:T(8,128)(2,1)}, u32[]{:S(2)}, u32[]{:S(2)}) collective-permute-start(bf16[64,2048]{1,0:T(8,128)(2,1)} %get-tuple-element.316), channel_id=1, source_target_pairs={{0,12},{4,8},{8,4},{12,0},{1,13},{5,9},{9,5},{13,1},{2,14},{6,10},... | collective-permute-start | bytes 786440 | tf_op jit(solution)/shard_map/ppermute | solution.py:401
  182.9 3.6 %collective-permute-start.25 = (s32[1,1]{1,0:T(1,128)}, s32[1,1]{1,0:T(1,128)}, u32[]{:S(2)}, u32[]{:S(2)}) collective-permute-start(s32[1,1]{1,0:T(1,128)} %get-tuple-element.237.refs_1_), channel_id=1, source_target_pairs={{0,16},{16,0},{1,17},{17,1},{2,18},{18,2},{3,19},{19,3},{4,20},{20... | collective-permute-start | bytes 20 | tf_op jit(solution)/shard_map/ppermute | solution.py:401
  (18 other events, 12.6 us)

commit v2 on v0

--- a/solution.py
+++ b/solution.py
@@ -31,30 +31,36 @@
     return v
 
 
-def score_kernel(dists, *refs):
+def score_kernel(dists, block, *refs):
+    me_ref, known_ref, refs = refs[0], refs[1], refs[2:]
     m = len(dists)
-    got, known, a_ref = refs[:m], refs[m:-m - 3], refs[-m - 3]
-    out_ref, slots, acc = refs[-m - 2], refs[-m - 1:-1], refs[-1]
+    got, a_ref, refs = refs[:1 if block else m], refs[1 if block else m], refs[(2 if block else m + 1):]
+    out_ref, told_ref, slots, acc = refs[0], refs[1], refs[2:-1], refs[-1]
     g = pl.program_id(0)
     per, width = a_ref.shape[0] // 16, a_ref.shape[1]
+
+    def view(i, low, high):
+        return got[0][me_ref[0] ^ (i + 1), :, low:high] if block else got[i][:, low:high]
 
     @pl.when(g == 0)
     def _():
         acc[...] = jnp.zeros_like(acc)
+        told_ref[...] = known_ref[0:1, 0:1]
         for i, dist in enumerate(dists):
             if dist is None:
-                slots[i][...] = known[0][...]
-            else:
-                meta = got[i][:, width:].astype(jnp.float32).astype(jnp.int32)
-                if dist == RELAY:
-                    dist = (2 + lax.broadcasted_iota(jnp.int32, (meta.shape[0], 1), 0) // SHARED) ^ 1
-                slots[i][...] = jnp.where(meta[:, 1:2] == dist, meta[:, 0:1] - 1, -1)
+                slots[i][...] = known_ref[...]
+                continue
+            meta = view(i, width, width + META).astype(jnp.float32).astype(jnp.int32)
+            if dist == RELAY:
+                dist = (2 + lax.broadcasted_iota(jnp.int32, (meta.shape[0], 1), 0) // SHARED) ^ 1
+            slots[i][...] = jnp.where(meta[:, 1:2] == dist, meta[:, 0:1] - 1, -1)
+            told_ref[...] = jnp.maximum(told_ref[...], meta[0:1, 2:3])
 
     off = 0
     for i in range(m):
-        n = got[i].shape[0]
+        n = slots[i].shape[0]
         s = lax.dot_general(
-            got[i][:, :width], a_ref[...], (((1,), (1,)), ((), ())), preferred_element_type=jnp.float32
+            view(i, 0, width), a_ref[...], (((1,), (1,)), ((), ())), preferred_element_type=jnp.float32
         )
         s = jnp.where(group_of(s.shape) + g * per == slots[i][...], s, 0.0)
         v = s[:, :128]
@@ -67,7 +73,7 @@
     def _():
         off = 0
         for i in range(m):
-            n = got[i].shape[0]
+            n = slots[i].shape[0]
             v = fold(acc[off:off + n, :])
             v = jnp.where(group_of(v.shape) == row_of(v.shape), v, 0.0)
             out_ref[off // 8:(off + n) // 8, :] = jnp.sum(v.reshape(n // 8, 8, 128), axis=1)
@@ -75,26 +81,28 @@
 
 
 def whole(shape):
-    return pl.BlockSpec(shape, lambda g: (0, 0))
-
-
-def scores(dists, got, known, store):
-    sizes = [v.shape[0] for v in got]
+    return pl.BlockSpec(shape, lambda g: (0,) * len(shape))
+
+
+def scores(me, known, dists, got, store):
+    block = got[0].ndim == 3
+    sizes = [got[0].shape[1]] * len(dists) if block else [v.shape[0] for v in got]
     total, width = sum(sizes), store.shape[1]
     blk = 256
     out = pl.pallas_call(
-        functools.partial(score_kernel, tuple(dists)),
+        functools.partial(score_kernel, tuple(dists), block),
         grid=(store.shape[0] // blk,),
-        in_specs=[whole(v.shape) for v in got + known] + [pl.BlockSpec((blk, width), lambda g: (g, 0))],
-        out_specs=[whole((total // 8, 128))] + [whole((n, 1)) for n in sizes],
-        out_shape=[jax.ShapeDtypeStruct((total // 8, 128), jnp.float32)]
+        in_specs=[pl.BlockSpec(memory_space=pltpu.SMEM), whole(known.shape)]
+        + [whole(v.shape) for v in got] + [pl.BlockSpec((blk, width), lambda g: (g, 0))],
+        out_specs=[whole((total // 8, 128)), whole((1, 1))] + [whole((n, 1)) for n in sizes],
+        out_shape=[jax.ShapeDtypeStruct((total // 8, 128), jnp.float32), jax.ShapeDtypeStruct((1, 1), jnp.int32)]
         + [jax.ShapeDtypeStruct((n, 1), jnp.int32) for n in sizes],
         scratch_shapes=[pltpu.VMEM((total, 128), jnp.float32)],
         compiler_params=pltpu.CompilerParams(vmem_limit_bytes=VMEM),
         cost_estimate=FREE,
         name="scores",
-    )(*got, *known, store)
-    return out[0], list(out[1:])
+    )(me, known, *got, store)
+    return out[0], out[1], list(out[2:])
 
 
 def spread_out(slots, packed, depth, spread):
@@ -259,7 +267,7 @@
 
 
 def pack_kernel(n_dp, seg_len, shift, me_ref, ids_ref, lives_ref, index_ref, x_ref,
-                table_ref, row_ref, self_ref, meta_ref, *outs):
+                table_ref, row_ref, self_ref, meta_ref, rounds_ref, *outs):
     me = me_ref[0]
     count, (rows, width) = ids_ref.shape[1], x_ref.shape
     big = 2 * rows
@@ -296,8 +304,9 @@
     for j in range(2, n_dp):
         held = OWN + 2 * SHARED if j % 2 == 0 else OWN + jnp.maximum(2 * SHARED - over_of(dist, lives, j), 0)
         left = jnp.maximum(left, total(dist, lives, j) - held)
-    rounds = ((jnp.maximum(left, 0) + ROUND - 1) // ROUND).astype(jnp.float32)
-    told = jnp.where(lax.broadcasted_iota(jnp.int32, (1, META), 1) == 2, rounds, 0.0)
+    rounds = (jnp.maximum(left, 0) + ROUND - 1) // ROUND
+    rounds_ref[...] = rounds
+    told = jnp.where(lax.broadcasted_iota(jnp.int32, (1, META), 1) == 2, rounds.astype(jnp.float32), 0.0)
 
     far = range(2, n_dp)
     codes = [far_code(big, j, over_of(dist, lives, j), 0) for j in far] + [near_code(big, 0)]
@@ -322,7 +331,7 @@
     sizes = [SHARED + OWN] * (n_dp - 2) + [NEAR]
     parts = [SHARED] * (n_dp - 2) + [NEAR - OWN] + [OWN] * (n_dp - 1)
     shapes = [((2, count), jnp.int32), ((rows, 1), jnp.int32), ((rows, 1), jnp.int32)]
-    shapes += [((rows, META), jnp.bfloat16)]
+    shapes += [((rows, META), jnp.bfloat16), ((1, 1), jnp.int32)]
     shapes += [((n, width + META), jnp.bfloat16) for n in sizes] + [((1, n), jnp.int32) for n in parts]
     return pl.pallas_call(
         functools.partial(pack_kernel, n_dp, seg_len, shift),
@@ -397,9 +406,17 @@
             k *= 2
         return v
 
-    def answer(dists, got, known=()):
-        scored, slots = scores(dists, got, list(known), shrink_store)
-        return slots, butterfly(scored, "tp", jnp.add)
+    def answer(dists, got, known):
+        scored, told, slots = scores(me, known, dists, got, shrink_store)
+        return slots, told, butterfly(scored, "tp", jnp.add)
+
+    def total_of(parts):
+        if len(parts) == 1:
+            return parts[0]
+        return functools.reduce(jnp.add, [v.astype(jnp.float32) for v in parts]).astype(jnp.bfloat16)
+
+    def a2a(v):
+        return lax.all_to_all(v, "dp", split_axis=0, concat_axis=0, tiled=True)
 
     def after(v, *others):
         return lax.optimization_barrier((v, others))[0]
@@ -411,15 +428,15 @@
         adapter_store_index.reshape(1, -1),
         x, n_dp, seg_len, shift,
     ))
-    table, row_code, self_slots, meta = packed[:4]
+    table, row_code, self_slots, meta, rounds = packed[:5]
     m = len(far)
-    out_far, out_near = packed[4:4 + m], packed[4 + m]
-    codes, block_codes = packed[5 + m:6 + 2 * m], packed[6 + 2 * m:]
+    out_far, out_near = packed[5:5 + m], packed[5 + m]
+    codes, block_codes = packed[6 + m:7 + 2 * m], packed[7 + 2 * m:]
 
     in_far = [swap(v, "dp", j) for v, j in zip(out_far, far)]
     in_near = swap(out_near, "dp", 1)
 
-    found, self_part = answer([None], [after(x, table)], [self_slots])
+    found, _, self_part = answer([None], [after(x, table)], self_slots)
     (self_delta,) = deltas(found, self_part, expand_store)
 
     at = after(lax.axis_index("tp").reshape(1), table)
@@ -427,60 +444,58 @@
     shares = {k: share(at ^ k, x, weight, cols) for k in reversed(range(n_tp))}
     (in_far, in_near, shares), _ = lax.optimization_barrier(((in_far, in_near, shares), self_delta))
 
+    found, rounds, part = answer(list(far) + [1], in_far + [in_near], rounds)
+    in_far, shares, _ = lax.optimization_barrier((in_far, shares, rounds))
     in_relay = swap(jnp.concatenate([v[:SHARED] for v in in_far]), "dp", 1)
-    found, part = answer(list(far) + [1], in_far + [in_near])
     direct = deltas(found, part, expand_store, me, n_dp)
-    block = lax.all_to_all(direct[-1], "dp", split_axis=0, concat_axis=0, tiled=True)
+    block = a2a(direct[-1])
 
     adds = {k: [shares[k]] for k in shares}
     for k in range(1, n_tp, 2):
         adds[k ^ 1].append(swap(adds.pop(k)[0], "tp", 1))
-    told = [v[0, width + 2] for v in in_far + [in_near, out_near]]
-    rounds = functools.reduce(jnp.maximum, told).astype(jnp.int32).reshape(1, 1)
-    rounds = butterfly(rounds, "rep", jnp.maximum)
-
-    found, part = answer([RELAY], [after(in_relay, direct)])
-    part, adds, rounds = lax.optimization_barrier((part, adds, rounds))
-    rounds = rounds[0, 0]
+    for k in range(2, n_tp, 2):
+        adds[k] = [total_of(adds[k])]
+
+    in_relay, direct, adds = lax.optimization_barrier((in_relay, direct, adds))
+    found, _, part = answer([RELAY], [in_relay], rounds)
+    part, adds = lax.optimization_barrier((part, adds))
     (relayed,) = deltas(found, part, expand_store)
     relayed = swap(relayed, "dp", 1)
     bit = 2
     while bit < n_tp:
         for k in sorted((k for k in adds if k & bit), reverse=True):
-            v = functools.reduce(jnp.add, [u.astype(jnp.float32) for u in adds.pop(k)])
-            adds[k ^ bit].append(swap(v.astype(jnp.bfloat16), "tp", bit))
+            adds[k ^ bit].append(swap(total_of(adds.pop(k)), "tp", bit))
         bit *= 2
-    near, _ = lax.optimization_barrier((direct[m], relayed))
+    relayed, block, near, direct = lax.optimization_barrier((relayed, block, direct[m], direct))
     back = [swap(direct[i] + relayed[i * SHARED:(i + 1) * SHARED], "dp", j) for i, j in enumerate(far)]
     back.append(swap(near, "dp", 1))
     adds = adds[0] + [self_delta]
-
-    def rest():
-        pos, alive = table[0], table[1]
+    rounds = butterfly(rounds, "rep", jnp.maximum)[0, 0]
+
+    def late_round(i, out):
+        tab, rows_in, rows_meta, places = lax.optimization_barrier((table, x, meta, row_code, i))[:4]
+        pos, alive = tab[0], tab[1]
         dist = (pos >> shift) ^ me[0]
         held = [None, jnp.int32(NEAR)]
         for j in range(2, n_dp, 2):
             extra = jnp.maximum(jnp.sum(jnp.where(dist == j, alive, 0)) - OWN, 0)
             held += [jnp.int32(OWN + 2 * SHARED), OWN + jnp.maximum(2 * SHARED - extra, 0)]
-        x_meta = jnp.concatenate([x, meta], axis=1)
-
-        def body(i, extra):
-            code = [j * big + held[j] + i * ROUND + jnp.arange(ROUND, dtype=jnp.int32) for j in range(1, n_dp)]
-            got = []
-            for j, c in zip(range(1, n_dp), code):
-                pick = (c[:, None] == row_code.reshape(1, rows)).astype(jnp.bfloat16)
-                v = jnp.dot(pick, x_meta, preferred_element_type=jnp.float32).astype(jnp.bfloat16)
-                got.append(swap(v, "dp", j))
-            found, part = answer(list(range(1, n_dp)), got)
-            for j, c, v in zip(range(1, n_dp), code, deltas(found, part, expand_store)):
-                put = (row_code == c[None, :]).astype(jnp.bfloat16)
-                extra = extra + jnp.dot(put, swap(v, "dp", j), preferred_element_type=jnp.float32)
-            return extra
-
-        extra = lax.fori_loop(0, rounds, body, jnp.zeros((rows, width), jnp.float32))
-        return finish(me, row_code, codes, block_codes, back, block, adds + [extra])
-
-    out = lax.cond(rounds > 0, rest, lambda: finish(me, row_code, codes, block_codes, back, block, adds))
+        x_meta = jnp.concatenate([rows_in, rows_meta], axis=1)
+        code = [j * big + held[j] + i * ROUND + jnp.arange(ROUND, dtype=jnp.int32) for j in range(1, n_dp)]
+        got = []
+        for j, c in zip(range(1, n_dp), code):
+            pick = (c[:, None] == places.reshape(1, rows)).astype(jnp.bfloat16)
+            v = jnp.dot(pick, x_meta, preferred_element_type=jnp.float32).astype(jnp.bfloat16)
+            got.append(swap(v, "dp", j))
+        found, _, part = answer(list(range(1, n_dp)), got, rounds.reshape(1, 1))
+        total = out.astype(jnp.float32)
+        for j, c, v in zip(range(1, n_dp), code, deltas(found, part, expand_store)):
+            put = (places == c[None, :]).astype(jnp.bfloat16)
+            total = total + jnp.dot(put, swap(v, "dp", j), preferred_element_type=jnp.float32)
+        return total.astype(jnp.bfloat16)
+
+    out = finish(me, row_code, codes, block_codes, back, block, adds)
+    out = lax.fori_loop(0, rounds, late_round, out)
     return out.reshape(steps, rows_dev, width)
 
 

time: 171 us -> 165 us (0.965)
  waiting for transfers between devices: 52.8 us -> 42 us
  local copies, waits for them, and re-layouts: 6.78 us -> 12.2 us
  other arithmetic: 5.44 us -> 8.21 us
  starting transfers between devices: 30.2 us -> 27.6 us
  between operations: 3.51 us -> 1.6 us
    ppermute x18, waiting for transfers between devices: 52.8 us -> 33.9 us  [swap(): return lax.ppermute(v, axis, [(i, i ^ k) for i in range(n)])]
    all_to_all x1, waiting for transfers between devices: 0.01 us -> 8.13 us  [a2a(): return lax.all_to_all(v, 'dp', split_axis=0, concat_axis=0, tiled=True)]
    unnamed x26 -> x50, local copies, waits for them, and re-layouts: 2.04 us -> 9.93 us
    pallas_call x3, Pallas kernels: 17.1 us -> 11.4 us  [deltas(): pl.pallas_call(kernel, grid=(width // cols,), in_specs=first + ins, out_s...]
    pallas_call x3, Pallas kernels: 12.9 us -> 18.5 us  [scores(): pl.pallas_call(functools.partial(score_kernel, tuple(dists), block), grid...]
    slice x4 -> x0, local copies, waits for them, and re-layouts: 3.18 us -> none  [per_device(): told = [v[0, width + 2] for v in in_far + [in_near, out_near]]]
    ppermute x18, starting transfers between devices: 26.4 us -> 23.8 us  [swap(): return lax.ppermute(v, axis, [(i, i ^ k) for i in range(n)])]
  transfers between devices with their start and end apart: 19 -> 19, of which waited for: 8 -> 9; matrix products, arithmetic and copies ran while one was open for 3% -> 5% of each run, Pallas kernels for 36% -> 32%
where the time goes in v2:
time: 165 us; the launch traced here: 164 us
  Pallas kernels  72.7 us (44%)
  waiting for transfers between devices  42 us (25%)
  starting transfers between devices  27.6 us (17%)
  local copies, waits for them, and re-layouts  12.2 us (7%)
  other arithmetic  8.21 us (5%)
    ppermute x18, waiting for transfers between devices, swap(): return lax.ppermute(v, axis, [(i, i ^ k) for i in range(n)])  33.9 us
    pallas_call x4, Pallas kernels, share(): pl.pallas_call(share_kernel, grid_spec=pltpu.PrefetchScalarGridSpec(num_s...  30.8 us
    ppermute x18, starting transfers between devices, swap(): return lax.ppermute(v, axis, [(i, i ^ k) for i in range(n)])  23.8 us
    pallas_call x3, Pallas kernels, scores(): pl.pallas_call(functools.partial(score_kernel, tuple(dists), block), grid...  18.5 us
    pallas_call x3, Pallas kernels, deltas(): pl.pallas_call(kernel, grid=(width // cols,), in_specs=first + ins, out_s...  11.4 us
    unnamed x50, local copies, waits for them, and re-layouts  9.93 us
    all_to_all x1, waiting for transfers between devices, a2a(): return lax.all_to_all(v, 'dp', split_axis=0, concat_axis=0, tiled=True)  8.13 us
    pallas_call x1, Pallas kernels, finish(): pl.pallas_call(functools.partial(finish_kernel, len(codes), n_dp), grid=(...  7.5 us
  transfers between devices with their start and end apart: 19, of which 9 were waited for; matrix products, arithmetic and copies ran while one was open for 5% of the time, Pallas kernels for 32%

profile of v2, /device:TPU:0, one launch (start us, length us, event | category | flops | bytes accessed | tf_op | source)
XLA Modules:
  0.0 164.3 jit_solution(15806997915468717928)
XLA Ops:
  2.2 4.5 %pack.1 = (s32[2,32]{1,0:T(2,128)}, s32[512,1]{1,0:T(8,128)S(1)}, s32[512,1]{1,0:T(8,128)S(1)}, bf16[512,128]{1,0:T(8,128)(2,1)}, s32[1,1]{1,0:T(1,128)}, /*inde...) custom-call(s32[1]{0:T(128)} %bitcast.1.me_ref.refs_0_, ...), custom_call_target="tpu_custom_call" | custom-call | tf_op jit(solution)/shard_map/pack/pallas_call | solution.py:336
  6.8 3.1 %collective-permute-start.10 = (bf16[208,2176]{1,0:T(8,128)(2,1)}, bf16[208,2176]{1,0:T(8,128)(2,1)}, u32[]{:S(2)}, u32[]{:S(2)}) collective-permute-start(bf16[208,2176]{1,0:T(8,128)(2,1)} %get-tuple-element.233), channel_id=1, source_target_pairs={{0,4},{4,0},{8,12},{12,8},{1,5},{5,1},{9,13},{13,9},{2,6},{6,2},{1... | collective-permute-start | bytes 2715656 | tf_op jit(solution)/shard_map/ppermute | solution.py:400
  9.9 2.6 %collective-permute-start.8 = (bf16[136,2176]{1,0:T(8,128)(2,1)}, bf16[136,2176]{1,0:T(8,128)(2,1)S(1)}, u32[]{:S(2)}, u32[]{:S(2)}) collective-permute-start(bf16[136,2176]{1,0:T(8,128)(2,1)} %get-tuple-element.231), channel_id=1, source_target_pairs={{0,8},{4,12},{8,0},{12,4},{1,9},{5,13},{9,1},{13,5},{2,10},{6,14},... | collective-permute-start | bytes 1775624 | tf_op jit(solution)/shard_map/ppermute | solution.py:400
  12.5 5.8 %scores.7 = (f32[64,128]{1,0:T(8,128)S(1)}, s32[1,1]{1,0:T(1,128)}, s32[512,1]{1,0:T(8,128)S(1)}) custom-call(s32[1]{0:T(128)} %bitcast.1.me_ref.refs_0_, s32[512,1]{1,0:T(8,128)S(1)} %get-tuple-element.236.refs_1_, bf16[512,2048]{1,0:T(8,128)(2,1)S(1)} %bitcast.40, bf16[1024,2048]{1,0:T(8,128)(2,1)} %bitcast.34), custom_call_target="tpu_custom_call" | custom-call | tf_op jit(solution)/shard_map/scores/pallas_call | solution.py:92
  20.8 1.7 %collective-permute-start.12 = (f32[64,128]{1,0:T(8,128)}, f32[64,128]{1,0:T(8,128)}, u32[]{:S(2)}, u32[]{:S(2)}) collective-permute-start(f32[64,128]{1,0:T(8,128)} %add.153), channel_id=1, source_target_pairs={{0,2},{1,3},{2,0},{3,1},{4,6},{5,7},{6,4},{7,5},{8,10},{9,11},{10,... | collective-permute-start | bytes 98312 | tf_op jit(solution)/shard_map/ppermute | solution.py:400
  22.6 7.1 %share.4.refs_10_ = bf16[512,2048]{1,0:T(8,128)(2,1)S(1)} custom-call(s32[1]{0:T(128)} %bitcast.4.at_ref, bf16[512,2048]{1,0:T(8,128)(2,1)S(1)} %bitcast.41, bf16[2048,8192]{1,0:T(8,128)(2,1)} %w_ref.7), custom_call_target="tpu_custom_call" | custom-call | tf_op jit(solution)/shard_map/share/pallas_call | solution.py:354
  31.0 8.3 %share.5 = bf16[512,2048]{1,0:T(8,128)(2,1)} custom-call(s32[1]{0:T(128)S(6)} %xor.22.at_ref, bf16[512,2048]{1,0:T(8,128)(2,1)S(1)} %bitcast.42, bf16[2048,8192]{1,0:T(8,128)(2,1)} %w_ref.7), custom_call_target="tpu_custom_call" | custom-call | tf_op jit(solution)/shard_map/share/pallas_call | solution.py:354
  39.3 7.1 %share.6 = bf16[512,2048]{1,0:T(8,128)(2,1)S(1)} custom-call(s32[1]{0:T(128)S(6)} %xor.23.at_ref, bf16[512,2048]{1,0:T(8,128)(2,1)S(1)} %bitcast.43, bf16[2048,8192]{1,0:T(8,128)(2,1)} %w_ref.7), custom_call_target="tpu_custom_call" | custom-call | tf_op jit(solution)/shard_map/share/pallas_call | solution.py:354
  46.4 8.3 %share.7 = bf16[512,2048]{1,0:T(8,128)(2,1)} custom-call(s32[1]{0:T(128)S(6)} %xor.24.at_ref, bf16[512,2048]{1,0:T(8,128)(2,1)S(1)} %bitcast.44, bf16[2048,8192]{1,0:T(8,128)(2,1)} %w_ref.7), custom_call_target="tpu_custom_call" | custom-call | tf_op jit(solution)/shard_map/share/pallas_call | solution.py:354
  55.5 4.1 %deltas.7.refs_13_ = bf16[512,2048]{1,0:T(8,128)(2,1)S(1)} custom-call(s32[512,1]{1,0:T(8,128)S(1)} %copy-done.5, f32[64,128]{1,0:T(8,128)S(1)} %add.154.refs_1_, bf16[1024,2048]{1,0:T(8,128)(2,1)S(1)} %bitcast.31), custom_call_target="tpu_custom_call" | custom-call | tf_op jit(solution)/shard_map/deltas/pallas_call | solution.py:168
  59.7 1.3 copy-done.2
  61.0 7.6 %scores.8 = (f32[60,128]{1,0:T(8,128)S(1)}, s32[1,1]{1,0:T(1,128)}, s32[136,1]{1,0:T(8,128)S(1)}, s32[136,1]{1,0:T(8,128)S(1)}, s32[208,1]{1,0:T(8,128)S(1)}) custom-call(s32[1]{0:T(128)} %bitcast.1.me_ref.refs_0_, s32[1,1]{1,0:T(1,128)} %get-tuple-element.230.refs_1_, bf16[136,2176]{1,0:T(8,128)(2,1)S(1)} %collective-permute-done.8.refs_2_, ...), custom_call_target="tpu_custom_call" | custom-call | tf_op jit(solution)/shard_map/scores/pallas_call | solution.py:92
  69.2 3.7 %collective-permute-done.14 = f32[60,128]{1,0:T(8,128)S(1)} collective-permute-done((f32[60,128]{1,0:T(8,128)S(1)}, f32[60,128]{1,0:T(8,128)S(1)}, u32[]{:S(2)}, u32[]{:S(2)}) %collective-permute-start.14) | collective-permute-done | bytes 30752 | tf_op jit(solution)/shard_map/ppermute | solution.py:400
  74.1 4.7 %collective-permute-start.13 = (bf16[128,2176]{1,0:T(8,128)(2,1)}, bf16[128,2176]{1,0:T(8,128)(2,1)}, u32[]{:S(2)}, u32[]{:S(2)}) collective-permute-start(bf16[128,2176]{1,0:T(8,128)(2,1)} %pad_maximum_fusion), channel_id=1, source_target_pairs={{0,4},{4,0},{8,12},{12,8},{1,5},{5,1},{9,13},{13,9},{2,6},{6,2},{1... | collective-permute-start | bytes 1671176 | tf_op jit(solution)/shard_map/ppermute | solution.py:400
  78.7 4.4 %deltas.8 = (bf16[64,2048]{1,0:T(8,128)(2,1)S(1)}, bf16[64,2048]{1,0:T(8,128)(2,1)S(1)}, bf16[136,2048]{1,0:T(8,128)(2,1)S(1)}, bf16[4,72,2048]{2,1,0:T(8,128)(2,1)S(1)}) custom-call(s32[1]{0:T(128)} %bitcast.1.me_ref.refs_0_, s32[136,1]{1,0:T(8,128)S(1)} %get-tuple-element.250.refs_0_, s32[136,1]{1,0:T(8,128)S(1)} %get-tuple-element.251.refs_1_, ...), custom_call_target="tpu_custom_call" | custom-call | tf_op jit(solution)/shard_map/deltas/pallas_call | solution.py:168
  86.4 3.8 %all-to-all-start = ((bf16[4,72,2048]{2,1,0:T(8,128)(2,1)}), bf16[4,72,2048]{2,1,0:T(8,128)(2,1)S(1)}, u32[]{:S(2)}, u32[]{:S(2)}) async-start(bf16[4,72,2048]{2,1,0:T(8,128)(2,1)} %copy-done.3), calls=%async_computation | async-start | bytes 2359296 | tf_op jit(solution)/shard_map/all_to_all | solution.py:419
  90.2 3.9 %add_convert_fusion.1 = bf16[512,2048]{1,0:T(8,128)(2,1)} fusion(bf16[512,2048]{1,0:T(8,128)(2,1)} %collective-permute-done.17, bf16[512,2048]{1,0:T(8,128)(2,1)S(1)} %share.6), kind=kLoop, calls=%fused_computation.32 | loop fusion | flops 4194304 | bytes 6291456 | tf_op jit(solution)/shard_map/convert_element_type | solution.py:416
  94.1 5.0 %scores.9 = (f32[16,128]{1,0:T(8,128)S(1)}, s32[1,1]{1,0:T(1,128)}, s32[128,1]{1,0:T(8,128)S(1)}) custom-call(s32[1]{0:T(128)} %bitcast.1.me_ref.refs_0_, s32[1,1]{1,0:T(1,128)} %get-tuple-element.243.refs_1_, bf16[128,2176]{1,0:T(8,128)(2,1)} %collective-permute-done.13.refs_2_, bf16[1024,2048]{1,0:T(8,128)(2,1)S(1)} %bitcast.37), custom_call_target="tpu_custom_call" | custom-call | tf_op jit(solution)/shard_map/scores/pallas_call | solution.py:92
  100.4 1.5 collective-permute-start.19
  101.9 2.1 %collective-permute-done.19 = f32[16,128]{1,0:T(8,128)S(1)} collective-permute-done((f32[16,128]{1,0:T(8,128)S(1)}, f32[16,128]{1,0:T(8,128)S(1)}, u32[]{:S(2)}, u32[]{:S(2)}) %collective-permute-start.19) | collective-permute-done | bytes 8224 | tf_op jit(solution)/shard_map/ppermute | solution.py:400
  104.0 1.5 collective-permute-start.24
  105.5 2.9 %deltas.9 = bf16[128,2048]{1,0:T(8,128)(2,1)} custom-call(s32[128,1]{1,0:T(8,128)S(1)} %get-tuple-element.263.refs_0_, f32[16,128]{1,0:T(8,128)S(1)} %add.159.refs_1_, bf16[1024,2048]{1,0:T(8,128)(2,1)S(1)} %bitcast.33), custom_call_target="tpu_custom_call" | custom-call | tf_op jit(solution)/shard_map/deltas/pallas_call | solution.py:168
  108.4 2.0 %collective-permute-start.20 = (bf16[128,2048]{1,0:T(8,128)(2,1)}, bf16[128,2048]{1,0:T(8,128)(2,1)}, u32[]{:S(2)}, u32[]{:S(2)}) collective-permute-start(bf16[128,2048]{1,0:T(8,128)(2,1)} %deltas.9), channel_id=1, source_target_pairs={{0,4},{4,0},{8,12},{12,8},{1,5},{5,1},{9,13},{13,9},{2,6},{6,2},{1... | collective-permute-start | bytes 1572872 | tf_op jit(solution)/shard_map/ppermute | solution.py:400
  110.4 8.1 %all-to-all-done.refs_9_ = bf16[4,72,2048]{2,1,0:T(8,128)(2,1)S(1)} async-done(((bf16[4,72,2048]{2,1,0:T(8,128)(2,1)}), bf16[4,72,2048]{2,1,0:T(8,128)(2,1)S(1)}, u32[]{:S(2)}, u32[]{:S(2)}) %all-to-all-start) | async-done | bytes 1179680 | tf_op jit(solution)/shard_map/all_to_all | solution.py:419
  118.6 8.6 %collective-permute-done.20 = bf16[128,2048]{1,0:T(8,128)(2,1)} collective-permute-done((bf16[128,2048]{1,0:T(8,128)(2,1)}, bf16[128,2048]{1,0:T(8,128)(2,1)}, u32[]{:S(2)}, u32[]{:S(2)}) %collective-permute-start.20) | collective-permute-done | bytes 524320 | tf_op jit(solution)/shard_map/ppermute | solution.py:400
  127.1 2.1 %slice_add_fusion = (bf16[64,2048]{1,0:T(8,128)(2,1)}, bf16[64,2048]{1,0:T(8,128)(2,1)}) fusion(bf16[64,2048]{1,0:T(8,128)(2,1)} %copy-done.7, bf16[128,2048]{1,0:T(8,128)(2,1)} %collective-permute-done.20, bf16[64,2048]{1,0:T(8,128)(2,1)} %copy-done.6), kind=kLoop, calls=%fused_computation.34 | loop fusion | flops 262144 | bytes 1572864 | tf_op jit(solution)/shard_map/add | solution.py:470
  129.2 4.0 %collective-permute-start.21 = (bf16[64,2048]{1,0:T(8,128)(2,1)}, bf16[64,2048]{1,0:T(8,128)(2,1)}, u32[]{:S(2)}, u32[]{:S(2)}) collective-permute-start(bf16[64,2048]{1,0:T(8,128)(2,1)} %get-tuple-element.319), channel_id=1, source_target_pairs={{0,8},{4,12},{8,0},{12,4},{1,9},{5,13},{9,1},{13,5},{2,10},{6,14},... | collective-permute-start | bytes 786440 | tf_op jit(solution)/shard_map/ppermute | solution.py:400
  134.3 1.5 collective-permute-start.25
  135.7 2.1 %collective-permute-done.25 = s32[1,1]{1,0:T(1,128)} collective-permute-done((s32[1,1]{1,0:T(1,128)}, s32[1,1]{1,0:T(1,128)}, u32[]{:S(2)}, u32[]{:S(2)}) %collective-permute-start.25) | collective-permute-done | bytes 36 | tf_op jit(solution)/shard_map/ppermute | solution.py:400
  139.2 7.0 %collective-permute-done.21.refs_6_ = bf16[64,2048]{1,0:T(8,128)(2,1)} collective-permute-done((bf16[64,2048]{1,0:T(8,128)(2,1)}, bf16[64,2048]{1,0:T(8,128)(2,1)}, u32[]{:S(2)}, u32[]{:S(2)}) %collective-permute-start.21) | collective-permute-done | bytes 262176 | tf_op jit(solution)/shard_map/ppermute | solution.py:400
  146.2 8.1 %collective-permute-done.22.refs_7_ = bf16[64,2048]{1,0:T(8,128)(2,1)} collective-permute-done((bf16[64,2048]{1,0:T(8,128)(2,1)}, bf16[64,2048]{1,0:T(8,128)(2,1)}, u32[]{:S(2)}, u32[]{:S(2)}) %collective-permute-start.22) | collective-permute-done | bytes 262176 | tf_op jit(solution)/shard_map/ppermute | solution.py:400
  156.8 7.5 %finish.1 = bf16[512,2048]{1,0:T(8,128)(2,1)} custom-call(s32[1]{0:T(128)} %bitcast.1.me_ref.refs_0_, s32[512,1]{1,0:T(8,128)S(1)} %get-tuple-element.288.row_ref, s32[1,64]{1,0:T(1,128)S(1)} %get-tuple-element.224.refs_0_, s32[1,64]{1,0:T(1,128)S(1)} %copy-done.10, s32[1,136]{1,0:T(1,128)S(1)} %get-tuple-element.226.refs_2_, s32[1,72]{1,0:T(1,128)S(1)} %copy-done.12, ...), custom_call_target="tpu_custom_call" | custom-call | tf_op jit(solution)/shard_map/finish/pallas_call | solution.py:200
  (83 shorter events, 16.7 us)
Async XLA Ops:
  2.2 10.3 %copy-start.23 = (bf16[4,128,2048]{2,1,0:T(8,128)(2,1)S(1)}, bf16[4,128,2048]{2,1,0:T(8,128)(2,1)}, u32[]{:S(2)}) copy-start(bf16[4,128,2048]{2,1,0:T(8,128)(2,1)} %param.9) | copy-start | bytes 6291460
  6.8 11.5 %copy-start.9 = (s32[1,64]{1,0:T(1,128)}, s32[1,64]{1,0:T(1,128)S(1)}, u32[]{:S(2)}) copy-start(s32[1,64]{1,0:T(1,128)S(1)} %get-tuple-element.225.refs_1_) | copy-start | bytes 772
  6.8 11.5 %copy-start.11 = (s32[1,72]{1,0:T(1,128)}, s32[1,72]{1,0:T(1,128)S(1)}, u32[]{:S(2)}) copy-start(s32[1,72]{1,0:T(1,128)S(1)} %get-tuple-element.227.refs_3_) | copy-start | bytes 868
  6.8 11.6 %copy-start.13 = (s32[1,72]{1,0:T(1,128)}, s32[1,72]{1,0:T(1,128)S(1)}, u32[]{:S(2)}) copy-start(s32[1,72]{1,0:T(1,128)S(1)} %get-tuple-element.228.refs_4_) | copy-start | bytes 868
  6.8 11.6 %copy-start.15 = (s32[1,72]{1,0:T(1,128)}, s32[1,72]{1,0:T(1,128)S(1)}, u32[]{:S(2)}) copy-start(s32[1,72]{1,0:T(1,128)S(1)} %get-tuple-element.229.refs_5_) | copy-start | bytes 868
  6.8 54.3 %collective-permute-start.10 = (bf16[208,2176]{1,0:T(8,128)(2,1)}, bf16[208,2176]{1,0:T(8,128)(2,1)}, u32[]{:S(2)}, u32[]{:S(2)}) collective-permute-start(bf16[208,2176]{1,0:T(8,128)(2,1)} %get-tuple-element.233), channel_id=1, source_target_pairs={{0,4},{4,0},{8,12},{12,8},{1,5},{5,1},{9,13},{13,9},{2,6},{6,2},{1... | collective-permute-start | bytes 2715656 | tf_op jit(solution)/shard_map/ppermute | solution.py:400
  9.9 51.2 %collective-permute-start.8 = (bf16[136,2176]{1,0:T(8,128)(2,1)}, bf16[136,2176]{1,0:T(8,128)(2,1)S(1)}, u32[]{:S(2)}, u32[]{:S(2)}) collective-permute-start(bf16[136,2176]{1,0:T(8,128)(2,1)} %get-tuple-element.231), channel_id=1, source_target_pairs={{0,8},{4,12},{8,0},{12,4},{1,9},{5,13},{9,1},{13,5},{2,10},{6,14},... | collective-permute-start | bytes 1775624 | tf_op jit(solution)/shard_map/ppermute | solution.py:400
  12.5 48.6 %collective-permute-start.9 = (bf16[136,2176]{1,0:T(8,128)(2,1)}, bf16[136,2176]{1,0:T(8,128)(2,1)S(1)}, u32[]{:S(2)}, u32[]{:S(2)}) collective-permute-start(bf16[136,2176]{1,0:T(8,128)(2,1)} %get-tuple-element.232), channel_id=1, source_target_pairs={{0,12},{4,8},{8,4},{12,0},{1,13},{5,9},{9,5},{13,1},{2,14},{6,10},... | collective-permute-start | bytes 1775624 | tf_op jit(solution)/shard_map/ppermute | solution.py:400
  12.5 10.1 %copy-start.24 = (bf16[4,128,2048]{2,1,0:T(8,128)(2,1)S(1)}, bf16[4,128,2048]{2,1,0:T(8,128)(2,1)}, u32[]{:S(2)}) copy-start(bf16[4,128,2048]{2,1,0:T(8,128)(2,1)} %param.9) | copy-start | bytes 6291460
  19.0 1.2 collective-permute-start.11
  20.8 33.9 %collective-permute-start.12 = (f32[64,128]{1,0:T(8,128)}, f32[64,128]{1,0:T(8,128)}, u32[]{:S(2)}, u32[]{:S(2)}) collective-permute-start(f32[64,128]{1,0:T(8,128)} %add.153), channel_id=1, source_target_pairs={{0,2},{1,3},{2,0},{3,1},{4,6},{5,7},{6,4},{7,5},{8,10},{9,11},{10,... | collective-permute-start | bytes 98312 | tf_op jit(solution)/shard_map/ppermute | solution.py:400
  31.0 8.3 %copy-start.25 = (bf16[4,128,2048]{2,1,0:T(8,128)(2,1)S(1)}, bf16[4,128,2048]{2,1,0:T(8,128)(2,1)}, u32[]{:S(2)}) copy-start(bf16[4,128,2048]{2,1,0:T(8,128)(2,1)} %param.9) | copy-start | bytes 6291460
  46.4 9.1 %copy-start.5 = (s32[512,1]{1,0:T(8,128)S(1)}, s32[512,1]{1,0:T(8,128)}, u32[]{:S(2)}) copy-start(s32[512,1]{1,0:T(8,128)} %copy-done.4) | copy-start | bytes 6148
  46.4 9.1 %copy-start.18 = (bf16[64,16,2048]{2,1,0:T(8,128)(2,1)S(1)}, bf16[64,16,2048]{2,1,0:T(8,128)(2,1)}, u32[]{:S(2)}) copy-start(bf16[64,16,2048]{2,1,0:T(8,128)(2,1)} %param.12) | copy-start | bytes 12582916
  55.5 5.5 %copy-start.21 = (bf16[64,16,2048]{2,1,0:T(8,128)(2,1)S(1)}, bf16[64,16,2048]{2,1,0:T(8,128)(2,1)}, u32[]{:S(2)}) copy-start(bf16[64,16,2048]{2,1,0:T(8,128)(2,1)} %param.11) | copy-start | bytes 12582916
  68.7 21.5 %collective-permute-start.17 = (bf16[512,2048]{1,0:T(8,128)(2,1)}, bf16[512,2048]{1,0:T(8,128)(2,1)}, u32[]{:S(2)}, u32[]{:S(2)}) collective-permute-start(bf16[512,2048]{1,0:T(8,128)(2,1)} %share.7), channel_id=1, source_target_pairs={{0,1},{1,0},{2,3},{3,2},{4,5},{5,4},{6,7},{7,6},{8,9},{9,8},{10,11... | collective-permute-start | bytes 6291464 | tf_op jit(solution)/shard_map/ppermute | solution.py:400
  68.7 25.4 %collective-permute-start.16 = (bf16[512,2048]{1,0:T(8,128)(2,1)}, bf16[512,2048]{1,0:T(8,128)(2,1)}, u32[]{:S(2)}, u32[]{:S(2)}) collective-permute-start(bf16[512,2048]{1,0:T(8,128)(2,1)} %share.5), channel_id=1, source_target_pairs={{0,1},{1,0},{2,3},{3,2},{4,5},{5,4},{6,7},{7,6},{8,9},{9,8},{10,11... | collective-permute-start | bytes 6291464 | tf_op jit(solution)/shard_map/ppermute | solution.py:400
  69.2 3.7 %collective-permute-start.14 = (f32[60,128]{1,0:T(8,128)S(1)}, f32[60,128]{1,0:T(8,128)S(1)}, u32[]{:S(2)}, u32[]{:S(2)}) collective-permute-start(f32[60,128]{1,0:T(8,128)S(1)} %get-tuple-element.253), channel_id=1, source_target_pairs={{0,1},{1,0},{2,3},{3,2},{4,5},{5,4},{6,7},{7,6},{8,9},{9,8},{10,11... | collective-permute-start | bytes 92168 | tf_op jit(solution)/shard_map/ppermute | solution.py:400
  72.9 5.8 %collective-permute-start.15 = (f32[60,128]{1,0:T(8,128)S(1)}, f32[60,128]{1,0:T(8,128)S(1)}, u32[]{:S(2)}, u32[]{:S(2)}) collective-permute-start(f32[60,128]{1,0:T(8,128)S(1)} %add.155), channel_id=1, source_target_pairs={{0,2},{1,3},{2,0},{3,1},{4,6},{5,7},{6,4},{7,5},{8,10},{9,11},{10,... | collective-permute-start | bytes 92168 | tf_op jit(solution)/shard_map/ppermute | solution.py:400
  74.1 20.0 %collective-permute-start.13 = (bf16[128,2176]{1,0:T(8,128)(2,1)}, bf16[128,2176]{1,0:T(8,128)(2,1)}, u32[]{:S(2)}, u32[]{:S(2)}) collective-permute-start(bf16[128,2176]{1,0:T(8,128)(2,1)} %pad_maximum_fusion), channel_id=1, source_target_pairs={{0,4},{4,0},{8,12},{12,8},{1,5},{5,1},{9,13},{13,9},{2,6},{6,2},{1... | collective-permute-start | bytes 1671176 | tf_op jit(solution)/shard_map/ppermute | solution.py:400
  86.4 32.1 %all-to-all-start = ((bf16[4,72,2048]{2,1,0:T(8,128)(2,1)}), bf16[4,72,2048]{2,1,0:T(8,128)(2,1)S(1)}, u32[]{:S(2)}, u32[]{:S(2)}) async-start(bf16[4,72,2048]{2,1,0:T(8,128)(2,1)} %copy-done.3), calls=%async_computation | async-start | bytes 2359296 | tf_op jit(solution)/shard_map/all_to_all | solution.py:419
  90.2 3.9 %copy-start.22 = (bf16[64,16,2048]{2,1,0:T(8,128)(2,1)S(1)}, bf16[64,16,2048]{2,1,0:T(8,128)(2,1)}, u32[]{:S(2)}) copy-start(bf16[64,16,2048]{2,1,0:T(8,128)(2,1)} %param.11) | copy-start | bytes 12582916
  94.1 11.4 %copy-start.19 = (bf16[64,16,2048]{2,1,0:T(8,128)(2,1)S(1)}, bf16[64,16,2048]{2,1,0:T(8,128)(2,1)}, u32[]{:S(2)}) copy-start(bf16[64,16,2048]{2,1,0:T(8,128)(2,1)} %param.12) | copy-start | bytes 12582916
  99.2 1.2 collective-permute-start.18
  100.4 3.7 %collective-permute-start.19 = (f32[16,128]{1,0:T(8,128)S(1)}, f32[16,128]{1,0:T(8,128)S(1)}, u32[]{:S(2)}, u32[]{:S(2)}) collective-permute-start(f32[16,128]{1,0:T(8,128)S(1)} %add.158), channel_id=1, source_target_pairs={{0,2},{1,3},{2,0},{3,1},{4,6},{5,7},{6,4},{7,5},{8,10},{9,11},{10,... | collective-permute-start | bytes 24584 | tf_op jit(solution)/shard_map/ppermute | solution.py:400
  104.0 50.2 %collective-permute-start.24 = (bf16[512,2048]{1,0:T(8,128)(2,1)}, bf16[512,2048]{1,0:T(8,128)(2,1)}, u32[]{:S(2)}, u32[]{:S(2)}) collective-permute-start(bf16[512,2048]{1,0:T(8,128)(2,1)} %add_convert_fusion.1), channel_id=1, source_target_pairs={{0,2},{1,3},{2,0},{3,1},{4,6},{5,7},{6,4},{7,5},{8,10},{9,11},{10,... | collective-permute-start | bytes 6291464 | tf_op jit(solution)/shard_map/ppermute | solution.py:400
  105.5 48.7 %copy-start.1 = (bf16[512,2048]{1,0:T(8,128)(2,1)S(1)}, bf16[512,2048]{1,0:T(8,128)(2,1)}, u32[]{:S(2)}) copy-start(bf16[512,2048]{1,0:T(8,128)(2,1)} %copy-done) | copy-start | bytes 6291460
  108.4 18.7 %collective-permute-start.20 = (bf16[128,2048]{1,0:T(8,128)(2,1)}, bf16[128,2048]{1,0:T(8,128)(2,1)}, u32[]{:S(2)}, u32[]{:S(2)}) collective-permute-start(bf16[128,2048]{1,0:T(8,128)(2,1)} %deltas.9), channel_id=1, source_target_pairs={{0,4},{4,0},{8,12},{12,8},{1,5},{5,1},{9,13},{13,9},{2,6},{6,2},{1... | collective-permute-start | bytes 1572872 | tf_op jit(solution)/shard_map/ppermute | solution.py:400
  127.1 27.1 %collective-permute-start.23 = (bf16[136,2048]{1,0:T(8,128)(2,1)}, bf16[136,2048]{1,0:T(8,128)(2,1)}, u32[]{:S(2)}, u32[]{:S(2)}) collective-permute-start(bf16[136,2048]{1,0:T(8,128)(2,1)} %copy-done.17), channel_id=1, source_target_pairs={{0,4},{4,0},{8,12},{12,8},{1,5},{5,1},{9,13},{13,9},{2,6},{6,2},{1... | collective-permute-start | bytes 1671176 | tf_op jit(solution)/shard_map/ppermute | solution.py:400
  129.2 17.0 %collective-permute-start.21 = (bf16[64,2048]{1,0:T(8,128)(2,1)}, bf16[64,2048]{1,0:T(8,128)(2,1)}, u32[]{:S(2)}, u32[]{:S(2)}) collective-permute-start(bf16[64,2048]{1,0:T(8,128)(2,1)} %get-tuple-element.319), channel_id=1, source_target_pairs={{0,8},{4,12},{8,0},{12,4},{1,9},{5,13},{9,1},{13,5},{2,10},{6,14},... | collective-permute-start | bytes 786440 | tf_op jit(solution)/shard_map/ppermute | solution.py:400
  133.2 21.1 %collective-permute-start.22 = (bf16[64,2048]{1,0:T(8,128)(2,1)}, bf16[64,2048]{1,0:T(8,128)(2,1)}, u32[]{:S(2)}, u32[]{:S(2)}) collective-permute-start(bf16[64,2048]{1,0:T(8,128)(2,1)} %get-tuple-element.318), channel_id=1, source_target_pairs={{0,12},{4,8},{8,4},{12,0},{1,13},{5,9},{9,5},{13,1},{2,14},{6,10},... | collective-permute-start | bytes 786440 | tf_op jit(solution)/shard_map/ppermute | solution.py:400
  134.3 3.6 %collective-permute-start.25 = (s32[1,1]{1,0:T(1,128)}, s32[1,1]{1,0:T(1,128)}, u32[]{:S(2)}, u32[]{:S(2)}) collective-permute-start(s32[1,1]{1,0:T(1,128)} %get-tuple-element.243.refs_1_), channel_id=1, source_target_pairs={{0,16},{16,0},{1,17},{17,1},{2,18},{18,2},{3,19},{19,3},{4,20},{20... | collective-permute-start | bytes 20 | tf_op jit(solution)/shard_map/ppermute | solution.py:400
  (12 other events, 9.9 us)

commit v3 on v1

--- a/solution.py
+++ b/solution.py
@@ -34,13 +34,16 @@
 def score_kernel(dists, block, *refs):
     me_ref, known_ref, refs = refs[0], refs[1], refs[2:]
     m = len(dists)
-    got, a_ref, refs = refs[:1 if block else m], refs[1 if block else m], refs[(2 if block else m + 1):]
+    count = m - block + (block > 0)
+    got, a_ref, refs = refs[:count], refs[count], refs[count + 1:]
     out_ref, told_ref, slots, acc = refs[0], refs[1], refs[2:-1], refs[-1]
     g = pl.program_id(0)
     per, width = a_ref.shape[0] // 16, a_ref.shape[1]
 
     def view(i, low, high):
-        return got[0][me_ref[0] ^ (i + 1), :, low:high] if block else got[i][:, low:high]
+        if i < block:
+            return got[0][me_ref[0] ^ (i + 1), :, low:high]
+        return got[i - block + (block > 0)][:, low:high]
 
     @pl.when(g == 0)
     def _():
@@ -85,8 +88,8 @@
 
 
 def scores(me, known, dists, got, store):
-    block = got[0].ndim == 3
-    sizes = [got[0].shape[1]] * len(dists) if block else [v.shape[0] for v in got]
+    block = got[0].shape[0] - 1 if got[0].ndim == 3 else 0
+    sizes = [OWN] * block + [v.shape[0] for v in got if v.ndim == 2]
     total, width = sum(sizes), store.shape[1]
     blk = 256
     out = pl.pallas_call(
@@ -105,8 +108,7 @@
     return out[0], out[1], list(out[2:])
 
 
-def spread_out(slots, packed, depth, spread):
-    off = 0
+def spread_out(slots, packed, depth, spread, off):
     for i in range(len(slots)):
         n = slots[i].shape[0]
         v = packed[off // 8:(off + n) // 8, :]
@@ -119,55 +121,44 @@
         off += n
 
 
-def delta_kernel(m, *refs):
+def delta_kernel(m, skip, block, me_ref, *refs):
     slots, packed, b_ref, outs, spread = refs[:m], refs[m], refs[m + 1], refs[m + 2:-m], refs[-m:]
 
     @pl.when(pl.program_id(0) == 0)
     def _():
-        spread_out(slots, packed, b_ref.shape[0], spread)
-
+        spread_out(slots, packed, b_ref.shape[0], spread, skip)
+
+    if block:
+        outs[0][me_ref[0]] = jnp.zeros(outs[0].shape[1:], outs[0].dtype)
     for i in range(m):
-        outs[i][...] = jnp.dot(spread[i][...], b_ref[...], preferred_element_type=jnp.float32).astype(jnp.bfloat16)
-
-
-def direct_kernel(m, me_ref, *refs):
-    slots, packed, b_ref, block, spread = refs[:m], refs[m], refs[m + 1], refs[m + 2], refs[m + 3:]
-    me = me_ref[0]
-
-    @pl.when(pl.program_id(0) == 0)
-    def _():
-        spread_out(slots, packed, b_ref.shape[0], spread)
-
-    block[me] = jnp.zeros(block.shape[1:], block.dtype)
-    for i in range(m):
-        v = jnp.dot(spread[i][...], b_ref[...], preferred_element_type=jnp.float32)
-        block[me ^ (i + 1)] = v.astype(jnp.bfloat16)
-
-
-def deltas(slots, packed, store, me=None):
+        v = jnp.dot(spread[i][...], b_ref[...], preferred_element_type=jnp.float32).astype(jnp.bfloat16)
+        if i < block:
+            outs[0][me_ref[0] ^ (i + 1)] = v
+        else:
+            outs[i - block + (block > 0)][...] = v
+
+
+def deltas(me, slots, packed, store, skip=0, block=0):
     depth, width = store.shape
     cols = width // 4
-    m, sizes = len(slots), [v.shape[0] for v in slots]
+    sizes = [v.shape[0] for v in slots]
     part = lambda n: pl.BlockSpec((n, cols), lambda g: (0, g))
-    ins = [whole(v.shape) for v in slots] + [whole(packed.shape), part(depth)]
-    args = [*slots, packed, store]
-    if me is None:
-        kernel, outs, shapes = delta_kernel, [part(n) for n in sizes], [(n, width) for n in sizes]
-    else:
-        kernel, ins, args = direct_kernel, [pl.BlockSpec(memory_space=pltpu.SMEM)] + ins, [me] + args
-        outs = [pl.BlockSpec((m + 1, OWN, cols), lambda g: (0, 0, g))]
-        shapes = [(m + 1, OWN, width)]
+    outs = [pl.BlockSpec((block + 1, OWN, cols), lambda g: (0, 0, g))] if block else []
+    shapes = [(block + 1, OWN, width)] if block else []
+    outs += [part(n) for n in sizes[block:]]
+    shapes += [(n, width) for n in sizes[block:]]
     return list(pl.pallas_call(
-        functools.partial(kernel, m),
+        functools.partial(delta_kernel, len(slots), skip, block),
         grid=(width // cols,),
-        in_specs=ins,
+        in_specs=[pl.BlockSpec(memory_space=pltpu.SMEM)] + [whole(v.shape) for v in slots]
+        + [whole(packed.shape), part(depth)],
         out_specs=outs,
         out_shape=[jax.ShapeDtypeStruct(v, jnp.bfloat16) for v in shapes],
         scratch_shapes=[pltpu.VMEM((n, depth), jnp.bfloat16) for n in sizes],
         compiler_params=pltpu.CompilerParams(vmem_limit_bytes=VMEM),
         cost_estimate=FREE,
         name="deltas",
-    )(*args))
+    )(me, *slots, packed, store))
 
 
 def finish_kernel(m, n_dp, me_ref, row_ref, *refs):
@@ -430,32 +421,25 @@
     out_shared, out_near, codes = packed[6:6 + m], packed[6 + m], packed[7 + m:]
     codes, block_codes = codes[:m + 1], codes[m + 1:]
 
-    block = a2a(block)
     in_shared = [swap(v, "dp", j) for v, j in zip(out_shared, far)]
     in_near = swap(out_near, "dp", 1)
 
     self_found, _, self_part = answer([None], [after(x, table)], self_slots)
+    block = a2a(after(block, self_part))
 
     at = after(lax.axis_index("tp").reshape(1), self_part)
     cols = weight.shape[1] // n_tp
     early = [k for k in reversed(range(n_tp)) if k >= n_tp // 2]
     shares = {k: share(at ^ k, x, weight, cols) for k in early}
 
-    block, shares = lax.optimization_barrier((block, shares))
-    found, rounds, part = answer(list(range(1, n_dp)), [block], rounds)
-    (block,) = deltas(found, part, expand_store, me)
-    at = after(at, block)
-    block = a2a(block)
-    for k in reversed(range(n_tp)):
-        if k not in early and k:
-            shares[k] = share(at ^ k, x, weight, cols)
-
-    in_shared, shares = lax.optimization_barrier((in_shared, shares))
+    in_shared, in_near, shares = lax.optimization_barrier((in_shared, in_near, shares))
     in_relay = jnp.concatenate(in_shared)
     at = after(at, in_relay)
     in_relay = swap(in_relay, "dp", 1)
-    shares[0] = share(at, x, weight, cols)
-    (self_delta,) = deltas(self_found, after(self_part, in_shared), expand_store)
+    for k in reversed(range(n_tp)):
+        if k not in early:
+            shares[k] = share(at ^ k, x, weight, cols)
+    (self_delta,) = deltas(me, self_found, after(self_part, in_relay), expand_store)
 
     adds = {k: [shares[k]] for k in shares}
     for k in range(1, n_tp, 2):
@@ -463,16 +447,22 @@
     for k in range(2, n_tp, 2):
         adds[k] = [total_of(adds[k])]
 
-    got, self_delta, adds = lax.optimization_barrier((in_shared + [in_near, in_relay], self_delta, adds))
-    found, _, part = answer(list(far) + [1, RELAY], got, rounds)
-    part, adds, block = lax.optimization_barrier((part, adds, block))
-    late = deltas(found, part, expand_store)
-    relayed = swap(late[-1], "dp", 1)
+    got, self_delta, adds = lax.optimization_barrier(
+        ([block] + in_shared + [in_near, in_relay], self_delta, adds)
+    )
+    found, rounds, part = answer(list(range(1, n_dp)) + list(far) + [1, RELAY], got, rounds)
+    part, adds = lax.optimization_barrier((part, adds))
+    skip = sum(v.shape[0] for v in found[:-1])
+    (relayed,) = deltas(me, found[-1:], part, expand_store, skip)
+    late = deltas(me, found[:-1], after(part, relayed), expand_store, 0, n_dp - 1)
+    relayed = swap(relayed, "dp", 1)
+    block = a2a(late[0])
     bit = 2
     while bit < n_tp:
         for k in sorted((k for k in adds if k & bit), reverse=True):
             adds[k ^ bit].append(swap(total_of(adds.pop(k)), "tp", bit))
         bit *= 2
+    relayed, block, late = lax.optimization_barrier((relayed, block, late[1:]))
     back = [swap(late[i] + relayed[i * SHARED:(i + 1) * SHARED], "dp", j) for i, j in enumerate(far)]
     back.append(swap(late[m], "dp", 1))
     adds = adds[0] + [self_delta]
@@ -495,7 +485,7 @@
             got.append(swap(v, "dp", j))
         found, _, part = answer(list(range(1, n_dp)), got, rounds.reshape(1, 1))
         total = out.astype(jnp.float32)
-        for j, c, v in zip(range(1, n_dp), code, deltas(found, part, expand_store)):
+        for j, c, v in zip(range(1, n_dp), code, deltas(me, found, part, expand_store)):
             put = (places == c[None, :]).astype(jnp.bfloat16)
             total = total + jnp.dot(put, swap(v, "dp", j), preferred_element_type=jnp.float32)
         return total.astype(jnp.bfloat16)

time: 211 us -> 208 us (0.986)
  Pallas kernels: 81.8 us -> 77.5 us
    ppermute x18 -> x16, waiting for transfers between devices: 63.3 us -> 75.3 us  [swap(): return lax.ppermute(v, axis, [(i, i ^ k) for i in range(n)])]
    all_to_all x2, waiting for transfers between devices: 10.4 us -> 0.01 us  [a2a(): return lax.all_to_all(v, 'dp', split_axis=0, concat_axis=0, tiled=True)]
    pallas_call x3 -> x2, Pallas kernels: 22.5 us -> 19 us  [scores(): pl.pallas_call(functools.partial(score_kernel, tuple(dists), block), grid...]
    ppermute x18 -> x16, starting transfers between devices: 19.6 us -> 20.7 us  [swap(): return lax.ppermute(v, axis, [(i, i ^ k) for i in range(n)])]
    unnamed x61 -> x67, local copies, waits for them, and re-layouts: 15.9 us -> 16.6 us
  transfers between devices with their start and end apart: 20 -> 18, of which waited for: 13 -> 9; matrix products, arithmetic and copies ran while one was open for 4% -> 3% of each run, Pallas kernels for 33% -> 21%
where the time goes in v3:
time: 208 us; the launch traced here: 207 us
  Pallas kernels  77.5 us (37%)
  waiting for transfers between devices  75.3 us (36%)
  starting transfers between devices  29.6 us (14%)
  local copies, waits for them, and re-layouts  17.3 us (8%)
  other arithmetic  5.79 us (3%)
    ppermute x16, waiting for transfers between devices, swap(): return lax.ppermute(v, axis, [(i, i ^ k) for i in range(n)])  75.3 us
    pallas_call x4, Pallas kernels, share(): pl.pallas_call(share_kernel, grid_spec=pltpu.PrefetchScalarGridSpec(num_s...  32.6 us
    ppermute x16, starting transfers between devices, swap(): return lax.ppermute(v, axis, [(i, i ^ k) for i in range(n)])  20.7 us
    pallas_call x2, Pallas kernels, scores(): pl.pallas_call(functools.partial(score_kernel, tuple(dists), block), grid...  19 us
    unnamed x67, local copies, waits for them, and re-layouts  16.6 us
    pallas_call x3, Pallas kernels, deltas(): pl.pallas_call(functools.partial(delta_kernel, len(slots), skip, block),...  12.9 us
    all_to_all x2, starting transfers between devices, a2a(): return lax.all_to_all(v, 'dp', split_axis=0, concat_axis=0, tiled=True)  8.9 us
    pallas_call x1, Pallas kernels, finish(): pl.pallas_call(functools.partial(finish_kernel, len(codes), n_dp), grid=(...  7.5 us
  transfers between devices with their start and end apart: 18, of which 9 were waited for; matrix products, arithmetic and copies ran while one was open for 3% of the time, Pallas kernels for 21%

profile of v3, /device:TPU:0, one launch (start us, length us, event | category | flops | bytes accessed | tf_op | source)
XLA Modules:
  0.0 206.9 jit_solution(14191731113036961983)
XLA Ops:
  2.0 5.5 %pack.1 = (s32[2,32]{1,0:T(2,128)}, s32[512,1]{1,0:T(8,128)S(1)}, s32[512,1]{1,0:T(8,128)S(1)}, bf16[512,128]{1,0:T(8,128)(2,1)}, s32[1,1]{1,0:T(1,128)}, /*inde...) custom-call(s32[1]{0:T(128)} %bitcast.1.me_ref.refs_0_, ...), custom_call_target="tpu_custom_call" | custom-call | tf_op jit(solution)/shard_map/pack/pallas_call | solution.py:328
  8.6 3.0 %collective-permute-start.12 = (bf16[136,2176]{1,0:T(8,128)(2,1)}, bf16[136,2176]{1,0:T(8,128)(2,1)S(1)}, u32[]{:S(2)}, u32[]{:S(2)}) collective-permute-start(bf16[136,2176]{1,0:T(8,128)(2,1)} %get-tuple-element.240), channel_id=1, source_target_pairs={{0,4},{4,0},{8,12},{12,8},{1,5},{5,1},{9,13},{13,9},{2,6},{6,2},{1... | collective-permute-start | bytes 1775624 | tf_op jit(solution)/shard_map/ppermute | solution.py:392
  11.6 2.6 %collective-permute-start.10 = (bf16[64,2176]{1,0:T(8,128)(2,1)}, bf16[64,2176]{1,0:T(8,128)(2,1)S(1)}, u32[]{:S(2)}, u32[]{:S(2)}) collective-permute-start(bf16[64,2176]{1,0:T(8,128)(2,1)} %get-tuple-element.238), channel_id=1, source_target_pairs={{0,8},{4,12},{8,0},{12,4},{1,9},{5,13},{9,1},{13,5},{2,10},{6,14},... | collective-permute-start | bytes 835592 | tf_op jit(solution)/shard_map/ppermute | solution.py:392
  14.2 5.8 %scores.6 = (f32[64,128]{1,0:T(8,128)S(1)}, s32[1,1]{1,0:T(1,128)}, s32[512,1]{1,0:T(8,128)S(1)}) custom-call(s32[1]{0:T(128)} %bitcast.1.me_ref.refs_0_, s32[512,1]{1,0:T(8,128)S(1)} %get-tuple-element.233.refs_1_, bf16[512,2048]{1,0:T(8,128)(2,1)S(1)} %bitcast.38, bf16[1024,2048]{1,0:T(8,128)(2,1)} %bitcast.41), custom_call_target="tpu_custom_call" | custom-call | tf_op jit(solution)/shard_map/scores/pallas_call | solution.py:95
  21.9 1.7 collective-permute-start.9
  23.7 2.2 %collective-permute-done.9 = f32[64,128]{1,0:T(8,128)S(1)} collective-permute-done((f32[64,128]{1,0:T(8,128)S(1)}, f32[64,128]{1,0:T(8,128)S(1)}, u32[]{:S(2)}, u32[]{:S(2)}) %collective-permute-start.9) | collective-permute-done | bytes 32800 | tf_op jit(solution)/shard_map/ppermute | solution.py:392
  25.9 7.9 %share.4 = bf16[512,2048]{1,0:T(8,128)(2,1)S(1)} custom-call(s32[1]{0:T(128)S(6)} %xor.22.at_ref, bf16[512,2048]{1,0:T(8,128)(2,1)} %bitcast.35, bf16[2048,8192]{1,0:T(8,128)(2,1)} %w_ref.7), custom_call_target="tpu_custom_call" | custom-call | tf_op jit(solution)/shard_map/share/pallas_call | solution.py:346
  33.8 8.1 %share.5 = bf16[512,2048]{1,0:T(8,128)(2,1)} custom-call(s32[1]{0:T(128)S(6)} %xor.23.at_ref, bf16[512,2048]{1,0:T(8,128)(2,1)S(1)} %bitcast.39, bf16[2048,8192]{1,0:T(8,128)(2,1)} %w_ref.7), custom_call_target="tpu_custom_call" | custom-call | tf_op jit(solution)/shard_map/share/pallas_call | solution.py:346
  42.1 8.6 %share.7 = bf16[512,2048]{1,0:T(8,128)(2,1)} custom-call(s32[1]{0:T(128)S(6)} %xor.24.at_ref, bf16[512,2048]{1,0:T(8,128)(2,1)S(1)} %bitcast.40, bf16[2048,8192]{1,0:T(8,128)(2,1)} %w_ref.7), custom_call_target="tpu_custom_call" | custom-call | tf_op jit(solution)/shard_map/share/pallas_call | solution.py:346
  51.1 5.1 %all-to-all-start = ((bf16[4,72,2176]{2,1,0:T(8,128)(2,1)}), bf16[4,72,2176]{2,1,0:T(8,128)(2,1)S(1)}, u32[]{:S(2)}, u32[]{:S(2)}) async-start(bf16[4,72,2176]{2,1,0:T(8,128)(2,1)} %copy-done.3), calls=%async_computation | async-start | bytes 2506752 | tf_op jit(solution)/shard_map/all_to_all | solution.py:411
  56.2 2.0 collective-permute-start.13
  58.2 7.9 %share.6.refs_10_ = bf16[512,2048]{1,0:T(8,128)(2,1)S(1)} custom-call(s32[1]{0:T(128)} %bitcast.5.at_ref, bf16[512,2048]{1,0:T(8,128)(2,1)} %bitcast.36, bf16[2048,8192]{1,0:T(8,128)(2,1)} %w_ref.7), custom_call_target="tpu_custom_call" | custom-call | tf_op jit(solution)/shard_map/share/pallas_call | solution.py:346
  67.5 23.6 %collective-permute-done.13.refs_6_ = bf16[128,2176]{1,0:T(8,128)(2,1)S(1)} collective-permute-done((bf16[128,2176]{1,0:T(8,128)(2,1)}, bf16[128,2176]{1,0:T(8,128)(2,1)S(1)}, u32[]{:S(2)}, u32[]{:S(2)}) %collective-permute-start.13) | collective-permute-done | bytes 557088 | tf_op jit(solution)/shard_map/ppermute | solution.py:392
  91.8 4.1 %deltas.7.refs_13_ = bf16[512,2048]{1,0:T(8,128)(2,1)S(1)} custom-call(s32[1]{0:T(128)} %bitcast.1.me_ref.refs_0_, s32[512,1]{1,0:T(8,128)S(1)} %copy-done.19, f32[64,128]{1,0:T(8,128)S(1)} %add.148.refs_1_, bf16[1024,2048]{1,0:T(8,128)(2,1)S(1)} %bitcast.31), custom_call_target="tpu_custom_call" | custom-call | tf_op jit(solution)/shard_map/deltas/pallas_call | solution.py:150
  97.3 3.7 %add_convert_fusion.1 = bf16[512,2048]{1,0:T(8,128)(2,1)} fusion(bf16[512,2048]{1,0:T(8,128)(2,1)} %collective-permute-done.15, bf16[512,2048]{1,0:T(8,128)(2,1)S(1)} %share.4), kind=kLoop, calls=%fused_computation.32 | loop fusion | flops 4194304 | bytes 6291456 | tf_op jit(solution)/shard_map/convert_element_type | solution.py:408
  105.1 13.2 %scores.7 = (f32[76,128]{1,0:T(8,128)S(1)}, s32[1,1]{1,0:T(1,128)}, s32[72,1]{1,0:T(8,128)S(1)}, s32[72,1]{1,0:T(8,128)S(1)}, s32[72,1]{1,0:T(8,128)S(1)}, /*ind...) custom-call(s32[1]{0:T(128)} %bitcast.1.me_ref.refs_0_, ...), custom_call_target="tpu_custom_call" | custom-call | tf_op jit(solution)/shard_map/scores/pallas_call | solution.py:95
  119.6 1.5 collective-permute-start.17
  121.1 2.5 %collective-permute-done.17 = f32[76,128]{1,0:T(8,128)S(1)} collective-permute-done((f32[76,128]{1,0:T(8,128)S(1)}, f32[76,128]{1,0:T(8,128)S(1)}, u32[]{:S(2)}, u32[]{:S(2)}) %collective-permute-start.17) | collective-permute-done | bytes 38944 | tf_op jit(solution)/shard_map/ppermute | solution.py:392
  123.6 2.0 deltas.8
  126.4 6.7 %deltas.9 = (bf16[4,72,2048]{2,1,0:T(8,128)(2,1)S(1)}, bf16[64,2048]{1,0:T(8,128)(2,1)S(1)}, bf16[64,2048]{1,0:T(8,128)(2,1)S(1)}, bf16[136,2048]{1,0:T(8,128)(2,1)S(1)}) custom-call(s32[1]{0:T(128)} %bitcast.1.me_ref.refs_0_, s32[72,1]{1,0:T(8,128)S(1)} %get-tuple-element.261.refs_0_, s32[72,1]{1,0:T(8,128)S(1)} %get-tuple-element.262.refs_1_, ...), custom_call_target="tpu_custom_call" | custom-call | tf_op jit(solution)/shard_map/deltas/pallas_call | solution.py:150
  136.4 3.8 %all-to-all-start.1 = ((bf16[4,72,2048]{2,1,0:T(8,128)(2,1)}), bf16[4,72,2048]{2,1,0:T(8,128)(2,1)S(1)}, u32[]{:S(2)}, u32[]{:S(2)}) async-start(bf16[4,72,2048]{2,1,0:T(8,128)(2,1)} %copy-done.4), calls=%async_computation.1 | async-start | bytes 2359296 | tf_op jit(solution)/shard_map/all_to_all | solution.py:411
  140.2 1.5 collective-permute-start.22
  141.7 2.0 collective-permute-start.18
  143.7 28.4 %collective-permute-done.18 = bf16[128,2048]{1,0:T(8,128)(2,1)} collective-permute-done((bf16[128,2048]{1,0:T(8,128)(2,1)}, bf16[128,2048]{1,0:T(8,128)(2,1)}, u32[]{:S(2)}, u32[]{:S(2)}) %collective-permute-start.18) | collective-permute-done | bytes 524320 | tf_op jit(solution)/shard_map/ppermute | solution.py:392
  172.5 2.0 slice_add_fusion
  174.5 2.6 %collective-permute-start.19 = (bf16[64,2048]{1,0:T(8,128)(2,1)}, bf16[64,2048]{1,0:T(8,128)(2,1)}, u32[]{:S(2)}, u32[]{:S(2)}) collective-permute-start(bf16[64,2048]{1,0:T(8,128)(2,1)} %get-tuple-element.321), channel_id=1, source_target_pairs={{0,8},{4,12},{8,0},{12,4},{1,9},{5,13},{9,1},{13,5},{2,10},{6,14},... | collective-permute-start | bytes 786440 | tf_op jit(solution)/shard_map/ppermute | solution.py:392
  177.1 1.5 collective-permute-start.20
  179.2 1.5 collective-permute-start.23
  180.7 2.2 %collective-permute-done.23 = s32[1,1]{1,0:T(1,128)} collective-permute-done((s32[1,1]{1,0:T(1,128)}, s32[1,1]{1,0:T(1,128)}, u32[]{:S(2)}, u32[]{:S(2)}) %collective-permute-start.23) | collective-permute-done | bytes 36 | tf_op jit(solution)/shard_map/ppermute | solution.py:392
  184.1 7.4 %collective-permute-done.19.refs_6_ = bf16[64,2048]{1,0:T(8,128)(2,1)} collective-permute-done((bf16[64,2048]{1,0:T(8,128)(2,1)}, bf16[64,2048]{1,0:T(8,128)(2,1)}, u32[]{:S(2)}, u32[]{:S(2)}) %collective-permute-start.19) | collective-permute-done | bytes 262176 | tf_op jit(solution)/shard_map/ppermute | solution.py:392
  191.5 6.7 %collective-permute-done.20.refs_7_ = bf16[64,2048]{1,0:T(8,128)(2,1)} collective-permute-done((bf16[64,2048]{1,0:T(8,128)(2,1)}, bf16[64,2048]{1,0:T(8,128)(2,1)}, u32[]{:S(2)}, u32[]{:S(2)}) %collective-permute-start.20) | collective-permute-done | bytes 262176 | tf_op jit(solution)/shard_map/ppermute | solution.py:392
  199.4 7.5 %finish.1 = bf16[512,2048]{1,0:T(8,128)(2,1)} custom-call(s32[1]{0:T(128)} %bitcast.1.me_ref.refs_0_, s32[512,1]{1,0:T(8,128)S(1)} %copy-done.10, s32[1,64]{1,0:T(1,128)S(1)} %get-tuple-element.225.refs_0_, s32[1,64]{1,0:T(1,128)S(1)} %get-tuple-element.226.refs_1_, s32[1,136]{1,0:T(1,128)S(1)} %get-tuple-element.227.refs_2_, ...), custom_call_target="tpu_custom_call" | custom-call | tf_op jit(solution)/shard_map/finish/pallas_call | solution.py:183
  (91 shorter events, 20.6 us)
Async XLA Ops:
  2.0 12.2 %copy-start.31 = (bf16[4,128,2048]{2,1,0:T(8,128)(2,1)S(1)}, bf16[4,128,2048]{2,1,0:T(8,128)(2,1)}, u32[]{:S(2)}) copy-start(bf16[4,128,2048]{2,1,0:T(8,128)(2,1)} %param.9) | copy-start | bytes 6291460
  8.6 11.4 %copy-start.9 = (s32[512,1]{1,0:T(8,128)}, s32[512,1]{1,0:T(8,128)S(1)}, u32[]{:S(2)}) copy-start(s32[512,1]{1,0:T(8,128)S(1)} %get-tuple-element.290.row_ref) | copy-start | bytes 6148
  8.6 11.4 %copy-start.23 = (s32[1,72]{1,0:T(1,128)}, s32[1,72]{1,0:T(1,128)S(1)}, u32[]{:S(2)}) copy-start(s32[1,72]{1,0:T(1,128)S(1)} %get-tuple-element.229.refs_4_) | copy-start | bytes 868
  8.6 11.4 %copy-start.25 = (s32[1,72]{1,0:T(1,128)}, s32[1,72]{1,0:T(1,128)S(1)}, u32[]{:S(2)}) copy-start(s32[1,72]{1,0:T(1,128)S(1)} %get-tuple-element.230.refs_5_) | copy-start | bytes 868
  8.6 33.4 %collective-permute-start.12 = (bf16[136,2176]{1,0:T(8,128)(2,1)}, bf16[136,2176]{1,0:T(8,128)(2,1)S(1)}, u32[]{:S(2)}, u32[]{:S(2)}) collective-permute-start(bf16[136,2176]{1,0:T(8,128)(2,1)} %get-tuple-element.240), channel_id=1, source_target_pairs={{0,4},{4,0},{8,12},{12,8},{1,5},{5,1},{9,13},{13,9},{2,6},{6,2},{1... | collective-permute-start | bytes 1775624 | tf_op jit(solution)/shard_map/ppermute | solution.py:392
  11.6 30.3 %collective-permute-start.10 = (bf16[64,2176]{1,0:T(8,128)(2,1)}, bf16[64,2176]{1,0:T(8,128)(2,1)S(1)}, u32[]{:S(2)}, u32[]{:S(2)}) collective-permute-start(bf16[64,2176]{1,0:T(8,128)(2,1)} %get-tuple-element.238), channel_id=1, source_target_pairs={{0,8},{4,12},{8,0},{12,4},{1,9},{5,13},{9,1},{13,5},{2,10},{6,14},... | collective-permute-start | bytes 835592 | tf_op jit(solution)/shard_map/ppermute | solution.py:392
  14.2 27.7 %collective-permute-start.11 = (bf16[64,2176]{1,0:T(8,128)(2,1)}, bf16[64,2176]{1,0:T(8,128)(2,1)S(1)}, u32[]{:S(2)}, u32[]{:S(2)}) collective-permute-start(bf16[64,2176]{1,0:T(8,128)(2,1)} %get-tuple-element.239), channel_id=1, source_target_pairs={{0,12},{4,8},{8,4},{12,0},{1,13},{5,9},{9,5},{13,1},{2,14},{6,10},... | collective-permute-start | bytes 835592 | tf_op jit(solution)/shard_map/ppermute | solution.py:392
  20.7 1.2 collective-permute-start.8
  21.9 3.9 %collective-permute-start.9 = (f32[64,128]{1,0:T(8,128)S(1)}, f32[64,128]{1,0:T(8,128)S(1)}, u32[]{:S(2)}, u32[]{:S(2)}) collective-permute-start(f32[64,128]{1,0:T(8,128)S(1)} %add.147), channel_id=1, source_target_pairs={{0,2},{1,3},{2,0},{3,1},{4,6},{5,7},{6,4},{7,5},{8,10},{9,11},{10,... | collective-permute-start | bytes 98312 | tf_op jit(solution)/shard_map/ppermute | solution.py:392
  25.8 7.9 %copy-start.32 = (bf16[4,128,2048]{2,1,0:T(8,128)(2,1)S(1)}, bf16[4,128,2048]{2,1,0:T(8,128)(2,1)}, u32[]{:S(2)}) copy-start(bf16[4,128,2048]{2,1,0:T(8,128)(2,1)} %param.9) | copy-start | bytes 6291460
  41.9 8.8 %copy-start.5 = (bf16[64,2176]{1,0:T(8,128)(2,1)}, bf16[64,2176]{1,0:T(8,128)(2,1)S(1)}, u32[]{:S(2)}) copy-start(bf16[64,2176]{1,0:T(8,128)(2,1)S(1)} %collective-permute-done.10.refs_3_) | copy-start | bytes 835588
  41.9 8.8 %copy-start.7 = (bf16[64,2176]{1,0:T(8,128)(2,1)}, bf16[64,2176]{1,0:T(8,128)(2,1)S(1)}, u32[]{:S(2)}) copy-start(bf16[64,2176]{1,0:T(8,128)(2,1)S(1)} %collective-permute-done.11.refs_4_) | copy-start | bytes 835588
  42.0 8.8 %copy-start.11 = (bf16[136,2176]{1,0:T(8,128)(2,1)}, bf16[136,2176]{1,0:T(8,128)(2,1)S(1)}, u32[]{:S(2)}) copy-start(bf16[136,2176]{1,0:T(8,128)(2,1)S(1)} %collective-permute-done.12.refs_5_) | copy-start | bytes 1775620
  42.0 55.4 %collective-permute-start.15 = (bf16[512,2048]{1,0:T(8,128)(2,1)}, bf16[512,2048]{1,0:T(8,128)(2,1)}, u32[]{:S(2)}, u32[]{:S(2)}) collective-permute-start(bf16[512,2048]{1,0:T(8,128)(2,1)} %share.5), channel_id=1, source_target_pairs={{0,1},{1,0},{2,3},{3,2},{4,5},{5,4},{6,7},{7,6},{8,9},{9,8},{10,11... | collective-permute-start | bytes 6291464 | tf_op jit(solution)/shard_map/ppermute | solution.py:392
  42.1 8.6 %copy-start.37 = (bf16[128,2176]{1,0:T(8,128)(2,1)}, bf16[128,2176]{1,0:T(8,128)(2,1)S(1)}, u32[]{:S(2)}) copy-start(bf16[128,2176]{1,0:T(8,128)(2,1)S(1)} %constant_dynamic-update-slice_fusion.2) | copy-start | bytes 1671172
  50.8 50.3 %collective-permute-start.14 = (bf16[512,2048]{1,0:T(8,128)(2,1)}, bf16[512,2048]{1,0:T(8,128)(2,1)}, u32[]{:S(2)}, u32[]{:S(2)}) collective-permute-start(bf16[512,2048]{1,0:T(8,128)(2,1)} %share.7), channel_id=1, source_target_pairs={{0,1},{1,0},{2,3},{3,2},{4,5},{5,4},{6,7},{7,6},{8,9},{9,8},{10,11... | collective-permute-start | bytes 6291464 | tf_op jit(solution)/shard_map/ppermute | solution.py:392
  51.1 50.0 %all-to-all-start = ((bf16[4,72,2176]{2,1,0:T(8,128)(2,1)}), bf16[4,72,2176]{2,1,0:T(8,128)(2,1)S(1)}, u32[]{:S(2)}, u32[]{:S(2)}) async-start(bf16[4,72,2176]{2,1,0:T(8,128)(2,1)} %copy-done.3), calls=%async_computation | async-start | bytes 2506752 | tf_op jit(solution)/shard_map/all_to_all | solution.py:411
  56.2 35.6 %copy-start.19 = (s32[512,1]{1,0:T(8,128)S(1)}, s32[512,1]{1,0:T(8,128)}, u32[]{:S(2)}) copy-start(s32[512,1]{1,0:T(8,128)} %copy-done.18) | copy-start | bytes 6148
  56.2 34.8 %collective-permute-start.13 = (bf16[128,2176]{1,0:T(8,128)(2,1)}, bf16[128,2176]{1,0:T(8,128)(2,1)S(1)}, u32[]{:S(2)}, u32[]{:S(2)}) collective-permute-start(bf16[128,2176]{1,0:T(8,128)(2,1)} %copy-done.37), channel_id=1, source_target_pairs={{0,4},{4,0},{8,12},{12,8},{1,5},{5,1},{9,13},{13,9},{2,6},{6,2},{1... | collective-permute-start | bytes 1671176 | tf_op jit(solution)/shard_map/ppermute | solution.py:392
  58.2 33.6 %copy-start.28 = (bf16[64,16,2048]{2,1,0:T(8,128)(2,1)S(1)}, bf16[64,16,2048]{2,1,0:T(8,128)(2,1)}, u32[]{:S(2)}) copy-start(bf16[64,16,2048]{2,1,0:T(8,128)(2,1)} %param.12) | copy-start | bytes 12582916
  105.1 18.5 %copy-start.29 = (bf16[64,16,2048]{2,1,0:T(8,128)(2,1)S(1)}, bf16[64,16,2048]{2,1,0:T(8,128)(2,1)}, u32[]{:S(2)}) copy-start(bf16[64,16,2048]{2,1,0:T(8,128)(2,1)} %param.12) | copy-start | bytes 12582916
  118.3 1.2 collective-permute-start.16
  119.6 4.0 %collective-permute-start.17 = (f32[76,128]{1,0:T(8,128)S(1)}, f32[76,128]{1,0:T(8,128)S(1)}, u32[]{:S(2)}, u32[]{:S(2)}) collective-permute-start(f32[76,128]{1,0:T(8,128)S(1)} %add.150), channel_id=1, source_target_pairs={{0,2},{1,3},{2,0},{3,1},{4,6},{5,7},{6,4},{7,5},{8,10},{9,11},{10,... | collective-permute-start | bytes 116744 | tf_op jit(solution)/shard_map/ppermute | solution.py:392
  136.4 42.2 %copy-start.10 = (s32[512,1]{1,0:T(8,128)S(1)}, s32[512,1]{1,0:T(8,128)}, u32[]{:S(2)}) copy-start(s32[512,1]{1,0:T(8,128)} %copy-done.9) | copy-start | bytes 6148
  136.4 61.8 %copy-start.1 = (bf16[512,2048]{1,0:T(8,128)(2,1)S(1)}, bf16[512,2048]{1,0:T(8,128)(2,1)}, u32[]{:S(2)}) copy-start(bf16[512,2048]{1,0:T(8,128)(2,1)} %copy-done) | copy-start | bytes 6291460
  136.4 35.7 %all-to-all-start.1 = ((bf16[4,72,2048]{2,1,0:T(8,128)(2,1)}), bf16[4,72,2048]{2,1,0:T(8,128)(2,1)S(1)}, u32[]{:S(2)}, u32[]{:S(2)}) async-start(bf16[4,72,2048]{2,1,0:T(8,128)(2,1)} %copy-done.4), calls=%async_computation.1 | async-start | bytes 2359296 | tf_op jit(solution)/shard_map/all_to_all | solution.py:411
  140.2 58.0 %collective-permute-start.22 = (bf16[512,2048]{1,0:T(8,128)(2,1)}, bf16[512,2048]{1,0:T(8,128)(2,1)}, u32[]{:S(2)}, u32[]{:S(2)}) collective-permute-start(bf16[512,2048]{1,0:T(8,128)(2,1)} %add_convert_fusion.1), channel_id=1, source_target_pairs={{0,2},{1,3},{2,0},{3,1},{4,6},{5,7},{6,4},{7,5},{8,10},{9,11},{10,... | collective-permute-start | bytes 6291464 | tf_op jit(solution)/shard_map/ppermute | solution.py:392
  141.7 30.4 %collective-permute-start.18 = (bf16[128,2048]{1,0:T(8,128)(2,1)}, bf16[128,2048]{1,0:T(8,128)(2,1)}, u32[]{:S(2)}, u32[]{:S(2)}) collective-permute-start(bf16[128,2048]{1,0:T(8,128)(2,1)} %copy-done.15), channel_id=1, source_target_pairs={{0,4},{4,0},{8,12},{12,8},{1,5},{5,1},{9,13},{13,9},{2,6},{6,2},{1... | collective-permute-start | bytes 1572872 | tf_op jit(solution)/shard_map/ppermute | solution.py:392
  172.1 26.0 %collective-permute-start.21 = (bf16[136,2048]{1,0:T(8,128)(2,1)}, bf16[136,2048]{1,0:T(8,128)(2,1)}, u32[]{:S(2)}, u32[]{:S(2)}) collective-permute-start(bf16[136,2048]{1,0:T(8,128)(2,1)} %copy-done.27), channel_id=1, source_target_pairs={{0,4},{4,0},{8,12},{12,8},{1,5},{5,1},{9,13},{13,9},{2,6},{6,2},{1... | collective-permute-start | bytes 1671176 | tf_op jit(solution)/shard_map/ppermute | solution.py:392
  174.5 17.0 %collective-permute-start.19 = (bf16[64,2048]{1,0:T(8,128)(2,1)}, bf16[64,2048]{1,0:T(8,128)(2,1)}, u32[]{:S(2)}, u32[]{:S(2)}) collective-permute-start(bf16[64,2048]{1,0:T(8,128)(2,1)} %get-tuple-element.321), channel_id=1, source_target_pairs={{0,8},{4,12},{8,0},{12,4},{1,9},{5,13},{9,1},{13,5},{2,10},{6,14},... | collective-permute-start | bytes 786440 | tf_op jit(solution)/shard_map/ppermute | solution.py:392
  177.1 21.1 %collective-permute-start.20 = (bf16[64,2048]{1,0:T(8,128)(2,1)}, bf16[64,2048]{1,0:T(8,128)(2,1)}, u32[]{:S(2)}, u32[]{:S(2)}) collective-permute-start(bf16[64,2048]{1,0:T(8,128)(2,1)} %get-tuple-element.320), channel_id=1, source_target_pairs={{0,12},{4,8},{8,4},{12,0},{1,13},{5,9},{9,5},{13,1},{2,14},{6,10},... | collective-permute-start | bytes 786440 | tf_op jit(solution)/shard_map/ppermute | solution.py:392
  179.2 3.7 %collective-permute-start.23 = (s32[1,1]{1,0:T(1,128)}, s32[1,1]{1,0:T(1,128)}, u32[]{:S(2)}, u32[]{:S(2)}) collective-permute-start(s32[1,1]{1,0:T(1,128)} %get-tuple-element.281), channel_id=1, source_target_pairs={{0,16},{16,0},{1,17},{17,1},{2,18},{18,2},{3,19},{19,3},{4,20},{20... | collective-permute-start | bytes 20 | tf_op jit(solution)/shard_map/ppermute | solution.py:392
  (19 other events, 16.6 us)

commit v4 on v2

--- a/solution.py
+++ b/solution.py
@@ -57,11 +57,10 @@
             told_ref[...] = jnp.maximum(told_ref[...], meta[0:1, 2:3])
 
     off = 0
+    turned = a_ref[...].T
     for i in range(m):
         n = slots[i].shape[0]
-        s = lax.dot_general(
-            view(i, 0, width), a_ref[...], (((1,), (1,)), ((), ())), preferred_element_type=jnp.float32
-        )
+        s = jnp.dot(view(i, 0, width), turned, preferred_element_type=jnp.float32)
         s = jnp.where(group_of(s.shape) + g * per == slots[i][...], s, 0.0)
         v = s[:, :128]
         for c in range(128, s.shape[1], 128):
@@ -170,7 +169,7 @@
         grid=(width // cols,),
         in_specs=first + ins,
         out_specs=outs,
-        out_shape=[jax.ShapeDtypeStruct(v, jnp.bfloat16) for v in shapes],
+        out_shape=[pltpu.HBM(v, jnp.bfloat16) for v in shapes],
         scratch_shapes=[pltpu.VMEM((v.shape[0], depth), jnp.bfloat16) for v in slots],
         compiler_params=pltpu.CompilerParams(vmem_limit_bytes=VMEM),
         cost_estimate=FREE,
@@ -178,36 +177,38 @@
     )(*args, *slots, packed, store))
 
 
-def finish_kernel(m, n_dp, me_ref, row_ref, *refs):
-    codes, block_codes = refs[:m], refs[m:m + n_dp - 1]
-    back, block, adds, out_ref = refs[m + n_dp - 1:2 * m + n_dp - 1], refs[2 * m + n_dp - 1], refs[2 * m + n_dp:-1], refs[-1]
-    total = adds[0][...].astype(jnp.float32)
-    for v in adds[1:]:
+def place_kernel(first, m, blocks, me_ref, row_ref, codes_ref, *refs):
+    back, refs = refs[:m], refs[m:]
+    pieces = [b[...] for b in back]
+    if blocks:
+        pieces += [refs[0][me_ref[0] ^ (1 + i)] for i in range(blocks)]
+        refs = refs[1:]
+    total = refs[0][...].astype(jnp.float32)
+    for v in refs[1:-1]:
         total += v[...].astype(jnp.float32)
-    codes = [c[...] for c in codes + block_codes]
-    back = [b[...] for b in back] + [block[me_ref[0] ^ (1 + i)] for i in range(n_dp - 1)]
-    for code, b in zip(codes, back):
+    for i, b in enumerate(pieces):
+        code = codes_ref[first + i:first + i + 1, :b.shape[0]]
         put = jnp.where(row_ref[...] == code, 1.0, 0.0).astype(jnp.bfloat16)
         total += jnp.dot(put, b, preferred_element_type=jnp.float32)
-    out_ref[...] = total.astype(out_ref.dtype)
-
-
-def finish(me, row_code, codes, block_codes, back, block, adds):
+    refs[-1][...] = total.astype(refs[-1].dtype)
+
+
+def place(me, row_code, codes, first, back, block, adds, kind):
     rows, width = adds[0].shape
     cols = width // 4
-    n_dp = block.shape[0]
     part = lambda v: pl.BlockSpec((v.shape[0], cols), lambda g: (0, g))
+    blocks = [pl.BlockSpec((v.shape[0], OWN, cols), lambda g: (0, 0, g)) for v in block]
     return pl.pallas_call(
-        functools.partial(finish_kernel, len(codes), n_dp),
+        functools.partial(place_kernel, first, len(back), sum(v.shape[0] - 1 for v in block)),
         grid=(width // cols,),
-        in_specs=[pl.BlockSpec(memory_space=pltpu.SMEM), whole(row_code.shape)]
-        + [whole(v.shape) for v in codes + block_codes] + [part(v) for v in back]
-        + [pl.BlockSpec((n_dp, OWN, cols), lambda g: (0, 0, g))] + [part(v) for v in adds],
+        in_specs=[pl.BlockSpec(memory_space=pltpu.SMEM), whole(row_code.shape), whole(codes.shape)]
+        + [part(v) for v in back] + blocks + [part(v) for v in adds],
         out_specs=pl.BlockSpec((rows, cols), lambda g: (0, g)),
-        out_shape=jax.ShapeDtypeStruct((rows, width), jnp.bfloat16),
+        out_shape=jax.ShapeDtypeStruct((rows, width), kind),
         compiler_params=pltpu.CompilerParams(vmem_limit_bytes=VMEM),
-        name="finish",
-    )(me, row_code, *codes, *block_codes, *back, block, *adds)
+        cost_estimate=FREE,
+        name="place",
+    )(me, row_code, codes, *back, *block, *adds)
 
 
 def column(row):
@@ -318,8 +319,8 @@
     lanes = [shared_code(big, j, over_of(dist, lives, j), 1) for j in far]
     lanes += [big + OWN + iota_of(NEAR - OWN, 1)]
     lanes += [own_code(big, j, 1) for j in range(1, n_dp)]
-    for c, out in zip(lanes, outs[m:]):
-        out[...] = c
+    for i, c in enumerate(lanes):
+        outs[m][i:i + 1, :c.shape[1]] = c
 
 
 def vmem(count):
@@ -329,10 +330,9 @@
 def packs(me, ids, lives, index, x, n_dp, seg_len, shift):
     count, (rows, width) = ids.shape[1], x.shape
     sizes = [SHARED + OWN] * (n_dp - 2) + [NEAR]
-    parts = [SHARED] * (n_dp - 2) + [NEAR - OWN] + [OWN] * (n_dp - 1)
     shapes = [((2, count), jnp.int32), ((rows, 1), jnp.int32), ((rows, 1), jnp.int32)]
     shapes += [((rows, META), jnp.bfloat16), ((1, 1), jnp.int32)]
-    shapes += [((n, width + META), jnp.bfloat16) for n in sizes] + [((1, n), jnp.int32) for n in parts]
+    shapes += [((n, width + META), jnp.bfloat16) for n in sizes] + [((2 * n_dp - 2, 256), jnp.int32)]
     return pl.pallas_call(
         functools.partial(pack_kernel, n_dp, seg_len, shift),
         in_specs=[pl.BlockSpec(memory_space=pltpu.SMEM)] + vmem(4),
@@ -362,7 +362,7 @@
             ],
             out_specs=pl.BlockSpec((rows, tile), lambda g, at: (0, g)),
         ),
-        out_shape=jax.ShapeDtypeStruct((rows, cols), jnp.bfloat16),
+        out_shape=pltpu.HBM((rows, cols), jnp.bfloat16),
         compiler_params=pltpu.CompilerParams(vmem_limit_bytes=VMEM),
         cost_estimate=FREE,
         name="share",
@@ -400,10 +400,10 @@
         return lax.ppermute(v, axis, [(i, i ^ k) for i in range(n)])
 
     def butterfly(v, axis, op):
-        k = 1
-        while k < lax.axis_size(axis):
+        k = lax.axis_size(axis) // 2
+        while k:
             v = op(v, swap(v, axis, k))
-            k *= 2
+            k //= 2
         return v
 
     def answer(dists, got, known):
@@ -431,7 +431,7 @@
     table, row_code, self_slots, meta, rounds = packed[:5]
     m = len(far)
     out_far, out_near = packed[5:5 + m], packed[5 + m]
-    codes, block_codes = packed[6 + m:7 + 2 * m], packed[7 + 2 * m:]
+    codes = packed[6 + m]
 
     in_far = [swap(v, "dp", j) for v, j in zip(out_far, far)]
     in_near = swap(out_near, "dp", 1)
@@ -461,15 +461,16 @@
     part, adds = lax.optimization_barrier((part, adds))
     (relayed,) = deltas(found, part, expand_store)
     relayed = swap(relayed, "dp", 1)
+    some, adds[0] = adds[0], []
     bit = 2
     while bit < n_tp:
         for k in sorted((k for k in adds if k & bit), reverse=True):
             adds[k ^ bit].append(swap(total_of(adds.pop(k)), "tp", bit))
         bit *= 2
-    relayed, block, near, direct = lax.optimization_barrier((relayed, block, direct[m], direct))
+    some = place(me, row_code, codes, m + 1, [], [block], some + [self_delta], jnp.float32)
+    relayed, some, near, direct = lax.optimization_barrier((relayed, some, direct[m], direct))
     back = [swap(direct[i] + relayed[i * SHARED:(i + 1) * SHARED], "dp", j) for i, j in enumerate(far)]
     back.append(swap(near, "dp", 1))
-    adds = adds[0] + [self_delta]
     rounds = butterfly(rounds, "rep", jnp.maximum)[0, 0]
 
     def late_round(i, out):
@@ -494,7 +495,7 @@
             total = total + jnp.dot(put, swap(v, "dp", j), preferred_element_type=jnp.float32)
         return total.astype(jnp.bfloat16)
 
-    out = finish(me, row_code, codes, block_codes, back, block, adds)
+    out = place(me, row_code, codes, 0, back, [], [some] + adds[0], jnp.bfloat16)
     out = lax.fori_loop(0, rounds, late_round, out)
     return out.reshape(steps, rows_dev, width)
 

time: 165 us -> 156 us (0.945)
  waiting for transfers between devices: 42 us -> 33.6 us
  Pallas kernels: 72.7 us -> 80.3 us
  local copies, waits for them, and re-layouts: 12.2 us -> 4.95 us
    ppermute x18, waiting for transfers between devices: 33.9 us -> 26.1 us  [swap(): return lax.ppermute(v, axis, [(i, i ^ k) for i in range(n)])]
    unnamed x50 -> x28, local copies, waits for them, and re-layouts: 9.93 us -> 2.32 us
    pallas_call x1 -> x2, Pallas kernels: 7.5 us -> 11.5 us  [place(): pl.pallas_call(functools.partial(place_kernel, first, len(back), sum((v.s...]
    pallas_call x4, Pallas kernels: 30.8 us -> 33.5 us  [share(): pl.pallas_call(share_kernel, grid_spec=pltpu.PrefetchScalarGridSpec(num_s...]
  transfers between devices with their start and end apart: 19 -> 19, of which waited for: 9 -> 10; matrix products, arithmetic and copies ran while one was open for 5% -> 5% of each run, Pallas kernels for 32% -> 41%
where the time goes in v4:
time: 156 us; the launch traced here: 155 us
  Pallas kernels  80.3 us (51%)
  waiting for transfers between devices  33.6 us (22%)
  starting transfers between devices  28.3 us (18%)
  other arithmetic  6.64 us (4%)
  local copies, waits for them, and re-layouts  4.95 us (3%)
    pallas_call x4, Pallas kernels, share(): pl.pallas_call(share_kernel, grid_spec=pltpu.PrefetchScalarGridSpec(num_s...  33.5 us
    ppermute x18, waiting for transfers between devices, swap(): return lax.ppermute(v, axis, [(i, i ^ k) for i in range(n)])  26.1 us
    ppermute x18, starting transfers between devices, swap(): return lax.ppermute(v, axis, [(i, i ^ k) for i in range(n)])  24.4 us
    pallas_call x3, Pallas kernels, scores(): pl.pallas_call(functools.partial(score_kernel, tuple(dists), block), grid...  17.9 us
    pallas_call x3, Pallas kernels, deltas(): pl.pallas_call(kernel, grid=(width // cols,), in_specs=first + ins, out_s...  12.8 us
    pallas_call x2, Pallas kernels, place(): pl.pallas_call(functools.partial(place_kernel, first, len(back), sum((v.s...  11.5 us
    all_to_all x1, waiting for transfers between devices, a2a(): return lax.all_to_all(v, 'dp', split_axis=0, concat_axis=0, tiled=True)  7.47 us
    convert_element_type x1, other arithmetic, total_of(): functools.reduce(jnp.add, [v.astype(jnp.float32) for v in parts])  4.68 us
  transfers between devices with their start and end apart: 19, of which 10 were waited for; matrix products, arithmetic and copies ran while one was open for 5% of the time, Pallas kernels for 41%

profile of v4, /device:TPU:0, one launch (start us, length us, event | category | flops | bytes accessed | tf_op | source)
XLA Modules:
  0.0 155.2 jit_solution(17135773594375758330)
XLA Ops:
  2.2 4.5 %pack.1 = (s32[2,32]{1,0:T(2,128)S(1)}, s32[512,1]{1,0:T(8,128)S(1)}, s32[512,1]{1,0:T(8,128)S(1)}, bf16[512,128]{1,0:T(8,128)(2,1)}, s32[1,1]{1,0:T(1,128)}, /*...) custom-call(s32[1]{0:T(128)} %bitcast.1.me_ref.refs_0_, ...), custom_call_target="tpu_custom_call" | custom-call | tf_op jit(solution)/shard_map/pack/pallas_call | solution.py:336
  6.7 3.0 %collective-permute-start.10 = (bf16[208,2176]{1,0:T(8,128)(2,1)}, bf16[208,2176]{1,0:T(8,128)(2,1)S(1)}, u32[]{:S(2)}, u32[]{:S(2)}) collective-permute-start(bf16[208,2176]{1,0:T(8,128)(2,1)} %get-tuple-element.223), channel_id=1, source_target_pairs={{0,4},{4,0},{8,12},{12,8},{1,5},{5,1},{9,13},{13,9},{2,6},{6,2},{1... | collective-permute-start | bytes 2715656 | tf_op jit(solution)/shard_map/ppermute | solution.py:400
  9.8 2.6 %collective-permute-start.8 = (bf16[136,2176]{1,0:T(8,128)(2,1)}, bf16[136,2176]{1,0:T(8,128)(2,1)S(1)}, u32[]{:S(2)}, u32[]{:S(2)}) collective-permute-start(bf16[136,2176]{1,0:T(8,128)(2,1)} %get-tuple-element.221), channel_id=1, source_target_pairs={{0,8},{4,12},{8,0},{12,4},{1,9},{5,13},{9,1},{13,5},{2,10},{6,14},... | collective-permute-start | bytes 1775624 | tf_op jit(solution)/shard_map/ppermute | solution.py:400
  12.4 5.7 %scores.7 = (f32[64,128]{1,0:T(8,128)S(1)}, s32[1,1]{1,0:T(1,128)}, s32[512,1]{1,0:T(8,128)S(1)}) custom-call(s32[1]{0:T(128)} %bitcast.1.me_ref.refs_0_, s32[512,1]{1,0:T(8,128)S(1)} %get-tuple-element.226.refs_1_, bf16[512,2048]{1,0:T(8,128)(2,1)S(1)} %bitcast.41, bf16[1024,2048]{1,0:T(8,128)(2,1)} %bitcast.34), custom_call_target="tpu_custom_call" | custom-call | tf_op jit(solution)/shard_map/scores/pallas_call | solution.py:91
  18.0 1.7 %collective-permute-start.11 = (f32[64,128]{1,0:T(8,128)S(1)}, f32[64,128]{1,0:T(8,128)S(1)}, u32[]{:S(2)}, u32[]{:S(2)}) collective-permute-start(f32[64,128]{1,0:T(8,128)S(1)} %get-tuple-element.229), channel_id=1, source_target_pairs={{0,2},{1,3},{2,0},{3,1},{4,6},{5,7},{6,4},{7,5},{8,10},{9,11},{10,... | collective-permute-start | bytes 98312 | tf_op jit(solution)/shard_map/ppermute | solution.py:400
  19.8 2.2 %collective-permute-done.11 = f32[64,128]{1,0:T(8,128)S(1)} collective-permute-done((f32[64,128]{1,0:T(8,128)S(1)}, f32[64,128]{1,0:T(8,128)S(1)}, u32[]{:S(2)}, u32[]{:S(2)}) %collective-permute-start.11) | collective-permute-done | bytes 32800 | tf_op jit(solution)/shard_map/ppermute | solution.py:400
  22.0 8.9 %share.4.refs_1_ = bf16[512,2048]{1,0:T(8,128)(2,1)} custom-call(s32[1]{0:T(128)} %bitcast.4.at_ref, bf16[512,2048]{1,0:T(8,128)(2,1)} %bitcast.39, bf16[2048,8192]{1,0:T(8,128)(2,1)} %w_ref.7), custom_call_target="tpu_custom_call" | custom-call | tf_op jit(solution)/shard_map/share/pallas_call | solution.py:354
  30.9 8.1 %share.5 = bf16[512,2048]{1,0:T(8,128)(2,1)} custom-call(s32[1]{0:T(128)S(6)} %xor.22.at_ref, bf16[512,2048]{1,0:T(8,128)(2,1)S(1)} %bitcast.42, bf16[2048,8192]{1,0:T(8,128)(2,1)} %w_ref.7), custom_call_target="tpu_custom_call" | custom-call | tf_op jit(solution)/shard_map/share/pallas_call | solution.py:354
  39.0 8.2 %share.6 = bf16[512,2048]{1,0:T(8,128)(2,1)} custom-call(s32[1]{0:T(128)S(6)} %xor.23.at_ref, bf16[512,2048]{1,0:T(8,128)(2,1)S(1)} %bitcast.43, bf16[2048,8192]{1,0:T(8,128)(2,1)} %w_ref.7), custom_call_target="tpu_custom_call" | custom-call | tf_op jit(solution)/shard_map/share/pallas_call | solution.py:354
  47.2 8.3 %share.7 = bf16[512,2048]{1,0:T(8,128)(2,1)} custom-call(s32[1]{0:T(128)S(6)} %xor.24.at_ref, bf16[512,2048]{1,0:T(8,128)(2,1)S(1)} %bitcast.44, bf16[2048,8192]{1,0:T(8,128)(2,1)} %w_ref.7), custom_call_target="tpu_custom_call" | custom-call | tf_op jit(solution)/shard_map/share/pallas_call | solution.py:354
  55.5 4.9 %deltas.7.refs_3_ = bf16[512,2048]{1,0:T(8,128)(2,1)} custom-call(s32[512,1]{1,0:T(8,128)S(1)} %get-tuple-element.228.refs_0_, f32[64,128]{1,0:T(8,128)S(1)} %add.154.refs_1_, bf16[1024,2048]{1,0:T(8,128)(2,1)S(1)} %bitcast.31), custom_call_target="tpu_custom_call" | custom-call | tf_op jit(solution)/shard_map/deltas/pallas_call | solution.py:167
  60.5 6.6 %scores.8 = (f32[60,128]{1,0:T(8,128)S(1)}, s32[1,1]{1,0:T(1,128)}, s32[136,1]{1,0:T(8,128)S(1)}, s32[136,1]{1,0:T(8,128)S(1)}, s32[208,1]{1,0:T(8,128)S(1)}) custom-call(s32[1]{0:T(128)} %bitcast.1.me_ref.refs_0_, s32[1,1]{1,0:T(1,128)} %get-tuple-element.220.refs_1_, bf16[136,2176]{1,0:T(8,128)(2,1)S(1)} %collective-permute-done.8.refs_2_, ...), custom_call_target="tpu_custom_call" | custom-call | tf_op jit(solution)/shard_map/scores/pallas_call | solution.py:91
  67.6 1.7 %collective-permute-start.14 = (f32[60,128]{1,0:T(8,128)S(1)}, f32[60,128]{1,0:T(8,128)S(1)}, u32[]{:S(2)}, u32[]{:S(2)}) collective-permute-start(f32[60,128]{1,0:T(8,128)S(1)} %get-tuple-element.243), channel_id=1, source_target_pairs={{0,2},{1,3},{2,0},{3,1},{4,6},{5,7},{6,4},{7,5},{8,10},{9,11},{10,... | collective-permute-start | bytes 92168 | tf_op jit(solution)/shard_map/ppermute | solution.py:400
  72.4 3.8 %collective-permute-start.13 = (bf16[128,2176]{1,0:T(8,128)(2,1)}, bf16[128,2176]{1,0:T(8,128)(2,1)}, u32[]{:S(2)}, u32[]{:S(2)}) collective-permute-start(bf16[128,2176]{1,0:T(8,128)(2,1)} %pad_maximum_fusion), channel_id=1, source_target_pairs={{0,4},{4,0},{8,12},{12,8},{1,5},{5,1},{9,13},{13,9},{2,6},{6,2},{1... | collective-permute-start | bytes 1671176 | tf_op jit(solution)/shard_map/ppermute | solution.py:400
  76.2 5.0 %deltas.8 = (bf16[64,2048]{1,0:T(8,128)(2,1)}, bf16[64,2048]{1,0:T(8,128)(2,1)}, bf16[136,2048]{1,0:T(8,128)(2,1)}, bf16[4,72,2048]{2,1,0:T(8,128)(2,1)}) custom-call(s32[1]{0:T(128)} %bitcast.1.me_ref.refs_0_, s32[136,1]{1,0:T(8,128)S(1)} %get-tuple-element.240.refs_0_, s32[136,1]{1,0:T(8,128)S(1)} %get-tuple-element.241.refs_1_, ...), custom_call_target="tpu_custom_call" | custom-call | tf_op jit(solution)/shard_map/deltas/pallas_call | solution.py:167
  81.3 3.9 %all-to-all-start = ((bf16[4,72,2048]{2,1,0:T(8,128)(2,1)}), bf16[4,72,2048]{2,1,0:T(8,128)(2,1)S(1)}, u32[]{:S(2)}, u32[]{:S(2)}) async-start(bf16[4,72,2048]{2,1,0:T(8,128)(2,1)} %get-tuple-element.247), calls=%async_computation | async-start | bytes 2359296 | tf_op jit(solution)/shard_map/all_to_all | solution.py:419
  85.1 4.7 %add_convert_fusion.1 = bf16[512,2048]{1,0:T(8,128)(2,1)} fusion(bf16[512,2048]{1,0:T(8,128)(2,1)} %collective-permute-done.17, bf16[512,2048]{1,0:T(8,128)(2,1)} %share.6), kind=kLoop, calls=%fused_computation.32 | loop fusion | flops 4194304 | bytes 6291456 | tf_op jit(solution)/shard_map/convert_element_type | solution.py:416
  90.0 5.7 %scores.9 = (f32[16,128]{1,0:T(8,128)S(1)}, s32[1,1]{1,0:T(1,128)}, s32[128,1]{1,0:T(8,128)S(1)}) custom-call(s32[1]{0:T(128)} %bitcast.1.me_ref.refs_0_, s32[1,1]{1,0:T(1,128)} %get-tuple-element.233.refs_1_, bf16[128,2176]{1,0:T(8,128)(2,1)} %collective-permute-done.13.refs_2_, bf16[1024,2048]{1,0:T(8,128)(2,1)S(1)} %bitcast.37), custom_call_target="tpu_custom_call" | custom-call | tf_op jit(solution)/shard_map/scores/pallas_call | solution.py:91
  95.7 1.5 collective-permute-start.18
  97.2 2.1 %collective-permute-done.18 = f32[16,128]{1,0:T(8,128)S(1)} collective-permute-done((f32[16,128]{1,0:T(8,128)S(1)}, f32[16,128]{1,0:T(8,128)S(1)}, u32[]{:S(2)}, u32[]{:S(2)}) %collective-permute-start.18) | collective-permute-done | bytes 8224 | tf_op jit(solution)/shard_map/ppermute | solution.py:400
  100.5 1.5 collective-permute-start.24
  102.1 2.9 %deltas.9 = bf16[128,2048]{1,0:T(8,128)(2,1)} custom-call(s32[128,1]{1,0:T(8,128)S(1)} %get-tuple-element.253.refs_0_, f32[16,128]{1,0:T(8,128)S(1)} %add.159.refs_1_, bf16[1024,2048]{1,0:T(8,128)(2,1)S(1)} %bitcast.33), custom_call_target="tpu_custom_call" | custom-call | tf_op jit(solution)/shard_map/deltas/pallas_call | solution.py:167
  104.9 1.9 %collective-permute-start.20 = (bf16[128,2048]{1,0:T(8,128)(2,1)}, bf16[128,2048]{1,0:T(8,128)(2,1)}, u32[]{:S(2)}, u32[]{:S(2)}) collective-permute-start(bf16[128,2048]{1,0:T(8,128)(2,1)} %deltas.9), channel_id=1, source_target_pairs={{0,4},{4,0},{8,12},{12,8},{1,5},{5,1},{9,13},{13,9},{2,6},{6,2},{1... | collective-permute-start | bytes 1572872 | tf_op jit(solution)/shard_map/ppermute | solution.py:400
  106.9 7.5 %all-to-all-done.refs_0_ = bf16[4,72,2048]{2,1,0:T(8,128)(2,1)S(1)} async-done(((bf16[4,72,2048]{2,1,0:T(8,128)(2,1)}), bf16[4,72,2048]{2,1,0:T(8,128)(2,1)S(1)}, u32[]{:S(2)}, u32[]{:S(2)}) %all-to-all-start) | async-done | bytes 1179680 | tf_op jit(solution)/shard_map/all_to_all | solution.py:419
  114.4 1.6 %copy-done.2 = bf16[512,2048]{1,0:T(8,128)(2,1)S(1)} copy-done((bf16[512,2048]{1,0:T(8,128)(2,1)S(1)}, bf16[512,2048]{1,0:T(8,128)(2,1)}, u32[]{:S(2)}) %copy-start.2) | copy-done | bytes 2097176
  116.0 5.7 %place.2.refs_3_ = f32[512,2048]{1,0:T(8,128)} custom-call(s32[1]{0:T(128)} %bitcast.1.me_ref.refs_0_, s32[512,1]{1,0:T(8,128)S(1)} %get-tuple-element.278.row_ref, s32[6,256]{1,0:T(8,128)S(1)} %get-tuple-element.219.codes_ref, bf16[4,72,2048]{2,1,0:T(8,128)(2,1)S(1)} %all-to-all-done.refs_0_, bf16[512,2048]{1,0:T(8,128)(2,1)S(1)} %copy-done, ...), custom_call_target="tpu_custom_call" | custom-call | tf_op jit(solution)/shard_map/place/pallas_call | solution.py:201
  123.5 4.1 %collective-permute-start.21 = (bf16[64,2048]{1,0:T(8,128)(2,1)S(1)}, bf16[64,2048]{1,0:T(8,128)(2,1)S(1)}, u32[]{:S(2)}, u32[]{:S(2)}) collective-permute-start(bf16[64,2048]{1,0:T(8,128)(2,1)S(1)} %get-tuple-element.309), channel_id=1, source_target_pairs={{0,8},{4,12},{8,0},{12,4},{1,9},{5,13},{9,1},{13,5},{2,10},{6,14},... | collective-permute-start | bytes 786440 | tf_op jit(solution)/shard_map/ppermute | solution.py:400
  128.1 1.5 collective-permute-start.25
  129.6 2.1 %collective-permute-done.25 = s32[1,1]{1,0:T(1,128)} collective-permute-done((s32[1,1]{1,0:T(1,128)}, s32[1,1]{1,0:T(1,128)}, u32[]{:S(2)}, u32[]{:S(2)}) %collective-permute-start.25) | collective-permute-done | bytes 36 | tf_op jit(solution)/shard_map/ppermute | solution.py:400
  133.0 8.4 %collective-permute-done.21.refs_0_ = bf16[64,2048]{1,0:T(8,128)(2,1)S(1)} collective-permute-done((bf16[64,2048]{1,0:T(8,128)(2,1)S(1)}, bf16[64,2048]{1,0:T(8,128)(2,1)S(1)}, u32[]{:S(2)}, u32[]{:S(2)}) %collective-permute-start.21) | collective-permute-done | bytes 262176 | tf_op jit(solution)/shard_map/ppermute | solution.py:400
  141.4 8.1 %collective-permute-done.22.refs_1_ = bf16[64,2048]{1,0:T(8,128)(2,1)S(1)} collective-permute-done((bf16[64,2048]{1,0:T(8,128)(2,1)S(1)}, bf16[64,2048]{1,0:T(8,128)(2,1)S(1)}, u32[]{:S(2)}, u32[]{:S(2)}) %collective-permute-start.22) | collective-permute-done | bytes 262176 | tf_op jit(solution)/shard_map/ppermute | solution.py:400
  149.4 5.8 %place.3 = bf16[512,2048]{1,0:T(8,128)(2,1)} custom-call(s32[1]{0:T(128)} %bitcast.1.me_ref.refs_0_, s32[512,1]{1,0:T(8,128)S(1)} %get-tuple-element.278.row_ref, s32[6,256]{1,0:T(8,128)S(1)} %get-tuple-element.219.codes_ref, bf16[64,2048]{1,0:T(8,128)(2,1)S(1)} %collective-permute-done.21.refs_0_, bf16[64,2048]{1,0:T(8,128)(2,1)S(1)} %collective-permute-done.22.refs_1_, ...), custom_call_target="tpu_custom_call" | custom-call | tf_op jit(solution)/shard_map/place/pallas_call | solution.py:201
  (62 shorter events, 9.5 us)
Async XLA Ops:
  2.2 10.2 %copy-start.10 = (bf16[4,128,2048]{2,1,0:T(8,128)(2,1)S(1)}, bf16[4,128,2048]{2,1,0:T(8,128)(2,1)}, u32[]{:S(2)}) copy-start(bf16[4,128,2048]{2,1,0:T(8,128)(2,1)} %param.9) | copy-start | bytes 6291460
  6.7 53.7 %collective-permute-start.10 = (bf16[208,2176]{1,0:T(8,128)(2,1)}, bf16[208,2176]{1,0:T(8,128)(2,1)S(1)}, u32[]{:S(2)}, u32[]{:S(2)}) collective-permute-start(bf16[208,2176]{1,0:T(8,128)(2,1)} %get-tuple-element.223), channel_id=1, source_target_pairs={{0,4},{4,0},{8,12},{12,8},{1,5},{5,1},{9,13},{13,9},{2,6},{6,2},{1... | collective-permute-start | bytes 2715656 | tf_op jit(solution)/shard_map/ppermute | solution.py:400
  9.8 50.7 %collective-permute-start.8 = (bf16[136,2176]{1,0:T(8,128)(2,1)}, bf16[136,2176]{1,0:T(8,128)(2,1)S(1)}, u32[]{:S(2)}, u32[]{:S(2)}) collective-permute-start(bf16[136,2176]{1,0:T(8,128)(2,1)} %get-tuple-element.221), channel_id=1, source_target_pairs={{0,8},{4,12},{8,0},{12,4},{1,9},{5,13},{9,1},{13,5},{2,10},{6,14},... | collective-permute-start | bytes 1775624 | tf_op jit(solution)/shard_map/ppermute | solution.py:400
  12.4 48.1 %collective-permute-start.9 = (bf16[136,2176]{1,0:T(8,128)(2,1)S(1)}, bf16[136,2176]{1,0:T(8,128)(2,1)S(1)}, u32[]{:S(2)}, u32[]{:S(2)}) collective-permute-start(bf16[136,2176]{1,0:T(8,128)(2,1)S(1)} %get-tuple-element.222), channel_id=1, source_target_pairs={{0,12},{4,8},{8,4},{12,0},{1,13},{5,9},{9,5},{13,1},{2,14},{6,10},... | collective-permute-start | bytes 1775624 | tf_op jit(solution)/shard_map/ppermute | solution.py:400
  18.0 3.9 %collective-permute-start.11 = (f32[64,128]{1,0:T(8,128)S(1)}, f32[64,128]{1,0:T(8,128)S(1)}, u32[]{:S(2)}, u32[]{:S(2)}) collective-permute-start(f32[64,128]{1,0:T(8,128)S(1)} %get-tuple-element.229), channel_id=1, source_target_pairs={{0,2},{1,3},{2,0},{3,1},{4,6},{5,7},{6,4},{7,5},{8,10},{9,11},{10,... | collective-permute-start | bytes 98312 | tf_op jit(solution)/shard_map/ppermute | solution.py:400
  21.9 33.6 %collective-permute-start.12 = (f32[64,128]{1,0:T(8,128)S(1)}, f32[64,128]{1,0:T(8,128)S(1)}, u32[]{:S(2)}, u32[]{:S(2)}) collective-permute-start(f32[64,128]{1,0:T(8,128)S(1)} %add.153), channel_id=1, source_target_pairs={{0,1},{1,0},{2,3},{3,2},{4,5},{5,4},{6,7},{7,6},{8,9},{9,8},{10,11... | collective-permute-start | bytes 98312 | tf_op jit(solution)/shard_map/ppermute | solution.py:400
  22.0 8.9 %copy-start.11 = (bf16[4,128,2048]{2,1,0:T(8,128)(2,1)S(1)}, bf16[4,128,2048]{2,1,0:T(8,128)(2,1)}, u32[]{:S(2)}) copy-start(bf16[4,128,2048]{2,1,0:T(8,128)(2,1)} %param.9) | copy-start | bytes 6291460
  47.2 8.3 %copy-start.5 = (bf16[64,16,2048]{2,1,0:T(8,128)(2,1)S(1)}, bf16[64,16,2048]{2,1,0:T(8,128)(2,1)}, u32[]{:S(2)}) copy-start(bf16[64,16,2048]{2,1,0:T(8,128)(2,1)} %param.12) | copy-start | bytes 12582916
  55.5 5.0 %copy-start.8 = (bf16[64,16,2048]{2,1,0:T(8,128)(2,1)S(1)}, bf16[64,16,2048]{2,1,0:T(8,128)(2,1)}, u32[]{:S(2)}) copy-start(bf16[64,16,2048]{2,1,0:T(8,128)(2,1)} %param.11) | copy-start | bytes 12582916
  60.5 6.6 %copy-start.3 = (bf16[136,2176]{1,0:T(8,128)(2,1)}, bf16[136,2176]{1,0:T(8,128)(2,1)S(1)}, u32[]{:S(2)}) copy-start(bf16[136,2176]{1,0:T(8,128)(2,1)S(1)} %collective-permute-done.9.refs_3_) | copy-start | bytes 1775620
  67.1 18.1 %collective-permute-start.17 = (bf16[512,2048]{1,0:T(8,128)(2,1)}, bf16[512,2048]{1,0:T(8,128)(2,1)}, u32[]{:S(2)}, u32[]{:S(2)}) collective-permute-start(bf16[512,2048]{1,0:T(8,128)(2,1)} %share.7), channel_id=1, source_target_pairs={{0,1},{1,0},{2,3},{3,2},{4,5},{5,4},{6,7},{7,6},{8,9},{9,8},{10,11... | collective-permute-start | bytes 6291464 | tf_op jit(solution)/shard_map/ppermute | solution.py:400
  67.6 22.4 %collective-permute-start.16 = (bf16[512,2048]{1,0:T(8,128)(2,1)}, bf16[512,2048]{1,0:T(8,128)(2,1)S(1)}, u32[]{:S(2)}, u32[]{:S(2)}) collective-permute-start(bf16[512,2048]{1,0:T(8,128)(2,1)} %share.5), channel_id=1, source_target_pairs={{0,1},{1,0},{2,3},{3,2},{4,5},{5,4},{6,7},{7,6},{8,9},{9,8},{10,11... | collective-permute-start | bytes 6291464 | tf_op jit(solution)/shard_map/ppermute | solution.py:400
  67.6 3.9 %collective-permute-start.14 = (f32[60,128]{1,0:T(8,128)S(1)}, f32[60,128]{1,0:T(8,128)S(1)}, u32[]{:S(2)}, u32[]{:S(2)}) collective-permute-start(f32[60,128]{1,0:T(8,128)S(1)} %get-tuple-element.243), channel_id=1, source_target_pairs={{0,2},{1,3},{2,0},{3,1},{4,6},{5,7},{6,4},{7,5},{8,10},{9,11},{10,... | collective-permute-start | bytes 92168 | tf_op jit(solution)/shard_map/ppermute | solution.py:400
  71.6 4.7 %collective-permute-start.15 = (f32[60,128]{1,0:T(8,128)S(1)}, f32[60,128]{1,0:T(8,128)S(1)}, u32[]{:S(2)}, u32[]{:S(2)}) collective-permute-start(f32[60,128]{1,0:T(8,128)S(1)} %add.155), channel_id=1, source_target_pairs={{0,1},{1,0},{2,3},{3,2},{4,5},{5,4},{6,7},{7,6},{8,9},{9,8},{10,11... | collective-permute-start | bytes 92168 | tf_op jit(solution)/shard_map/ppermute | solution.py:400
  72.4 17.6 %collective-permute-start.13 = (bf16[128,2176]{1,0:T(8,128)(2,1)}, bf16[128,2176]{1,0:T(8,128)(2,1)}, u32[]{:S(2)}, u32[]{:S(2)}) collective-permute-start(bf16[128,2176]{1,0:T(8,128)(2,1)} %pad_maximum_fusion), channel_id=1, source_target_pairs={{0,4},{4,0},{8,12},{12,8},{1,5},{5,1},{9,13},{13,9},{2,6},{6,2},{1... | collective-permute-start | bytes 1671176 | tf_op jit(solution)/shard_map/ppermute | solution.py:400
  81.3 33.1 %all-to-all-start = ((bf16[4,72,2048]{2,1,0:T(8,128)(2,1)}), bf16[4,72,2048]{2,1,0:T(8,128)(2,1)S(1)}, u32[]{:S(2)}, u32[]{:S(2)}) async-start(bf16[4,72,2048]{2,1,0:T(8,128)(2,1)} %get-tuple-element.247), calls=%async_computation | async-start | bytes 2359296 | tf_op jit(solution)/shard_map/all_to_all | solution.py:419
  85.1 4.9 %copy-start.9 = (bf16[64,16,2048]{2,1,0:T(8,128)(2,1)S(1)}, bf16[64,16,2048]{2,1,0:T(8,128)(2,1)}, u32[]{:S(2)}) copy-start(bf16[64,16,2048]{2,1,0:T(8,128)(2,1)} %param.11) | copy-start | bytes 12582916
  90.0 5.7 %copy-start.1 = (bf16[512,2048]{1,0:T(8,128)(2,1)}, bf16[512,2048]{1,0:T(8,128)(2,1)S(1)}, u32[]{:S(2)}) copy-start(bf16[512,2048]{1,0:T(8,128)(2,1)S(1)} %collective-permute-done.16.refs_2_) | copy-start | bytes 6291460
  90.0 12.0 %copy-start.6 = (bf16[64,16,2048]{2,1,0:T(8,128)(2,1)S(1)}, bf16[64,16,2048]{2,1,0:T(8,128)(2,1)}, u32[]{:S(2)}) copy-start(bf16[64,16,2048]{2,1,0:T(8,128)(2,1)} %param.12) | copy-start | bytes 12582916
  95.7 3.7 %collective-permute-start.18 = (f32[16,128]{1,0:T(8,128)S(1)}, f32[16,128]{1,0:T(8,128)S(1)}, u32[]{:S(2)}, u32[]{:S(2)}) collective-permute-start(f32[16,128]{1,0:T(8,128)S(1)} %get-tuple-element.254), channel_id=1, source_target_pairs={{0,2},{1,3},{2,0},{3,1},{4,6},{5,7},{6,4},{7,5},{8,10},{9,11},{10,... | collective-permute-start | bytes 24584 | tf_op jit(solution)/shard_map/ppermute | solution.py:400
  99.3 1.2 collective-permute-start.19
  100.5 48.9 %collective-permute-start.24 = (bf16[512,2048]{1,0:T(8,128)(2,1)}, bf16[512,2048]{1,0:T(8,128)(2,1)}, u32[]{:S(2)}, u32[]{:S(2)}) collective-permute-start(bf16[512,2048]{1,0:T(8,128)(2,1)} %add_convert_fusion.1), channel_id=1, source_target_pairs={{0,2},{1,3},{2,0},{3,1},{4,6},{5,7},{6,4},{7,5},{8,10},{9,11},{10,... | collective-permute-start | bytes 6291464 | tf_op jit(solution)/shard_map/ppermute | solution.py:400
  102.1 12.3 %copy-start = (bf16[512,2048]{1,0:T(8,128)(2,1)S(1)}, bf16[512,2048]{1,0:T(8,128)(2,1)}, u32[]{:S(2)}) copy-start(bf16[512,2048]{1,0:T(8,128)(2,1)} %share.4.refs_1_) | copy-start | bytes 6291460
  104.9 17.5 %collective-permute-start.20 = (bf16[128,2048]{1,0:T(8,128)(2,1)}, bf16[128,2048]{1,0:T(8,128)(2,1)}, u32[]{:S(2)}, u32[]{:S(2)}) collective-permute-start(bf16[128,2048]{1,0:T(8,128)(2,1)} %deltas.9), channel_id=1, source_target_pairs={{0,4},{4,0},{8,12},{12,8},{1,5},{5,1},{9,13},{13,9},{2,6},{6,2},{1... | collective-permute-start | bytes 1572872 | tf_op jit(solution)/shard_map/ppermute | solution.py:400
  114.4 1.6 %copy-start.2 = (bf16[512,2048]{1,0:T(8,128)(2,1)S(1)}, bf16[512,2048]{1,0:T(8,128)(2,1)}, u32[]{:S(2)}) copy-start(bf16[512,2048]{1,0:T(8,128)(2,1)} %copy-done.1) | copy-start | bytes 6291460
  116.0 6.4 %copy-start.16 = (bf16[64,2048]{1,0:T(8,128)(2,1)S(1)}, bf16[64,2048]{1,0:T(8,128)(2,1)}, u32[]{:S(2)}) copy-start(bf16[64,2048]{1,0:T(8,128)(2,1)} %get-tuple-element.264) | copy-start | bytes 786436
  116.0 6.4 %copy-start.17 = (bf16[64,2048]{1,0:T(8,128)(2,1)S(1)}, bf16[64,2048]{1,0:T(8,128)(2,1)}, u32[]{:S(2)}) copy-start(bf16[64,2048]{1,0:T(8,128)(2,1)} %get-tuple-element.266) | copy-start | bytes 786436
  122.4 27.0 %collective-permute-start.23 = (bf16[136,2048]{1,0:T(8,128)(2,1)}, bf16[136,2048]{1,0:T(8,128)(2,1)S(1)}, u32[]{:S(2)}, u32[]{:S(2)}) collective-permute-start(bf16[136,2048]{1,0:T(8,128)(2,1)} %get-tuple-element.267), channel_id=1, source_target_pairs={{0,4},{4,0},{8,12},{12,8},{1,5},{5,1},{9,13},{13,9},{2,6},{6,2},{1... | collective-permute-start | bytes 1671176 | tf_op jit(solution)/shard_map/ppermute | solution.py:400
  123.5 17.8 %collective-permute-start.21 = (bf16[64,2048]{1,0:T(8,128)(2,1)S(1)}, bf16[64,2048]{1,0:T(8,128)(2,1)S(1)}, u32[]{:S(2)}, u32[]{:S(2)}) collective-permute-start(bf16[64,2048]{1,0:T(8,128)(2,1)S(1)} %get-tuple-element.309), channel_id=1, source_target_pairs={{0,8},{4,12},{8,0},{12,4},{1,9},{5,13},{9,1},{13,5},{2,10},{6,14},... | collective-permute-start | bytes 786440 | tf_op jit(solution)/shard_map/ppermute | solution.py:400
  127.6 21.8 %collective-permute-start.22 = (bf16[64,2048]{1,0:T(8,128)(2,1)S(1)}, bf16[64,2048]{1,0:T(8,128)(2,1)S(1)}, u32[]{:S(2)}, u32[]{:S(2)}) collective-permute-start(bf16[64,2048]{1,0:T(8,128)(2,1)S(1)} %get-tuple-element.308), channel_id=1, source_target_pairs={{0,12},{4,8},{8,4},{12,0},{1,13},{5,9},{9,5},{13,1},{2,14},{6,10},... | collective-permute-start | bytes 786440 | tf_op jit(solution)/shard_map/ppermute | solution.py:400
  128.1 3.6 %collective-permute-start.25 = (s32[1,1]{1,0:T(1,128)}, s32[1,1]{1,0:T(1,128)}, u32[]{:S(2)}, u32[]{:S(2)}) collective-permute-start(s32[1,1]{1,0:T(1,128)} %get-tuple-element.233.refs_1_), channel_id=1, source_target_pairs={{0,16},{16,0},{1,17},{17,1},{2,18},{18,2},{3,19},{19,3},{4,20},{20... | collective-permute-start | bytes 20 | tf_op jit(solution)/shard_map/ppermute | solution.py:400
  133.0 22.3 %copy-start.14 = (bf16[512,128]{1,0:T(8,128)(2,1)S(1)}, bf16[512,128]{1,0:T(8,128)(2,1)}, u32[]{:S(2)}) copy-start(bf16[512,128]{1,0:T(8,128)(2,1)} %get-tuple-element.411) | copy-start | bytes 393220
  (1 other events, 0.7 us)

commit v5 on v4

--- a/solution.py
+++ b/solution.py
@@ -444,20 +444,22 @@
     shares = {k: share(at ^ k, x, weight, cols) for k in reversed(range(n_tp))}
     (in_far, in_near, shares), _ = lax.optimization_barrier(((in_far, in_near, shares), self_delta))
 
+    in_relay = jnp.concatenate([v[:SHARED] for v in in_far])
+    in_far, in_relay = lax.optimization_barrier((in_far, in_relay))
+    in_relay = swap(in_relay, "dp", 1)
     found, rounds, part = answer(list(far) + [1], in_far + [in_near], rounds)
-    in_far, shares, _ = lax.optimization_barrier((in_far, shares, rounds))
-    in_relay = swap(jnp.concatenate([v[:SHARED] for v in in_far]), "dp", 1)
+    shares, _ = lax.optimization_barrier((shares, rounds))
     direct = deltas(found, part, expand_store, me, n_dp)
     block = a2a(direct[-1])
 
     adds = {k: [shares[k]] for k in shares}
     for k in range(1, n_tp, 2):
         adds[k ^ 1].append(swap(adds.pop(k)[0], "tp", 1))
+    in_relay, direct = lax.optimization_barrier((in_relay, direct))
+    found, scored, part = answer([RELAY], [in_relay], rounds)
+    adds, _ = lax.optimization_barrier((adds, scored))
     for k in range(2, n_tp, 2):
         adds[k] = [total_of(adds[k])]
-
-    in_relay, direct, adds = lax.optimization_barrier((in_relay, direct, adds))
-    found, _, part = answer([RELAY], [in_relay], rounds)
     part, adds = lax.optimization_barrier((part, adds))
     (relayed,) = deltas(found, part, expand_store)
     relayed = swap(relayed, "dp", 1)
@@ -467,8 +469,9 @@
         for k in sorted((k for k in adds if k & bit), reverse=True):
             adds[k ^ bit].append(swap(total_of(adds.pop(k)), "tp", bit))
         bit *= 2
+    near = after(direct[m], block)
     some = place(me, row_code, codes, m + 1, [], [block], some + [self_delta], jnp.float32)
-    relayed, some, near, direct = lax.optimization_barrier((relayed, some, direct[m], direct))
+    relayed, some, direct = lax.optimization_barrier((relayed, some, direct))
     back = [swap(direct[i] + relayed[i * SHARED:(i + 1) * SHARED], "dp", j) for i, j in enumerate(far)]
     back.append(swap(near, "dp", 1))
     rounds = butterfly(rounds, "rep", jnp.maximum)[0, 0]

time: 156 us -> 164 us (1.051)
  waiting for transfers between devices: 33.6 us -> 41.5 us
  Pallas kernels: 80.3 us -> 78.3 us
    all_to_all x1, waiting for transfers between devices: 7.47 us -> 16.9 us  [a2a(): return lax.all_to_all(v, 'dp', split_axis=0, concat_axis=0, tiled=True)]
    pallas_call x3, Pallas kernels: 17.9 us -> 15.8 us  [scores(): pl.pallas_call(functools.partial(score_kernel, tuple(dists), block), grid...]
  transfers between devices with their start and end apart: 19 -> 19, of which waited for: 10 -> 9; matrix products, arithmetic and copies ran while one was open for 5% -> 4% of each run, Pallas kernels for 41% -> 38%
where the time goes in v5:
time: 164 us; the launch traced here: 162 us
  Pallas kernels  78.3 us (48%)
  waiting for transfers between devices  41.5 us (25%)
  starting transfers between devices  28.4 us (17%)
  other arithmetic  7.17 us (4%)
  local copies, waits for them, and re-layouts  4.63 us (3%)
    pallas_call x4, Pallas kernels, share(): pl.pallas_call(share_kernel, grid_spec=pltpu.PrefetchScalarGridSpec(num_s...  33.4 us
    ppermute x18, waiting for transfers between devices, swap(): return lax.ppermute(v, axis, [(i, i ^ k) for i in range(n)])  24.6 us
    ppermute x18, starting transfers between devices, swap(): return lax.ppermute(v, axis, [(i, i ^ k) for i in range(n)])  24.4 us
    all_to_all x1, waiting for transfers between devices, a2a(): return lax.all_to_all(v, 'dp', split_axis=0, concat_axis=0, tiled=True)  16.9 us
    pallas_call x3, Pallas kernels, scores(): pl.pallas_call(functools.partial(score_kernel, tuple(dists), block), grid...  15.8 us
    pallas_call x3, Pallas kernels, deltas(): pl.pallas_call(kernel, grid=(width // cols,), in_specs=first + ins, out_s...  12.8 us
    pallas_call x2, Pallas kernels, place(): pl.pallas_call(functools.partial(place_kernel, first, len(back), sum((v.s...  11.6 us
    convert_element_type x1, other arithmetic, total_of(): functools.reduce(jnp.add, [v.astype(jnp.float32) for v in parts])  5.32 us
  transfers between devices with their start and end apart: 19, of which 9 were waited for; matrix products, arithmetic and copies ran while one was open for 4% of the time, Pallas kernels for 38%

profile of v5, /device:TPU:0, one launch (start us, length us, event | category | flops | bytes accessed | tf_op | source)
XLA Modules:
  0.0 161.6 jit_solution(5990524301412646576)
XLA Ops:
  2.2 4.5 %pack.1 = (s32[2,32]{1,0:T(2,128)}, s32[512,1]{1,0:T(8,128)S(1)}, s32[512,1]{1,0:T(8,128)S(1)}, bf16[512,128]{1,0:T(8,128)(2,1)}, s32[1,1]{1,0:T(1,128)}, /*inde...) custom-call(s32[1]{0:T(128)} %bitcast.1.me_ref.refs_0_, ...), custom_call_target="tpu_custom_call" | custom-call | tf_op jit(solution)/shard_map/pack/pallas_call | solution.py:336
  6.7 3.0 %collective-permute-start.10 = (bf16[208,2176]{1,0:T(8,128)(2,1)}, bf16[208,2176]{1,0:T(8,128)(2,1)S(1)}, u32[]{:S(2)}, u32[]{:S(2)}) collective-permute-start(bf16[208,2176]{1,0:T(8,128)(2,1)} %get-tuple-element.225), channel_id=1, source_target_pairs={{0,4},{4,0},{8,12},{12,8},{1,5},{5,1},{9,13},{13,9},{2,6},{6,2},{1... | collective-permute-start | bytes 2715656 | tf_op jit(solution)/shard_map/ppermute | solution.py:400
  9.8 2.6 %collective-permute-start.8 = (bf16[136,2176]{1,0:T(8,128)(2,1)}, bf16[136,2176]{1,0:T(8,128)(2,1)S(1)}, u32[]{:S(2)}, u32[]{:S(2)}) collective-permute-start(bf16[136,2176]{1,0:T(8,128)(2,1)} %get-tuple-element.223), channel_id=1, source_target_pairs={{0,8},{4,12},{8,0},{12,4},{1,9},{5,13},{9,1},{13,5},{2,10},{6,14},... | collective-permute-start | bytes 1775624 | tf_op jit(solution)/shard_map/ppermute | solution.py:400
  12.4 5.7 %scores.7 = (f32[64,128]{1,0:T(8,128)S(1)}, s32[1,1]{1,0:T(1,128)}, s32[512,1]{1,0:T(8,128)S(1)}) custom-call(s32[1]{0:T(128)} %bitcast.1.me_ref.refs_0_, s32[512,1]{1,0:T(8,128)S(1)} %get-tuple-element.228.refs_1_, bf16[512,2048]{1,0:T(8,128)(2,1)S(1)} %bitcast.41, bf16[1024,2048]{1,0:T(8,128)(2,1)} %bitcast.34), custom_call_target="tpu_custom_call" | custom-call | tf_op jit(solution)/shard_map/scores/pallas_call | solution.py:91
  18.0 1.7 %collective-permute-start.11 = (f32[64,128]{1,0:T(8,128)S(1)}, f32[64,128]{1,0:T(8,128)S(1)}, u32[]{:S(2)}, u32[]{:S(2)}) collective-permute-start(f32[64,128]{1,0:T(8,128)S(1)} %get-tuple-element.231), channel_id=1, source_target_pairs={{0,2},{1,3},{2,0},{3,1},{4,6},{5,7},{6,4},{7,5},{8,10},{9,11},{10,... | collective-permute-start | bytes 98312 | tf_op jit(solution)/shard_map/ppermute | solution.py:400
  19.8 2.2 %collective-permute-done.11 = f32[64,128]{1,0:T(8,128)S(1)} collective-permute-done((f32[64,128]{1,0:T(8,128)S(1)}, f32[64,128]{1,0:T(8,128)S(1)}, u32[]{:S(2)}, u32[]{:S(2)}) %collective-permute-start.11) | collective-permute-done | bytes 32800 | tf_op jit(solution)/shard_map/ppermute | solution.py:400
  22.0 8.9 %share.4.refs_1_ = bf16[512,2048]{1,0:T(8,128)(2,1)} custom-call(s32[1]{0:T(128)} %bitcast.4.at_ref, bf16[512,2048]{1,0:T(8,128)(2,1)} %bitcast.39, bf16[2048,8192]{1,0:T(8,128)(2,1)} %w_ref.7), custom_call_target="tpu_custom_call" | custom-call | tf_op jit(solution)/shard_map/share/pallas_call | solution.py:354
  30.9 8.1 %share.5 = bf16[512,2048]{1,0:T(8,128)(2,1)} custom-call(s32[1]{0:T(128)S(6)} %xor.22.at_ref, bf16[512,2048]{1,0:T(8,128)(2,1)S(1)} %bitcast.42, bf16[2048,8192]{1,0:T(8,128)(2,1)} %w_ref.7), custom_call_target="tpu_custom_call" | custom-call | tf_op jit(solution)/shard_map/share/pallas_call | solution.py:354
  39.0 8.2 %share.6 = bf16[512,2048]{1,0:T(8,128)(2,1)} custom-call(s32[1]{0:T(128)S(6)} %xor.23.at_ref, bf16[512,2048]{1,0:T(8,128)(2,1)S(1)} %bitcast.43, bf16[2048,8192]{1,0:T(8,128)(2,1)} %w_ref.7), custom_call_target="tpu_custom_call" | custom-call | tf_op jit(solution)/shard_map/share/pallas_call | solution.py:354
  47.1 8.3 %share.7 = bf16[512,2048]{1,0:T(8,128)(2,1)} custom-call(s32[1]{0:T(128)S(6)} %xor.24.at_ref, bf16[512,2048]{1,0:T(8,128)(2,1)S(1)} %bitcast.44, bf16[2048,8192]{1,0:T(8,128)(2,1)} %w_ref.7), custom_call_target="tpu_custom_call" | custom-call | tf_op jit(solution)/shard_map/share/pallas_call | solution.py:354
  55.5 4.9 %deltas.7.refs_3_ = bf16[512,2048]{1,0:T(8,128)(2,1)} custom-call(s32[512,1]{1,0:T(8,128)S(1)} %get-tuple-element.230.refs_0_, f32[64,128]{1,0:T(8,128)S(1)} %add.154.refs_1_, bf16[1024,2048]{1,0:T(8,128)(2,1)S(1)} %bitcast.31), custom_call_target="tpu_custom_call" | custom-call | tf_op jit(solution)/shard_map/deltas/pallas_call | solution.py:167
  60.5 6.5 %scores.8 = (f32[60,128]{1,0:T(8,128)S(1)}, s32[1,1]{1,0:T(1,128)}, s32[136,1]{1,0:T(8,128)S(1)}, s32[136,1]{1,0:T(8,128)S(1)}, s32[208,1]{1,0:T(8,128)S(1)}) custom-call(s32[1]{0:T(128)} %bitcast.1.me_ref.refs_0_, s32[1,1]{1,0:T(1,128)} %get-tuple-element.222.refs_1_, bf16[136,2176]{1,0:T(8,128)(2,1)S(1)} %collective-permute-done.8.refs_2_, ...), custom_call_target="tpu_custom_call" | custom-call | tf_op jit(solution)/shard_map/scores/pallas_call | solution.py:91
  67.6 3.9 %collective-permute-start.13 = (bf16[128,2176]{1,0:T(8,128)(2,1)S(1)}, bf16[128,2176]{1,0:T(8,128)(2,1)S(1)}, u32[]{:S(2)}, u32[]{:S(2)}) collective-permute-start(bf16[128,2176]{1,0:T(8,128)(2,1)S(1)} %pad_maximum_fusion), channel_id=1, source_target_pairs={{0,4},{4,0},{8,12},{12,8},{1,5},{5,1},{9,13},{13,9},{2,6},{6,2},{1... | collective-permute-start | bytes 1671176 | tf_op jit(solution)/shard_map/ppermute | solution.py:400
  73.1 2.4 %collective-permute-done.14 = f32[60,128]{1,0:T(8,128)S(1)} collective-permute-done((f32[60,128]{1,0:T(8,128)S(1)}, f32[60,128]{1,0:T(8,128)S(1)}, u32[]{:S(2)}, u32[]{:S(2)}) %collective-permute-start.14) | collective-permute-done | bytes 30752 | tf_op jit(solution)/shard_map/ppermute | solution.py:400
  76.7 5.0 %deltas.8 = (bf16[64,2048]{1,0:T(8,128)(2,1)}, bf16[64,2048]{1,0:T(8,128)(2,1)}, bf16[136,2048]{1,0:T(8,128)(2,1)}, bf16[4,72,2048]{2,1,0:T(8,128)(2,1)}) custom-call(s32[1]{0:T(128)} %bitcast.1.me_ref.refs_0_, s32[136,1]{1,0:T(8,128)S(1)} %get-tuple-element.239.refs_0_, s32[136,1]{1,0:T(8,128)S(1)} %get-tuple-element.240.refs_1_, ...), custom_call_target="tpu_custom_call" | custom-call | tf_op jit(solution)/shard_map/deltas/pallas_call | solution.py:167
  81.7 2.7 %collective-permute-done.13.refs_2_ = bf16[128,2176]{1,0:T(8,128)(2,1)S(1)} collective-permute-done((bf16[128,2176]{1,0:T(8,128)(2,1)S(1)}, bf16[128,2176]{1,0:T(8,128)(2,1)S(1)}, u32[]{:S(2)}, u32[]{:S(2)}) %collective-permute-start.13) | collective-permute-done | bytes 557088 | tf_op jit(solution)/shard_map/ppermute | solution.py:400
  84.3 3.7 %scores.9 = (f32[16,128]{1,0:T(8,128)S(1)}, s32[1,1]{1,0:T(1,128)}, s32[128,1]{1,0:T(8,128)S(1)}) custom-call(s32[1]{0:T(128)} %bitcast.1.me_ref.refs_0_, s32[1,1]{1,0:T(1,128)} %get-tuple-element.237.refs_1_, bf16[128,2176]{1,0:T(8,128)(2,1)S(1)} %collective-permute-done.13.refs_2_, bf16[1024,2048]{1,0:T(8,128)(2,1)S(1)} %bitcast.37), custom_call_target="tpu_custom_call" | custom-call | tf_op jit(solution)/shard_map/scores/pallas_call | solution.py:91
  90.1 2.1 %collective-permute-done.16 = f32[16,128]{1,0:T(8,128)S(1)} collective-permute-done((f32[16,128]{1,0:T(8,128)S(1)}, f32[16,128]{1,0:T(8,128)S(1)}, u32[]{:S(2)}, u32[]{:S(2)}) %collective-permute-start.16) | collective-permute-done | bytes 8224 | tf_op jit(solution)/shard_map/ppermute | solution.py:400
  92.3 4.0 %all-to-all-start = ((bf16[4,72,2048]{2,1,0:T(8,128)(2,1)}), bf16[4,72,2048]{2,1,0:T(8,128)(2,1)S(1)}, u32[]{:S(2)}, u32[]{:S(2)}) async-start(bf16[4,72,2048]{2,1,0:T(8,128)(2,1)} %get-tuple-element.246), calls=%async_computation | async-start | bytes 2359296 | tf_op jit(solution)/shard_map/all_to_all | solution.py:419
  97.0 5.3 %add_convert_fusion.1 = bf16[512,2048]{1,0:T(8,128)(2,1)} fusion(bf16[512,2048]{1,0:T(8,128)(2,1)} %collective-permute-done.19, bf16[512,2048]{1,0:T(8,128)(2,1)} %share.6), kind=kLoop, calls=%fused_computation.32 | loop fusion | flops 4194304 | bytes 6291456 | tf_op jit(solution)/shard_map/convert_element_type | solution.py:416
  103.9 2.9 %deltas.9 = bf16[128,2048]{1,0:T(8,128)(2,1)} custom-call(s32[128,1]{1,0:T(8,128)S(1)} %copy-done.4, f32[16,128]{1,0:T(8,128)S(1)} %add.158.refs_1_, bf16[1024,2048]{1,0:T(8,128)(2,1)S(1)} %bitcast.33), custom_call_target="tpu_custom_call" | custom-call | tf_op jit(solution)/shard_map/deltas/pallas_call | solution.py:167
  106.8 2.0 %collective-permute-start.20 = (bf16[128,2048]{1,0:T(8,128)(2,1)}, bf16[128,2048]{1,0:T(8,128)(2,1)}, u32[]{:S(2)}, u32[]{:S(2)}) collective-permute-start(bf16[128,2048]{1,0:T(8,128)(2,1)} %deltas.9), channel_id=1, source_target_pairs={{0,4},{4,0},{8,12},{12,8},{1,5},{5,1},{9,13},{13,9},{2,6},{6,2},{1... | collective-permute-start | bytes 1572872 | tf_op jit(solution)/shard_map/ppermute | solution.py:400
  108.8 16.9 %all-to-all-done.refs_0_ = bf16[4,72,2048]{2,1,0:T(8,128)(2,1)S(1)} async-done(((bf16[4,72,2048]{2,1,0:T(8,128)(2,1)}), bf16[4,72,2048]{2,1,0:T(8,128)(2,1)S(1)}, u32[]{:S(2)}, u32[]{:S(2)}) %all-to-all-start) | async-done | bytes 1179680 | tf_op jit(solution)/shard_map/all_to_all | solution.py:419
  125.7 1.6 copy-done.2
  127.3 5.7 %place.2.refs_3_ = f32[512,2048]{1,0:T(8,128)} custom-call(s32[1]{0:T(128)} %bitcast.1.me_ref.refs_0_, s32[512,1]{1,0:T(8,128)S(1)} %get-tuple-element.282.row_ref, s32[6,256]{1,0:T(8,128)S(1)} %get-tuple-element.221.codes_ref, bf16[4,72,2048]{2,1,0:T(8,128)(2,1)S(1)} %all-to-all-done.refs_0_, bf16[512,2048]{1,0:T(8,128)(2,1)S(1)} %copy-done, ...), custom_call_target="tpu_custom_call" | custom-call | tf_op jit(solution)/shard_map/place/pallas_call | solution.py:201
  134.1 2.0 %collective-permute-start.21 = (bf16[64,2048]{1,0:T(8,128)(2,1)S(1)}, bf16[64,2048]{1,0:T(8,128)(2,1)S(1)}, u32[]{:S(2)}, u32[]{:S(2)}) collective-permute-start(bf16[64,2048]{1,0:T(8,128)(2,1)S(1)} %get-tuple-element.313), channel_id=1, source_target_pairs={{0,8},{4,12},{8,0},{12,4},{1,9},{5,13},{9,1},{13,5},{2,10},{6,14},... | collective-permute-start | bytes 786440 | tf_op jit(solution)/shard_map/ppermute | solution.py:400
  136.1 2.4 %collective-permute-start.22 = (bf16[64,2048]{1,0:T(8,128)(2,1)S(1)}, bf16[64,2048]{1,0:T(8,128)(2,1)S(1)}, u32[]{:S(2)}, u32[]{:S(2)}) collective-permute-start(bf16[64,2048]{1,0:T(8,128)(2,1)S(1)} %get-tuple-element.312), channel_id=1, source_target_pairs={{0,12},{4,8},{8,4},{12,0},{1,13},{5,9},{9,5},{13,1},{2,14},{6,10},... | collective-permute-start | bytes 786440 | tf_op jit(solution)/shard_map/ppermute | solution.py:400
  138.6 1.5 collective-permute-start.25
  140.2 2.2 %collective-permute-done.25 = s32[1,1]{1,0:T(1,128)} collective-permute-done((s32[1,1]{1,0:T(1,128)}, s32[1,1]{1,0:T(1,128)}, u32[]{:S(2)}, u32[]{:S(2)}) %collective-permute-start.25) | collective-permute-done | bytes 36 | tf_op jit(solution)/shard_map/ppermute | solution.py:400
  143.7 3.0 %collective-permute-done.23.refs_2_ = bf16[136,2048]{1,0:T(8,128)(2,1)} collective-permute-done((bf16[136,2048]{1,0:T(8,128)(2,1)}, bf16[136,2048]{1,0:T(8,128)(2,1)}, u32[]{:S(2)}, u32[]{:S(2)}) %collective-permute-start.23) | collective-permute-done | bytes 557088 | tf_op jit(solution)/shard_map/ppermute | solution.py:400
  146.8 8.8 %collective-permute-done.21.refs_0_ = bf16[64,2048]{1,0:T(8,128)(2,1)S(1)} collective-permute-done((bf16[64,2048]{1,0:T(8,128)(2,1)S(1)}, bf16[64,2048]{1,0:T(8,128)(2,1)S(1)}, u32[]{:S(2)}, u32[]{:S(2)}) %collective-permute-start.21) | collective-permute-done | bytes 262176 | tf_op jit(solution)/shard_map/ppermute | solution.py:400
  155.5 5.9 %place.3 = bf16[512,2048]{1,0:T(8,128)(2,1)} custom-call(s32[1]{0:T(128)} %bitcast.1.me_ref.refs_0_, s32[512,1]{1,0:T(8,128)S(1)} %get-tuple-element.282.row_ref, s32[6,256]{1,0:T(8,128)S(1)} %get-tuple-element.221.codes_ref, bf16[64,2048]{1,0:T(8,128)(2,1)S(1)} %collective-permute-done.21.refs_0_, bf16[64,2048]{1,0:T(8,128)(2,1)S(1)} %collective-permute-done.22.refs_1_, ...), custom_call_target="tpu_custom_call" | custom-call | tf_op jit(solution)/shard_map/place/pallas_call | solution.py:201
  (64 shorter events, 11.3 us)
Async XLA Ops:
  2.2 10.2 %copy-start.10 = (bf16[4,128,2048]{2,1,0:T(8,128)(2,1)S(1)}, bf16[4,128,2048]{2,1,0:T(8,128)(2,1)}, u32[]{:S(2)}) copy-start(bf16[4,128,2048]{2,1,0:T(8,128)(2,1)} %param.9) | copy-start | bytes 6291460
  6.7 53.7 %collective-permute-start.10 = (bf16[208,2176]{1,0:T(8,128)(2,1)}, bf16[208,2176]{1,0:T(8,128)(2,1)S(1)}, u32[]{:S(2)}, u32[]{:S(2)}) collective-permute-start(bf16[208,2176]{1,0:T(8,128)(2,1)} %get-tuple-element.225), channel_id=1, source_target_pairs={{0,4},{4,0},{8,12},{12,8},{1,5},{5,1},{9,13},{13,9},{2,6},{6,2},{1... | collective-permute-start | bytes 2715656 | tf_op jit(solution)/shard_map/ppermute | solution.py:400
  9.8 50.6 %collective-permute-start.8 = (bf16[136,2176]{1,0:T(8,128)(2,1)}, bf16[136,2176]{1,0:T(8,128)(2,1)S(1)}, u32[]{:S(2)}, u32[]{:S(2)}) collective-permute-start(bf16[136,2176]{1,0:T(8,128)(2,1)} %get-tuple-element.223), channel_id=1, source_target_pairs={{0,8},{4,12},{8,0},{12,4},{1,9},{5,13},{9,1},{13,5},{2,10},{6,14},... | collective-permute-start | bytes 1775624 | tf_op jit(solution)/shard_map/ppermute | solution.py:400
  12.4 48.0 %collective-permute-start.9 = (bf16[136,2176]{1,0:T(8,128)(2,1)S(1)}, bf16[136,2176]{1,0:T(8,128)(2,1)S(1)}, u32[]{:S(2)}, u32[]{:S(2)}) collective-permute-start(bf16[136,2176]{1,0:T(8,128)(2,1)S(1)} %get-tuple-element.224), channel_id=1, source_target_pairs={{0,12},{4,8},{8,4},{12,0},{1,13},{5,9},{9,5},{13,1},{2,14},{6,10},... | collective-permute-start | bytes 1775624 | tf_op jit(solution)/shard_map/ppermute | solution.py:400
  18.0 3.9 %collective-permute-start.11 = (f32[64,128]{1,0:T(8,128)S(1)}, f32[64,128]{1,0:T(8,128)S(1)}, u32[]{:S(2)}, u32[]{:S(2)}) collective-permute-start(f32[64,128]{1,0:T(8,128)S(1)} %get-tuple-element.231), channel_id=1, source_target_pairs={{0,2},{1,3},{2,0},{3,1},{4,6},{5,7},{6,4},{7,5},{8,10},{9,11},{10,... | collective-permute-start | bytes 98312 | tf_op jit(solution)/shard_map/ppermute | solution.py:400
  21.9 33.5 %collective-permute-start.12 = (f32[64,128]{1,0:T(8,128)S(1)}, f32[64,128]{1,0:T(8,128)S(1)}, u32[]{:S(2)}, u32[]{:S(2)}) collective-permute-start(f32[64,128]{1,0:T(8,128)S(1)} %add.153), channel_id=1, source_target_pairs={{0,1},{1,0},{2,3},{3,2},{4,5},{5,4},{6,7},{7,6},{8,9},{9,8},{10,11... | collective-permute-start | bytes 98312 | tf_op jit(solution)/shard_map/ppermute | solution.py:400
  22.0 8.9 %copy-start.11 = (bf16[4,128,2048]{2,1,0:T(8,128)(2,1)S(1)}, bf16[4,128,2048]{2,1,0:T(8,128)(2,1)}, u32[]{:S(2)}) copy-start(bf16[4,128,2048]{2,1,0:T(8,128)(2,1)} %param.9) | copy-start | bytes 6291460
  47.1 8.3 %copy-start.6 = (bf16[64,16,2048]{2,1,0:T(8,128)(2,1)S(1)}, bf16[64,16,2048]{2,1,0:T(8,128)(2,1)}, u32[]{:S(2)}) copy-start(bf16[64,16,2048]{2,1,0:T(8,128)(2,1)} %param.12) | copy-start | bytes 12582916
  55.4 5.1 %copy-start.9 = (bf16[64,16,2048]{2,1,0:T(8,128)(2,1)S(1)}, bf16[64,16,2048]{2,1,0:T(8,128)(2,1)}, u32[]{:S(2)}) copy-start(bf16[64,16,2048]{2,1,0:T(8,128)(2,1)} %param.11) | copy-start | bytes 12582916
  67.1 30.0 %collective-permute-start.18 = (bf16[512,2048]{1,0:T(8,128)(2,1)}, bf16[512,2048]{1,0:T(8,128)(2,1)S(1)}, u32[]{:S(2)}, u32[]{:S(2)}) collective-permute-start(bf16[512,2048]{1,0:T(8,128)(2,1)} %share.5), channel_id=1, source_target_pairs={{0,1},{1,0},{2,3},{3,2},{4,5},{5,4},{6,7},{7,6},{8,9},{9,8},{10,11... | collective-permute-start | bytes 6291464 | tf_op jit(solution)/shard_map/ppermute | solution.py:400
  67.6 29.4 %collective-permute-start.19 = (bf16[512,2048]{1,0:T(8,128)(2,1)}, bf16[512,2048]{1,0:T(8,128)(2,1)}, u32[]{:S(2)}, u32[]{:S(2)}) collective-permute-start(bf16[512,2048]{1,0:T(8,128)(2,1)} %share.7), channel_id=1, source_target_pairs={{0,1},{1,0},{2,3},{3,2},{4,5},{5,4},{6,7},{7,6},{8,9},{9,8},{10,11... | collective-permute-start | bytes 6291464 | tf_op jit(solution)/shard_map/ppermute | solution.py:400
  67.6 16.7 %collective-permute-start.13 = (bf16[128,2176]{1,0:T(8,128)(2,1)S(1)}, bf16[128,2176]{1,0:T(8,128)(2,1)S(1)}, u32[]{:S(2)}, u32[]{:S(2)}) collective-permute-start(bf16[128,2176]{1,0:T(8,128)(2,1)S(1)} %pad_maximum_fusion), channel_id=1, source_target_pairs={{0,4},{4,0},{8,12},{12,8},{1,5},{5,1},{9,13},{13,9},{2,6},{6,2},{1... | collective-permute-start | bytes 1671176 | tf_op jit(solution)/shard_map/ppermute | solution.py:400
  71.5 3.9 %collective-permute-start.14 = (f32[60,128]{1,0:T(8,128)S(1)}, f32[60,128]{1,0:T(8,128)S(1)}, u32[]{:S(2)}, u32[]{:S(2)}) collective-permute-start(f32[60,128]{1,0:T(8,128)S(1)} %get-tuple-element.242), channel_id=1, source_target_pairs={{0,2},{1,3},{2,0},{3,1},{4,6},{5,7},{6,4},{7,5},{8,10},{9,11},{10,... | collective-permute-start | bytes 92168 | tf_op jit(solution)/shard_map/ppermute | solution.py:400
  75.5 1.2 collective-permute-start.15
  88.6 3.7 %collective-permute-start.16 = (f32[16,128]{1,0:T(8,128)S(1)}, f32[16,128]{1,0:T(8,128)S(1)}, u32[]{:S(2)}, u32[]{:S(2)}) collective-permute-start(f32[16,128]{1,0:T(8,128)S(1)} %get-tuple-element.249), channel_id=1, source_target_pairs={{0,2},{1,3},{2,0},{3,1},{4,6},{5,7},{6,4},{7,5},{8,10},{9,11},{10,... | collective-permute-start | bytes 24584 | tf_op jit(solution)/shard_map/ppermute | solution.py:400
  92.3 4.0 %collective-permute-start.17 = (f32[16,128]{1,0:T(8,128)S(1)}, f32[16,128]{1,0:T(8,128)}, u32[]{:S(2)}, u32[]{:S(2)}) collective-permute-start(f32[16,128]{1,0:T(8,128)S(1)} %add.157), channel_id=1, source_target_pairs={{0,1},{1,0},{2,3},{3,2},{4,5},{5,4},{6,7},{7,6},{8,9},{9,8},{10,11... | collective-permute-start | bytes 24584 | tf_op jit(solution)/shard_map/ppermute | solution.py:400
  92.3 33.4 %all-to-all-start = ((bf16[4,72,2048]{2,1,0:T(8,128)(2,1)}), bf16[4,72,2048]{2,1,0:T(8,128)(2,1)S(1)}, u32[]{:S(2)}, u32[]{:S(2)}) async-start(bf16[4,72,2048]{2,1,0:T(8,128)(2,1)} %get-tuple-element.246), calls=%async_computation | async-start | bytes 2359296 | tf_op jit(solution)/shard_map/all_to_all | solution.py:419
  97.0 6.9 %copy-start.4 = (s32[128,1]{1,0:T(8,128)S(1)}, s32[128,1]{1,0:T(8,128)}, u32[]{:S(2)}) copy-start(s32[128,1]{1,0:T(8,128)} %copy-done.3) | copy-start | bytes 1540
  97.0 6.9 %copy-start.7 = (bf16[64,16,2048]{2,1,0:T(8,128)(2,1)S(1)}, bf16[64,16,2048]{2,1,0:T(8,128)(2,1)}, u32[]{:S(2)}) copy-start(bf16[64,16,2048]{2,1,0:T(8,128)(2,1)} %param.12) | copy-start | bytes 12582916
  97.0 5.3 %copy-start.1 = (bf16[512,2048]{1,0:T(8,128)(2,1)}, bf16[512,2048]{1,0:T(8,128)(2,1)S(1)}, u32[]{:S(2)}) copy-start(bf16[512,2048]{1,0:T(8,128)(2,1)S(1)} %collective-permute-done.18.refs_2_) | copy-start | bytes 6291460
  102.4 53.2 %collective-permute-start.24 = (bf16[512,2048]{1,0:T(8,128)(2,1)}, bf16[512,2048]{1,0:T(8,128)(2,1)}, u32[]{:S(2)}, u32[]{:S(2)}) collective-permute-start(bf16[512,2048]{1,0:T(8,128)(2,1)} %add_convert_fusion.1), channel_id=1, source_target_pairs={{0,2},{1,3},{2,0},{3,1},{4,6},{5,7},{6,4},{7,5},{8,10},{9,11},{10,... | collective-permute-start | bytes 6291464 | tf_op jit(solution)/shard_map/ppermute | solution.py:400
  103.9 21.8 %copy-start = (bf16[512,2048]{1,0:T(8,128)(2,1)S(1)}, bf16[512,2048]{1,0:T(8,128)(2,1)}, u32[]{:S(2)}) copy-start(bf16[512,2048]{1,0:T(8,128)(2,1)} %share.4.refs_1_) | copy-start | bytes 6291460
  106.8 26.2 %collective-permute-start.20 = (bf16[128,2048]{1,0:T(8,128)(2,1)}, bf16[128,2048]{1,0:T(8,128)(2,1)}, u32[]{:S(2)}, u32[]{:S(2)}) collective-permute-start(bf16[128,2048]{1,0:T(8,128)(2,1)} %deltas.9), channel_id=1, source_target_pairs={{0,4},{4,0},{8,12},{12,8},{1,5},{5,1},{9,13},{13,9},{2,6},{6,2},{1... | collective-permute-start | bytes 1572872 | tf_op jit(solution)/shard_map/ppermute | solution.py:400
  125.7 21.1 %collective-permute-start.23 = (bf16[136,2048]{1,0:T(8,128)(2,1)}, bf16[136,2048]{1,0:T(8,128)(2,1)}, u32[]{:S(2)}, u32[]{:S(2)}) collective-permute-start(bf16[136,2048]{1,0:T(8,128)(2,1)} %get-tuple-element.271), channel_id=1, source_target_pairs={{0,4},{4,0},{8,12},{12,8},{1,5},{5,1},{9,13},{13,9},{2,6},{6,2},{1... | collective-permute-start | bytes 1671176 | tf_op jit(solution)/shard_map/ppermute | solution.py:400
  125.7 1.6 copy-start.2
  127.3 5.7 %copy-start.15 = (bf16[64,2048]{1,0:T(8,128)(2,1)S(1)}, bf16[64,2048]{1,0:T(8,128)(2,1)}, u32[]{:S(2)}) copy-start(bf16[64,2048]{1,0:T(8,128)(2,1)} %get-tuple-element.268) | copy-start | bytes 786436
  127.3 5.7 %copy-start.16 = (bf16[64,2048]{1,0:T(8,128)(2,1)S(1)}, bf16[64,2048]{1,0:T(8,128)(2,1)}, u32[]{:S(2)}) copy-start(bf16[64,2048]{1,0:T(8,128)(2,1)} %get-tuple-element.270) | copy-start | bytes 786436
  134.1 21.4 %collective-permute-start.21 = (bf16[64,2048]{1,0:T(8,128)(2,1)S(1)}, bf16[64,2048]{1,0:T(8,128)(2,1)S(1)}, u32[]{:S(2)}, u32[]{:S(2)}) collective-permute-start(bf16[64,2048]{1,0:T(8,128)(2,1)S(1)} %get-tuple-element.313), channel_id=1, source_target_pairs={{0,8},{4,12},{8,0},{12,4},{1,9},{5,13},{9,1},{13,5},{2,10},{6,14},... | collective-permute-start | bytes 786440 | tf_op jit(solution)/shard_map/ppermute | solution.py:400
  136.1 19.4 %collective-permute-start.22 = (bf16[64,2048]{1,0:T(8,128)(2,1)S(1)}, bf16[64,2048]{1,0:T(8,128)(2,1)S(1)}, u32[]{:S(2)}, u32[]{:S(2)}) collective-permute-start(bf16[64,2048]{1,0:T(8,128)(2,1)S(1)} %get-tuple-element.312), channel_id=1, source_target_pairs={{0,12},{4,8},{8,4},{12,0},{1,13},{5,9},{9,5},{13,1},{2,14},{6,10},... | collective-permute-start | bytes 786440 | tf_op jit(solution)/shard_map/ppermute | solution.py:400
  138.6 3.7 %collective-permute-start.25 = (s32[1,1]{1,0:T(1,128)}, s32[1,1]{1,0:T(1,128)}, u32[]{:S(2)}, u32[]{:S(2)}) collective-permute-start(s32[1,1]{1,0:T(1,128)} %get-tuple-element.237.refs_1_), channel_id=1, source_target_pairs={{0,16},{16,0},{1,17},{17,1},{2,18},{18,2},{3,19},{19,3},{4,20},{20... | collective-permute-start | bytes 20 | tf_op jit(solution)/shard_map/ppermute | solution.py:400
  143.7 17.8 %copy-start.14 = (bf16[512,128]{1,0:T(8,128)(2,1)S(1)}, bf16[512,128]{1,0:T(8,128)(2,1)}, u32[]{:S(2)}) copy-start(bf16[512,128]{1,0:T(8,128)(2,1)} %get-tuple-element.415) | copy-start | bytes 393220
  143.7 17.8 %copy-start.17 = (s32[2,32]{1,0:T(2,128)S(1)}, s32[2,32]{1,0:T(2,128)}, u32[]{:S(2)}) copy-start(s32[2,32]{1,0:T(2,128)} %get-tuple-element.413) | copy-start | bytes 772
  (2 other events, 1.3 us)

commit v6 on v4

--- a/solution.py
+++ b/solution.py
@@ -436,13 +436,12 @@
     in_far = [swap(v, "dp", j) for v, j in zip(out_far, far)]
     in_near = swap(out_near, "dp", 1)
 
-    found, _, self_part = answer([None], [after(x, table)], self_slots)
-    (self_delta,) = deltas(found, self_part, expand_store)
+    self_found, _, self_part = answer([None], [after(x, table)], self_slots)
 
     at = after(lax.axis_index("tp").reshape(1), table)
     cols = weight.shape[1] // n_tp
     shares = {k: share(at ^ k, x, weight, cols) for k in reversed(range(n_tp))}
-    (in_far, in_near, shares), _ = lax.optimization_barrier(((in_far, in_near, shares), self_delta))
+    (in_far, in_near, shares), _ = lax.optimization_barrier(((in_far, in_near, shares), self_part))
 
     found, rounds, part = answer(list(far) + [1], in_far + [in_near], rounds)
     in_far, shares, _ = lax.optimization_barrier((in_far, shares, rounds))
@@ -460,6 +459,7 @@
     found, _, part = answer([RELAY], [in_relay], rounds)
     part, adds = lax.optimization_barrier((part, adds))
     (relayed,) = deltas(found, part, expand_store)
+    (self_delta,) = deltas(self_found, after(self_part, relayed), expand_store)
     relayed = swap(relayed, "dp", 1)
     some, adds[0] = adds[0], []
     bit = 2

time: 156 us -> 156 us (level)
  waiting for transfers between devices: 33.6 us -> 30.9 us
  starting transfers between devices: 28.3 us -> 30.8 us
    all_to_all x1, waiting for transfers between devices: 7.47 us -> 2.54 us  [a2a(): return lax.all_to_all(v, 'dp', split_axis=0, concat_axis=0, tiled=True)]
    ppermute x18, starting transfers between devices: 24.4 us -> 27 us  [swap(): return lax.ppermute(v, axis, [(i, i ^ k) for i in range(n)])]
    ppermute x18, waiting for transfers between devices: 26.1 us -> 28.3 us  [swap(): return lax.ppermute(v, axis, [(i, i ^ k) for i in range(n)])]
  transfers between devices with their start and end apart: 19 -> 19, of which waited for: 10 -> 11; matrix products, arithmetic and copies ran while one was open for 5% -> 5% of each run, Pallas kernels for 41% -> 41%
where the time goes in v6:
time: 156 us
  Pallas kernels  80.3 us (51%)
  waiting for transfers between devices  30.9 us (20%)
  starting transfers between devices  30.8 us (20%)
  other arithmetic  7.23 us (5%)
  local copies, waits for them, and re-layouts  4.96 us (3%)
    pallas_call x4, Pallas kernels, share(): pl.pallas_call(share_kernel, grid_spec=pltpu.PrefetchScalarGridSpec(num_s...  33.4 us
    ppermute x18, waiting for transfers between devices, swap(): return lax.ppermute(v, axis, [(i, i ^ k) for i in range(n)])  28.3 us
    ppermute x18, starting transfers between devices, swap(): return lax.ppermute(v, axis, [(i, i ^ k) for i in range(n)])  27 us
    pallas_call x3, Pallas kernels, scores(): pl.pallas_call(functools.partial(score_kernel, tuple(dists), block), grid...  18.1 us
    pallas_call x3, Pallas kernels, deltas(): pl.pallas_call(kernel, grid=(width // cols,), in_specs=first + ins, out_s...  12.8 us
    pallas_call x2, Pallas kernels, place(): pl.pallas_call(functools.partial(place_kernel, first, len(back), sum((v.s...  11.5 us
    convert_element_type x1, other arithmetic, total_of(): functools.reduce(jnp.add, [v.astype(jnp.float32) for v in parts])  4.63 us
    pallas_call x1, Pallas kernels, packs(): pl.pallas_call(functools.partial(pack_kernel, n_dp, seg_len, shift), in_s...  4.55 us
  transfers between devices with their start and end apart: 19, of which 11 were waited for; matrix products, arithmetic and copies ran while one was open for 5% of the time, Pallas kernels for 41%

profile of v6, /device:TPU:0, one launch (start us, length us, event | category | flops | bytes accessed | tf_op | source)
XLA Modules:
  0.0 155.5 jit_solution(1490288525569491719)
XLA Ops:
  2.2 4.6 %pack.1 = (s32[2,32]{1,0:T(2,128)S(1)}, s32[512,1]{1,0:T(8,128)S(1)}, s32[512,1]{1,0:T(8,128)S(1)}, bf16[512,128]{1,0:T(8,128)(2,1)}, s32[1,1]{1,0:T(1,128)}, /*...) custom-call(s32[1]{0:T(128)} %bitcast.1.me_ref.refs_0_, ...), custom_call_target="tpu_custom_call" | custom-call | tf_op jit(solution)/shard_map/pack/pallas_call | solution.py:336
  6.8 3.0 %collective-permute-start.10 = (bf16[208,2176]{1,0:T(8,128)(2,1)}, bf16[208,2176]{1,0:T(8,128)(2,1)S(1)}, u32[]{:S(2)}, u32[]{:S(2)}) collective-permute-start(bf16[208,2176]{1,0:T(8,128)(2,1)} %get-tuple-element.224), channel_id=1, source_target_pairs={{0,4},{4,0},{8,12},{12,8},{1,5},{5,1},{9,13},{13,9},{2,6},{6,2},{1... | collective-permute-start | bytes 2715656 | tf_op jit(solution)/shard_map/ppermute | solution.py:400
  9.8 2.6 %collective-permute-start.8 = (bf16[136,2176]{1,0:T(8,128)(2,1)}, bf16[136,2176]{1,0:T(8,128)(2,1)S(1)}, u32[]{:S(2)}, u32[]{:S(2)}) collective-permute-start(bf16[136,2176]{1,0:T(8,128)(2,1)} %get-tuple-element.222), channel_id=1, source_target_pairs={{0,8},{4,12},{8,0},{12,4},{1,9},{5,13},{9,1},{13,5},{2,10},{6,14},... | collective-permute-start | bytes 1775624 | tf_op jit(solution)/shard_map/ppermute | solution.py:400
  12.4 5.7 %scores.7 = (f32[64,128]{1,0:T(8,128)S(1)}, s32[1,1]{1,0:T(1,128)}, s32[512,1]{1,0:T(8,128)S(1)}) custom-call(s32[1]{0:T(128)} %bitcast.1.me_ref.refs_0_, s32[512,1]{1,0:T(8,128)S(1)} %get-tuple-element.227.refs_1_, bf16[512,2048]{1,0:T(8,128)(2,1)S(1)} %bitcast.41, bf16[1024,2048]{1,0:T(8,128)(2,1)} %bitcast.34), custom_call_target="tpu_custom_call" | custom-call | tf_op jit(solution)/shard_map/scores/pallas_call | solution.py:91
  18.0 1.7 %collective-permute-start.11 = (f32[64,128]{1,0:T(8,128)S(1)}, f32[64,128]{1,0:T(8,128)S(1)}, u32[]{:S(2)}, u32[]{:S(2)}) collective-permute-start(f32[64,128]{1,0:T(8,128)S(1)} %get-tuple-element.229), channel_id=1, source_target_pairs={{0,2},{1,3},{2,0},{3,1},{4,6},{5,7},{6,4},{7,5},{8,10},{9,11},{10,... | collective-permute-start | bytes 98312 | tf_op jit(solution)/shard_map/ppermute | solution.py:400
  19.8 2.2 %collective-permute-done.11 = f32[64,128]{1,0:T(8,128)S(1)} collective-permute-done((f32[64,128]{1,0:T(8,128)S(1)}, f32[64,128]{1,0:T(8,128)S(1)}, u32[]{:S(2)}, u32[]{:S(2)}) %collective-permute-start.11) | collective-permute-done | bytes 32800 | tf_op jit(solution)/shard_map/ppermute | solution.py:400
  22.0 8.9 %share.4.refs_1_ = bf16[512,2048]{1,0:T(8,128)(2,1)} custom-call(s32[1]{0:T(128)} %bitcast.4.at_ref, bf16[512,2048]{1,0:T(8,128)(2,1)} %bitcast.39, bf16[2048,8192]{1,0:T(8,128)(2,1)} %w_ref.7), custom_call_target="tpu_custom_call" | custom-call | tf_op jit(solution)/shard_map/share/pallas_call | solution.py:354
  30.9 8.1 %share.5 = bf16[512,2048]{1,0:T(8,128)(2,1)} custom-call(s32[1]{0:T(128)S(6)} %xor.22.at_ref, bf16[512,2048]{1,0:T(8,128)(2,1)S(1)} %bitcast.42, bf16[2048,8192]{1,0:T(8,128)(2,1)} %w_ref.7), custom_call_target="tpu_custom_call" | custom-call | tf_op jit(solution)/shard_map/share/pallas_call | solution.py:354
  39.0 8.1 %share.6 = bf16[512,2048]{1,0:T(8,128)(2,1)} custom-call(s32[1]{0:T(128)S(6)} %xor.23.at_ref, bf16[512,2048]{1,0:T(8,128)(2,1)S(1)} %bitcast.43, bf16[2048,8192]{1,0:T(8,128)(2,1)} %w_ref.7), custom_call_target="tpu_custom_call" | custom-call | tf_op jit(solution)/shard_map/share/pallas_call | solution.py:354
  47.1 8.3 %share.7 = bf16[512,2048]{1,0:T(8,128)(2,1)} custom-call(s32[1]{0:T(128)S(6)} %xor.24.at_ref, bf16[512,2048]{1,0:T(8,128)(2,1)S(1)} %bitcast.44, bf16[2048,8192]{1,0:T(8,128)(2,1)} %w_ref.7), custom_call_target="tpu_custom_call" | custom-call | tf_op jit(solution)/shard_map/share/pallas_call | solution.py:354
  56.0 1.8 %collective-permute-done.9.refs_3_ = bf16[136,2176]{1,0:T(8,128)(2,1)S(1)} collective-permute-done((bf16[136,2176]{1,0:T(8,128)(2,1)S(1)}, bf16[136,2176]{1,0:T(8,128)(2,1)S(1)}, u32[]{:S(2)}, u32[]{:S(2)}) %collective-permute-start.9) | collective-permute-done | bytes 591904 | tf_op jit(solution)/shard_map/ppermute | solution.py:400
  57.8 6.7 %scores.8 = (f32[60,128]{1,0:T(8,128)S(1)}, s32[1,1]{1,0:T(1,128)}, s32[136,1]{1,0:T(8,128)S(1)}, s32[136,1]{1,0:T(8,128)S(1)}, s32[208,1]{1,0:T(8,128)S(1)}) custom-call(s32[1]{0:T(128)} %bitcast.1.me_ref.refs_0_, s32[1,1]{1,0:T(1,128)} %get-tuple-element.221.refs_1_, bf16[136,2176]{1,0:T(8,128)(2,1)S(1)} %collective-permute-done.8.refs_2_, ...), custom_call_target="tpu_custom_call" | custom-call | tf_op jit(solution)/shard_map/scores/pallas_call | solution.py:91
  65.0 1.5 collective-permute-start.14
  69.8 6.6 %collective-permute-start.13 = (bf16[128,2176]{1,0:T(8,128)(2,1)}, bf16[128,2176]{1,0:T(8,128)(2,1)}, u32[]{:S(2)}, u32[]{:S(2)}) collective-permute-start(bf16[128,2176]{1,0:T(8,128)(2,1)} %pad_maximum_fusion), channel_id=1, source_target_pairs={{0,4},{4,0},{8,12},{12,8},{1,5},{5,1},{9,13},{13,9},{2,6},{6,2},{1... | collective-permute-start | bytes 1671176 | tf_op jit(solution)/shard_map/ppermute | solution.py:400
  76.5 5.1 %deltas.7 = (bf16[64,2048]{1,0:T(8,128)(2,1)}, bf16[64,2048]{1,0:T(8,128)(2,1)}, bf16[136,2048]{1,0:T(8,128)(2,1)}, bf16[4,72,2048]{2,1,0:T(8,128)(2,1)}) custom-call(s32[1]{0:T(128)} %bitcast.1.me_ref.refs_0_, s32[136,1]{1,0:T(8,128)S(1)} %get-tuple-element.240.refs_0_, s32[136,1]{1,0:T(8,128)S(1)} %get-tuple-element.241.refs_1_, ...), custom_call_target="tpu_custom_call" | custom-call | tf_op jit(solution)/shard_map/deltas/pallas_call | solution.py:167
  81.5 3.8 %all-to-all-start = ((bf16[4,72,2048]{2,1,0:T(8,128)(2,1)}), bf16[4,72,2048]{2,1,0:T(8,128)(2,1)S(1)}, u32[]{:S(2)}, u32[]{:S(2)}) async-start(bf16[4,72,2048]{2,1,0:T(8,128)(2,1)} %get-tuple-element.247), calls=%async_computation | async-start | bytes 2359296 | tf_op jit(solution)/shard_map/all_to_all | solution.py:419
  85.4 4.6 %add_convert_fusion.1 = bf16[512,2048]{1,0:T(8,128)(2,1)} fusion(bf16[512,2048]{1,0:T(8,128)(2,1)} %collective-permute-done.17, bf16[512,2048]{1,0:T(8,128)(2,1)} %share.6), kind=kLoop, calls=%fused_computation.32 | loop fusion | flops 4194304 | bytes 6291456 | tf_op jit(solution)/shard_map/convert_element_type | solution.py:416
  90.3 5.7 %scores.9 = (f32[16,128]{1,0:T(8,128)S(1)}, s32[1,1]{1,0:T(1,128)}, s32[128,1]{1,0:T(8,128)S(1)}) custom-call(s32[1]{0:T(128)} %bitcast.1.me_ref.refs_0_, s32[1,1]{1,0:T(1,128)} %get-tuple-element.233.refs_1_, bf16[128,2176]{1,0:T(8,128)(2,1)} %collective-permute-done.13.refs_2_, bf16[1024,2048]{1,0:T(8,128)(2,1)S(1)} %bitcast.37), custom_call_target="tpu_custom_call" | custom-call | tf_op jit(solution)/shard_map/scores/pallas_call | solution.py:91
  96.0 1.5 collective-permute-start.18
  97.5 2.1 %collective-permute-done.18 = f32[16,128]{1,0:T(8,128)S(1)} collective-permute-done((f32[16,128]{1,0:T(8,128)S(1)}, f32[16,128]{1,0:T(8,128)S(1)}, u32[]{:S(2)}, u32[]{:S(2)}) %collective-permute-start.18) | collective-permute-done | bytes 8224 | tf_op jit(solution)/shard_map/ppermute | solution.py:400
  100.8 1.5 collective-permute-start.24
  102.3 2.8 %deltas.8 = bf16[128,2048]{1,0:T(8,128)(2,1)} custom-call(s32[128,1]{1,0:T(8,128)S(1)} %get-tuple-element.253.refs_0_, f32[16,128]{1,0:T(8,128)S(1)} %add.159.refs_1_, bf16[1024,2048]{1,0:T(8,128)(2,1)S(1)} %bitcast.32), custom_call_target="tpu_custom_call" | custom-call | tf_op jit(solution)/shard_map/deltas/pallas_call | solution.py:167
  105.2 1.9 %collective-permute-start.20 = (bf16[128,2048]{1,0:T(8,128)(2,1)}, bf16[128,2048]{1,0:T(8,128)(2,1)}, u32[]{:S(2)}, u32[]{:S(2)}) collective-permute-start(bf16[128,2048]{1,0:T(8,128)(2,1)} %deltas.8), channel_id=1, source_target_pairs={{0,4},{4,0},{8,12},{12,8},{1,5},{5,1},{9,13},{13,9},{2,6},{6,2},{1... | collective-permute-start | bytes 1572872 | tf_op jit(solution)/shard_map/ppermute | solution.py:400
  107.1 4.9 %deltas.9.refs_3_ = bf16[512,2048]{1,0:T(8,128)(2,1)} custom-call(s32[512,1]{1,0:T(8,128)S(1)} %copy-done.5, f32[64,128]{1,0:T(8,128)S(1)} %copy-done.6, bf16[1024,2048]{1,0:T(8,128)(2,1)S(1)} %bitcast.33), custom_call_target="tpu_custom_call" | custom-call | tf_op jit(solution)/shard_map/deltas/pallas_call | solution.py:167
  112.1 2.5 %all-to-all-done.refs_0_ = bf16[4,72,2048]{2,1,0:T(8,128)(2,1)S(1)} async-done(((bf16[4,72,2048]{2,1,0:T(8,128)(2,1)}), bf16[4,72,2048]{2,1,0:T(8,128)(2,1)S(1)}, u32[]{:S(2)}, u32[]{:S(2)}) %all-to-all-start) | async-done | bytes 1179680 | tf_op jit(solution)/shard_map/all_to_all | solution.py:419
  114.6 1.6 %copy-done.2 = bf16[512,2048]{1,0:T(8,128)(2,1)S(1)} copy-done((bf16[512,2048]{1,0:T(8,128)(2,1)S(1)}, bf16[512,2048]{1,0:T(8,128)(2,1)}, u32[]{:S(2)}) %copy-start.2) | copy-done | bytes 2097176
  116.2 5.7 %place.2.refs_3_ = f32[512,2048]{1,0:T(8,128)} custom-call(s32[1]{0:T(128)} %bitcast.1.me_ref.refs_0_, s32[512,1]{1,0:T(8,128)S(1)} %get-tuple-element.280.row_ref, s32[6,256]{1,0:T(8,128)S(1)} %get-tuple-element.220.codes_ref, bf16[4,72,2048]{2,1,0:T(8,128)(2,1)S(1)} %all-to-all-done.refs_0_, bf16[512,2048]{1,0:T(8,128)(2,1)S(1)} %copy-done, ...), custom_call_target="tpu_custom_call" | custom-call | tf_op jit(solution)/shard_map/place/pallas_call | solution.py:201
  123.8 4.1 %collective-permute-start.21 = (bf16[64,2048]{1,0:T(8,128)(2,1)S(1)}, bf16[64,2048]{1,0:T(8,128)(2,1)S(1)}, u32[]{:S(2)}, u32[]{:S(2)}) collective-permute-start(bf16[64,2048]{1,0:T(8,128)(2,1)S(1)} %get-tuple-element.311), channel_id=1, source_target_pairs={{0,8},{4,12},{8,0},{12,4},{1,9},{5,13},{9,1},{13,5},{2,10},{6,14},... | collective-permute-start | bytes 786440 | tf_op jit(solution)/shard_map/ppermute | solution.py:400
  129.9 2.4 %collective-permute-done.25 = s32[1,1]{1,0:T(1,128)} collective-permute-done((s32[1,1]{1,0:T(1,128)}, s32[1,1]{1,0:T(1,128)}, u32[]{:S(2)}, u32[]{:S(2)}) %collective-permute-start.25) | collective-permute-done | bytes 36 | tf_op jit(solution)/shard_map/ppermute | solution.py:400
  133.4 8.2 %collective-permute-done.21.refs_0_ = bf16[64,2048]{1,0:T(8,128)(2,1)S(1)} collective-permute-done((bf16[64,2048]{1,0:T(8,128)(2,1)S(1)}, bf16[64,2048]{1,0:T(8,128)(2,1)S(1)}, u32[]{:S(2)}, u32[]{:S(2)}) %collective-permute-start.21) | collective-permute-done | bytes 262176 | tf_op jit(solution)/shard_map/ppermute | solution.py:400
  141.6 8.1 %collective-permute-done.22.refs_1_ = bf16[64,2048]{1,0:T(8,128)(2,1)S(1)} collective-permute-done((bf16[64,2048]{1,0:T(8,128)(2,1)S(1)}, bf16[64,2048]{1,0:T(8,128)(2,1)S(1)}, u32[]{:S(2)}, u32[]{:S(2)}) %collective-permute-start.22) | collective-permute-done | bytes 262176 | tf_op jit(solution)/shard_map/ppermute | solution.py:400
  149.7 5.8 %place.3 = bf16[512,2048]{1,0:T(8,128)(2,1)} custom-call(s32[1]{0:T(128)} %bitcast.1.me_ref.refs_0_, s32[512,1]{1,0:T(8,128)S(1)} %get-tuple-element.280.row_ref, s32[6,256]{1,0:T(8,128)S(1)} %get-tuple-element.220.codes_ref, bf16[64,2048]{1,0:T(8,128)(2,1)S(1)} %collective-permute-done.21.refs_0_, bf16[64,2048]{1,0:T(8,128)(2,1)S(1)} %collective-permute-done.22.refs_1_, ...), custom_call_target="tpu_custom_call" | custom-call | tf_op jit(solution)/shard_map/place/pallas_call | solution.py:201
  (68 shorter events, 12.0 us)
Async XLA Ops:
  2.2 10.2 %copy-start.13 = (bf16[4,128,2048]{2,1,0:T(8,128)(2,1)S(1)}, bf16[4,128,2048]{2,1,0:T(8,128)(2,1)}, u32[]{:S(2)}) copy-start(bf16[4,128,2048]{2,1,0:T(8,128)(2,1)} %param.9) | copy-start | bytes 6291460
  6.8 51.0 %collective-permute-start.10 = (bf16[208,2176]{1,0:T(8,128)(2,1)}, bf16[208,2176]{1,0:T(8,128)(2,1)S(1)}, u32[]{:S(2)}, u32[]{:S(2)}) collective-permute-start(bf16[208,2176]{1,0:T(8,128)(2,1)} %get-tuple-element.224), channel_id=1, source_target_pairs={{0,4},{4,0},{8,12},{12,8},{1,5},{5,1},{9,13},{13,9},{2,6},{6,2},{1... | collective-permute-start | bytes 2715656 | tf_op jit(solution)/shard_map/ppermute | solution.py:400
  9.8 46.2 %collective-permute-start.8 = (bf16[136,2176]{1,0:T(8,128)(2,1)}, bf16[136,2176]{1,0:T(8,128)(2,1)S(1)}, u32[]{:S(2)}, u32[]{:S(2)}) collective-permute-start(bf16[136,2176]{1,0:T(8,128)(2,1)} %get-tuple-element.222), channel_id=1, source_target_pairs={{0,8},{4,12},{8,0},{12,4},{1,9},{5,13},{9,1},{13,5},{2,10},{6,14},... | collective-permute-start | bytes 1775624 | tf_op jit(solution)/shard_map/ppermute | solution.py:400
  12.4 45.4 %collective-permute-start.9 = (bf16[136,2176]{1,0:T(8,128)(2,1)S(1)}, bf16[136,2176]{1,0:T(8,128)(2,1)S(1)}, u32[]{:S(2)}, u32[]{:S(2)}) collective-permute-start(bf16[136,2176]{1,0:T(8,128)(2,1)S(1)} %get-tuple-element.223), channel_id=1, source_target_pairs={{0,12},{4,8},{8,4},{12,0},{1,13},{5,9},{9,5},{13,1},{2,14},{6,10},... | collective-permute-start | bytes 1775624 | tf_op jit(solution)/shard_map/ppermute | solution.py:400
  18.0 12.8 %copy-start.4 = (s32[512,1]{1,0:T(8,128)}, s32[512,1]{1,0:T(8,128)S(1)}, u32[]{:S(2)}) copy-start(s32[512,1]{1,0:T(8,128)S(1)} %get-tuple-element.261.refs_0_) | copy-start | bytes 6148
  18.0 3.9 %collective-permute-start.11 = (f32[64,128]{1,0:T(8,128)S(1)}, f32[64,128]{1,0:T(8,128)S(1)}, u32[]{:S(2)}, u32[]{:S(2)}) collective-permute-start(f32[64,128]{1,0:T(8,128)S(1)} %get-tuple-element.229), channel_id=1, source_target_pairs={{0,2},{1,3},{2,0},{3,1},{4,6},{5,7},{6,4},{7,5},{8,10},{9,11},{10,... | collective-permute-start | bytes 98312 | tf_op jit(solution)/shard_map/ppermute | solution.py:400
  22.0 33.4 %collective-permute-start.12 = (f32[64,128]{1,0:T(8,128)S(1)}, f32[64,128]{1,0:T(8,128)S(1)}, u32[]{:S(2)}, u32[]{:S(2)}) collective-permute-start(f32[64,128]{1,0:T(8,128)S(1)} %add.153), channel_id=1, source_target_pairs={{0,1},{1,0},{2,3},{3,2},{4,5},{5,4},{6,7},{7,6},{8,9},{9,8},{10,11... | collective-permute-start | bytes 98312 | tf_op jit(solution)/shard_map/ppermute | solution.py:400
  22.0 8.9 %copy-start.14 = (bf16[4,128,2048]{2,1,0:T(8,128)(2,1)S(1)}, bf16[4,128,2048]{2,1,0:T(8,128)(2,1)}, u32[]{:S(2)}) copy-start(bf16[4,128,2048]{2,1,0:T(8,128)(2,1)} %param.9) | copy-start | bytes 6291460
  47.1 10.6 %copy-start.11 = (bf16[64,16,2048]{2,1,0:T(8,128)(2,1)S(1)}, bf16[64,16,2048]{2,1,0:T(8,128)(2,1)}, u32[]{:S(2)}) copy-start(bf16[64,16,2048]{2,1,0:T(8,128)(2,1)} %param.11) | copy-start | bytes 12582916
  57.7 6.7 %copy-start.3 = (bf16[136,2176]{1,0:T(8,128)(2,1)}, bf16[136,2176]{1,0:T(8,128)(2,1)S(1)}, u32[]{:S(2)}) copy-start(bf16[136,2176]{1,0:T(8,128)(2,1)S(1)} %collective-permute-done.9.refs_3_) | copy-start | bytes 1775620
  57.8 18.7 %copy-start.8 = (bf16[64,16,2048]{2,1,0:T(8,128)(2,1)S(1)}, bf16[64,16,2048]{2,1,0:T(8,128)(2,1)}, u32[]{:S(2)}) copy-start(bf16[64,16,2048]{2,1,0:T(8,128)(2,1)} %param.12) | copy-start | bytes 12582916
  64.5 20.9 %collective-permute-start.17 = (bf16[512,2048]{1,0:T(8,128)(2,1)}, bf16[512,2048]{1,0:T(8,128)(2,1)}, u32[]{:S(2)}, u32[]{:S(2)}) collective-permute-start(bf16[512,2048]{1,0:T(8,128)(2,1)} %share.7), channel_id=1, source_target_pairs={{0,1},{1,0},{2,3},{3,2},{4,5},{5,4},{6,7},{7,6},{8,9},{9,8},{10,11... | collective-permute-start | bytes 6291464 | tf_op jit(solution)/shard_map/ppermute | solution.py:400
  64.5 25.8 %collective-permute-start.16 = (bf16[512,2048]{1,0:T(8,128)(2,1)}, bf16[512,2048]{1,0:T(8,128)(2,1)S(1)}, u32[]{:S(2)}, u32[]{:S(2)}) collective-permute-start(bf16[512,2048]{1,0:T(8,128)(2,1)} %share.5), channel_id=1, source_target_pairs={{0,1},{1,0},{2,3},{3,2},{4,5},{5,4},{6,7},{7,6},{8,9},{9,8},{10,11... | collective-permute-start | bytes 6291464 | tf_op jit(solution)/shard_map/ppermute | solution.py:400
  65.0 3.9 %collective-permute-start.14 = (f32[60,128]{1,0:T(8,128)S(1)}, f32[60,128]{1,0:T(8,128)S(1)}, u32[]{:S(2)}, u32[]{:S(2)}) collective-permute-start(f32[60,128]{1,0:T(8,128)S(1)} %get-tuple-element.243), channel_id=1, source_target_pairs={{0,2},{1,3},{2,0},{3,1},{4,6},{5,7},{6,4},{7,5},{8,10},{9,11},{10,... | collective-permute-start | bytes 92168 | tf_op jit(solution)/shard_map/ppermute | solution.py:400
  68.9 7.5 %collective-permute-start.15 = (f32[60,128]{1,0:T(8,128)S(1)}, f32[60,128]{1,0:T(8,128)S(1)}, u32[]{:S(2)}, u32[]{:S(2)}) collective-permute-start(f32[60,128]{1,0:T(8,128)S(1)} %add.155), channel_id=1, source_target_pairs={{0,1},{1,0},{2,3},{3,2},{4,5},{5,4},{6,7},{7,6},{8,9},{9,8},{10,11... | collective-permute-start | bytes 92168 | tf_op jit(solution)/shard_map/ppermute | solution.py:400
  69.8 20.4 %collective-permute-start.13 = (bf16[128,2176]{1,0:T(8,128)(2,1)}, bf16[128,2176]{1,0:T(8,128)(2,1)}, u32[]{:S(2)}, u32[]{:S(2)}) collective-permute-start(bf16[128,2176]{1,0:T(8,128)(2,1)} %pad_maximum_fusion), channel_id=1, source_target_pairs={{0,4},{4,0},{8,12},{12,8},{1,5},{5,1},{9,13},{13,9},{2,6},{6,2},{1... | collective-permute-start | bytes 1671176 | tf_op jit(solution)/shard_map/ppermute | solution.py:400
  81.5 33.1 %all-to-all-start = ((bf16[4,72,2048]{2,1,0:T(8,128)(2,1)}), bf16[4,72,2048]{2,1,0:T(8,128)(2,1)S(1)}, u32[]{:S(2)}, u32[]{:S(2)}) async-start(bf16[4,72,2048]{2,1,0:T(8,128)(2,1)} %get-tuple-element.247), calls=%async_computation | async-start | bytes 2359296 | tf_op jit(solution)/shard_map/all_to_all | solution.py:419
  85.4 4.9 %copy-start.12 = (bf16[64,16,2048]{2,1,0:T(8,128)(2,1)S(1)}, bf16[64,16,2048]{2,1,0:T(8,128)(2,1)}, u32[]{:S(2)}) copy-start(bf16[64,16,2048]{2,1,0:T(8,128)(2,1)} %param.11) | copy-start | bytes 12582916
  90.2 5.7 %copy-start.1 = (bf16[512,2048]{1,0:T(8,128)(2,1)}, bf16[512,2048]{1,0:T(8,128)(2,1)S(1)}, u32[]{:S(2)}) copy-start(bf16[512,2048]{1,0:T(8,128)(2,1)S(1)} %collective-permute-done.16.refs_2_) | copy-start | bytes 6291460
  90.2 12.1 %copy-start.9 = (bf16[64,16,2048]{2,1,0:T(8,128)(2,1)S(1)}, bf16[64,16,2048]{2,1,0:T(8,128)(2,1)}, u32[]{:S(2)}) copy-start(bf16[64,16,2048]{2,1,0:T(8,128)(2,1)} %param.12) | copy-start | bytes 12582916
  96.0 3.7 %collective-permute-start.18 = (f32[16,128]{1,0:T(8,128)S(1)}, f32[16,128]{1,0:T(8,128)S(1)}, u32[]{:S(2)}, u32[]{:S(2)}) collective-permute-start(f32[16,128]{1,0:T(8,128)S(1)} %get-tuple-element.254), channel_id=1, source_target_pairs={{0,2},{1,3},{2,0},{3,1},{4,6},{5,7},{6,4},{7,5},{8,10},{9,11},{10,... | collective-permute-start | bytes 24584 | tf_op jit(solution)/shard_map/ppermute | solution.py:400
  99.6 1.2 collective-permute-start.19
  100.8 48.9 %collective-permute-start.24 = (bf16[512,2048]{1,0:T(8,128)(2,1)}, bf16[512,2048]{1,0:T(8,128)(2,1)}, u32[]{:S(2)}, u32[]{:S(2)}) collective-permute-start(bf16[512,2048]{1,0:T(8,128)(2,1)} %add_convert_fusion.1), channel_id=1, source_target_pairs={{0,2},{1,3},{2,0},{3,1},{4,6},{5,7},{6,4},{7,5},{8,10},{9,11},{10,... | collective-permute-start | bytes 6291464 | tf_op jit(solution)/shard_map/ppermute | solution.py:400
  105.2 17.5 %collective-permute-start.20 = (bf16[128,2048]{1,0:T(8,128)(2,1)}, bf16[128,2048]{1,0:T(8,128)(2,1)}, u32[]{:S(2)}, u32[]{:S(2)}) collective-permute-start(bf16[128,2048]{1,0:T(8,128)(2,1)} %deltas.8), channel_id=1, source_target_pairs={{0,4},{4,0},{8,12},{12,8},{1,5},{5,1},{9,13},{13,9},{2,6},{6,2},{1... | collective-permute-start | bytes 1572872 | tf_op jit(solution)/shard_map/ppermute | solution.py:400
  107.1 7.5 %copy-start = (bf16[512,2048]{1,0:T(8,128)(2,1)S(1)}, bf16[512,2048]{1,0:T(8,128)(2,1)}, u32[]{:S(2)}) copy-start(bf16[512,2048]{1,0:T(8,128)(2,1)} %share.4.refs_1_) | copy-start | bytes 6291460
  116.2 6.5 %copy-start.19 = (bf16[64,2048]{1,0:T(8,128)(2,1)S(1)}, bf16[64,2048]{1,0:T(8,128)(2,1)}, u32[]{:S(2)}) copy-start(bf16[64,2048]{1,0:T(8,128)(2,1)} %get-tuple-element.266) | copy-start | bytes 786436
  116.2 6.5 %copy-start.20 = (bf16[64,2048]{1,0:T(8,128)(2,1)S(1)}, bf16[64,2048]{1,0:T(8,128)(2,1)}, u32[]{:S(2)}) copy-start(bf16[64,2048]{1,0:T(8,128)(2,1)} %get-tuple-element.268) | copy-start | bytes 786436
  122.7 27.0 %collective-permute-start.23 = (bf16[136,2048]{1,0:T(8,128)(2,1)}, bf16[136,2048]{1,0:T(8,128)(2,1)S(1)}, u32[]{:S(2)}, u32[]{:S(2)}) collective-permute-start(bf16[136,2048]{1,0:T(8,128)(2,1)} %get-tuple-element.269), channel_id=1, source_target_pairs={{0,4},{4,0},{8,12},{12,8},{1,5},{5,1},{9,13},{13,9},{2,6},{6,2},{1... | collective-permute-start | bytes 1671176 | tf_op jit(solution)/shard_map/ppermute | solution.py:400
  123.8 17.8 %collective-permute-start.21 = (bf16[64,2048]{1,0:T(8,128)(2,1)S(1)}, bf16[64,2048]{1,0:T(8,128)(2,1)S(1)}, u32[]{:S(2)}, u32[]{:S(2)}) collective-permute-start(bf16[64,2048]{1,0:T(8,128)(2,1)S(1)} %get-tuple-element.311), channel_id=1, source_target_pairs={{0,8},{4,12},{8,0},{12,4},{1,9},{5,13},{9,1},{13,5},{2,10},{6,14},... | collective-permute-start | bytes 786440 | tf_op jit(solution)/shard_map/ppermute | solution.py:400
  127.9 21.8 %collective-permute-start.22 = (bf16[64,2048]{1,0:T(8,128)(2,1)S(1)}, bf16[64,2048]{1,0:T(8,128)(2,1)S(1)}, u32[]{:S(2)}, u32[]{:S(2)}) collective-permute-start(bf16[64,2048]{1,0:T(8,128)(2,1)S(1)} %get-tuple-element.310), channel_id=1, source_target_pairs={{0,12},{4,8},{8,4},{12,0},{1,13},{5,9},{9,5},{13,1},{2,14},{6,10},... | collective-permute-start | bytes 786440 | tf_op jit(solution)/shard_map/ppermute | solution.py:400
  128.3 3.9 %collective-permute-start.25 = (s32[1,1]{1,0:T(1,128)}, s32[1,1]{1,0:T(1,128)}, u32[]{:S(2)}, u32[]{:S(2)}) collective-permute-start(s32[1,1]{1,0:T(1,128)} %get-tuple-element.233.refs_1_), channel_id=1, source_target_pairs={{0,16},{16,0},{1,17},{17,1},{2,18},{18,2},{3,19},{19,3},{4,20},{20... | collective-permute-start | bytes 20 | tf_op jit(solution)/shard_map/ppermute | solution.py:400
  133.4 22.1 %copy-start.17 = (bf16[512,128]{1,0:T(8,128)(2,1)S(1)}, bf16[512,128]{1,0:T(8,128)(2,1)}, u32[]{:S(2)}) copy-start(bf16[512,128]{1,0:T(8,128)(2,1)} %get-tuple-element.413) | copy-start | bytes 393220
  (4 other events, 11.9 us)

commit v7 on v6

--- a/solution.py
+++ b/solution.py
@@ -467,8 +467,9 @@
         for k in sorted((k for k in adds if k & bit), reverse=True):
             adds[k ^ bit].append(swap(total_of(adds.pop(k)), "tp", bit))
         bit *= 2
+    near = after(direct[m], block)
     some = place(me, row_code, codes, m + 1, [], [block], some + [self_delta], jnp.float32)
-    relayed, some, near, direct = lax.optimization_barrier((relayed, some, direct[m], direct))
+    relayed, some, direct = lax.optimization_barrier((relayed, some, direct))
     back = [swap(direct[i] + relayed[i * SHARED:(i + 1) * SHARED], "dp", j) for i, j in enumerate(far)]
     back.append(swap(near, "dp", 1))
     rounds = butterfly(rounds, "rep", jnp.maximum)[0, 0]

time: 156 us -> 160 us (1.026); the launches traced: 156 us -> 157 us
    all_to_all x1, waiting for transfers between devices: 2.54 us -> 8.21 us  [a2a(): return lax.all_to_all(v, 'dp', split_axis=0, concat_axis=0, tiled=True)]
    ppermute x18, waiting for transfers between devices: 28.3 us -> 23.6 us  [swap(): return lax.ppermute(v, axis, [(i, i ^ k) for i in range(n)])]
    pallas_call x3, Pallas kernels: 12.8 us -> 14.6 us  [deltas(): pl.pallas_call(kernel, grid=(width // cols,), in_specs=first + ins, out_s...]
  transfers between devices with their start and end apart: 19 -> 19, of which waited for: 11 -> 9; matrix products, arithmetic and copies ran while one was open for 5% -> 5% of each run, Pallas kernels for 41% -> 41%
where the time goes in v7:
time: 160 us; the launch traced here: 157 us
  Pallas kernels  81.5 us (51%)
  waiting for transfers between devices  31.8 us (20%)
  starting transfers between devices  30.9 us (19%)
  other arithmetic  7.26 us (5%)
  local copies, waits for them, and re-layouts  4.11 us (3%)
    pallas_call x4, Pallas kernels, share(): pl.pallas_call(share_kernel, grid_spec=pltpu.PrefetchScalarGridSpec(num_s...  33.5 us
    ppermute x18, starting transfers between devices, swap(): return lax.ppermute(v, axis, [(i, i ^ k) for i in range(n)])  27 us
    ppermute x18, waiting for transfers between devices, swap(): return lax.ppermute(v, axis, [(i, i ^ k) for i in range(n)])  23.6 us
    pallas_call x3, Pallas kernels, scores(): pl.pallas_call(functools.partial(score_kernel, tuple(dists), block), grid...  17.3 us
    pallas_call x3, Pallas kernels, deltas(): pl.pallas_call(kernel, grid=(width // cols,), in_specs=first + ins, out_s...  14.6 us
    pallas_call x2, Pallas kernels, place(): pl.pallas_call(functools.partial(place_kernel, first, len(back), sum((v.s...  11.6 us
    all_to_all x1, waiting for transfers between devices, a2a(): return lax.all_to_all(v, 'dp', split_axis=0, concat_axis=0, tiled=True)  8.21 us
    convert_element_type x1, other arithmetic, total_of(): functools.reduce(jnp.add, [v.astype(jnp.float32) for v in parts])  4.68 us
  transfers between devices with their start and end apart: 19, of which 9 were waited for; matrix products, arithmetic and copies ran while one was open for 5% of the time, Pallas kernels for 41%

profile of v7, /device:TPU:0, one launch (start us, length us, event | category | flops | bytes accessed | tf_op | source)
XLA Modules:
  0.0 157.1 jit_solution(3621249393575946734)
XLA Ops:
  2.2 4.6 %pack.1 = (s32[2,32]{1,0:T(2,128)}, s32[512,1]{1,0:T(8,128)S(1)}, s32[512,1]{1,0:T(8,128)S(1)}, bf16[512,128]{1,0:T(8,128)(2,1)}, s32[1,1]{1,0:T(1,128)}, /*inde...) custom-call(s32[1]{0:T(128)} %bitcast.1.me_ref.refs_0_, ...), custom_call_target="tpu_custom_call" | custom-call | tf_op jit(solution)/shard_map/pack/pallas_call | solution.py:336
  6.8 3.0 %collective-permute-start.10 = (bf16[208,2176]{1,0:T(8,128)(2,1)}, bf16[208,2176]{1,0:T(8,128)(2,1)S(1)}, u32[]{:S(2)}, u32[]{:S(2)}) collective-permute-start(bf16[208,2176]{1,0:T(8,128)(2,1)} %get-tuple-element.224), channel_id=1, source_target_pairs={{0,4},{4,0},{8,12},{12,8},{1,5},{5,1},{9,13},{13,9},{2,6},{6,2},{1... | collective-permute-start | bytes 2715656 | tf_op jit(solution)/shard_map/ppermute | solution.py:400
  9.8 2.6 %collective-permute-start.8 = (bf16[136,2176]{1,0:T(8,128)(2,1)}, bf16[136,2176]{1,0:T(8,128)(2,1)S(1)}, u32[]{:S(2)}, u32[]{:S(2)}) collective-permute-start(bf16[136,2176]{1,0:T(8,128)(2,1)} %get-tuple-element.222), channel_id=1, source_target_pairs={{0,8},{4,12},{8,0},{12,4},{1,9},{5,13},{9,1},{13,5},{2,10},{6,14},... | collective-permute-start | bytes 1775624 | tf_op jit(solution)/shard_map/ppermute | solution.py:400
  12.4 5.7 %scores.7 = (f32[64,128]{1,0:T(8,128)S(1)}, s32[1,1]{1,0:T(1,128)}, s32[512,1]{1,0:T(8,128)S(1)}) custom-call(s32[1]{0:T(128)} %bitcast.1.me_ref.refs_0_, s32[512,1]{1,0:T(8,128)S(1)} %get-tuple-element.227.refs_1_, bf16[512,2048]{1,0:T(8,128)(2,1)S(1)} %bitcast.41, bf16[1024,2048]{1,0:T(8,128)(2,1)} %bitcast.34), custom_call_target="tpu_custom_call" | custom-call | tf_op jit(solution)/shard_map/scores/pallas_call | solution.py:91
  18.1 1.7 %collective-permute-start.11 = (f32[64,128]{1,0:T(8,128)S(1)}, f32[64,128]{1,0:T(8,128)S(1)}, u32[]{:S(2)}, u32[]{:S(2)}) collective-permute-start(f32[64,128]{1,0:T(8,128)S(1)} %get-tuple-element.229), channel_id=1, source_target_pairs={{0,2},{1,3},{2,0},{3,1},{4,6},{5,7},{6,4},{7,5},{8,10},{9,11},{10,... | collective-permute-start | bytes 98312 | tf_op jit(solution)/shard_map/ppermute | solution.py:400
  19.8 2.2 %collective-permute-done.11 = f32[64,128]{1,0:T(8,128)S(1)} collective-permute-done((f32[64,128]{1,0:T(8,128)S(1)}, f32[64,128]{1,0:T(8,128)S(1)}, u32[]{:S(2)}, u32[]{:S(2)}) %collective-permute-start.11) | collective-permute-done | bytes 32800 | tf_op jit(solution)/shard_map/ppermute | solution.py:400
  22.0 8.9 %share.4.refs_1_ = bf16[512,2048]{1,0:T(8,128)(2,1)} custom-call(s32[1]{0:T(128)} %bitcast.4.at_ref, bf16[512,2048]{1,0:T(8,128)(2,1)} %bitcast.39, bf16[2048,8192]{1,0:T(8,128)(2,1)} %w_ref.7), custom_call_target="tpu_custom_call" | custom-call | tf_op jit(solution)/shard_map/share/pallas_call | solution.py:354
  30.9 8.1 %share.5 = bf16[512,2048]{1,0:T(8,128)(2,1)} custom-call(s32[1]{0:T(128)S(6)} %xor.22.at_ref, bf16[512,2048]{1,0:T(8,128)(2,1)S(1)} %bitcast.42, bf16[2048,8192]{1,0:T(8,128)(2,1)} %w_ref.7), custom_call_target="tpu_custom_call" | custom-call | tf_op jit(solution)/shard_map/share/pallas_call | solution.py:354
  39.0 8.2 %share.6 = bf16[512,2048]{1,0:T(8,128)(2,1)} custom-call(s32[1]{0:T(128)S(6)} %xor.23.at_ref, bf16[512,2048]{1,0:T(8,128)(2,1)S(1)} %bitcast.43, bf16[2048,8192]{1,0:T(8,128)(2,1)} %w_ref.7), custom_call_target="tpu_custom_call" | custom-call | tf_op jit(solution)/shard_map/share/pallas_call | solution.py:354
  47.2 8.3 %share.7 = bf16[512,2048]{1,0:T(8,128)(2,1)} custom-call(s32[1]{0:T(128)S(6)} %xor.24.at_ref, bf16[512,2048]{1,0:T(8,128)(2,1)S(1)} %bitcast.44, bf16[2048,8192]{1,0:T(8,128)(2,1)} %w_ref.7), custom_call_target="tpu_custom_call" | custom-call | tf_op jit(solution)/shard_map/share/pallas_call | solution.py:354
  56.1 1.6 %collective-permute-done.9.refs_3_ = bf16[136,2176]{1,0:T(8,128)(2,1)S(1)} collective-permute-done((bf16[136,2176]{1,0:T(8,128)(2,1)S(1)}, bf16[136,2176]{1,0:T(8,128)(2,1)S(1)}, u32[]{:S(2)}, u32[]{:S(2)}) %collective-permute-start.9) | collective-permute-done | bytes 591904 | tf_op jit(solution)/shard_map/ppermute | solution.py:400
  57.8 6.7 %scores.8 = (f32[60,128]{1,0:T(8,128)S(1)}, s32[1,1]{1,0:T(1,128)}, s32[136,1]{1,0:T(8,128)S(1)}, s32[136,1]{1,0:T(8,128)S(1)}, s32[208,1]{1,0:T(8,128)S(1)}) custom-call(s32[1]{0:T(128)} %bitcast.1.me_ref.refs_0_, s32[1,1]{1,0:T(1,128)} %get-tuple-element.221.refs_1_, bf16[136,2176]{1,0:T(8,128)(2,1)S(1)} %collective-permute-done.8.refs_2_, ...), custom_call_target="tpu_custom_call" | custom-call | tf_op jit(solution)/shard_map/scores/pallas_call | solution.py:91
  64.9 1.5 collective-permute-start.14
  66.5 2.3 %collective-permute-done.14 = f32[60,128]{1,0:T(8,128)S(1)} collective-permute-done((f32[60,128]{1,0:T(8,128)S(1)}, f32[60,128]{1,0:T(8,128)S(1)}, u32[]{:S(2)}, u32[]{:S(2)}) %collective-permute-start.14) | collective-permute-done | bytes 30752 | tf_op jit(solution)/shard_map/ppermute | solution.py:400
  69.7 6.7 %collective-permute-start.13 = (bf16[128,2176]{1,0:T(8,128)(2,1)}, bf16[128,2176]{1,0:T(8,128)(2,1)}, u32[]{:S(2)}, u32[]{:S(2)}) collective-permute-start(bf16[128,2176]{1,0:T(8,128)(2,1)} %pad_maximum_fusion), channel_id=1, source_target_pairs={{0,4},{4,0},{8,12},{12,8},{1,5},{5,1},{9,13},{13,9},{2,6},{6,2},{1... | collective-permute-start | bytes 1671176 | tf_op jit(solution)/shard_map/ppermute | solution.py:400
  76.4 5.0 %deltas.7 = (bf16[64,2048]{1,0:T(8,128)(2,1)}, bf16[64,2048]{1,0:T(8,128)(2,1)}, bf16[136,2048]{1,0:T(8,128)(2,1)}, bf16[4,72,2048]{2,1,0:T(8,128)(2,1)}) custom-call(s32[1]{0:T(128)} %bitcast.1.me_ref.refs_0_, s32[136,1]{1,0:T(8,128)S(1)} %get-tuple-element.240.refs_0_, s32[136,1]{1,0:T(8,128)S(1)} %get-tuple-element.241.refs_1_, ...), custom_call_target="tpu_custom_call" | custom-call | tf_op jit(solution)/shard_map/deltas/pallas_call | solution.py:167
  81.4 3.9 %all-to-all-start = ((bf16[4,72,2048]{2,1,0:T(8,128)(2,1)}), bf16[4,72,2048]{2,1,0:T(8,128)(2,1)S(1)}, u32[]{:S(2)}, u32[]{:S(2)}) async-start(bf16[4,72,2048]{2,1,0:T(8,128)(2,1)} %get-tuple-element.247), calls=%async_computation | async-start | bytes 2359296 | tf_op jit(solution)/shard_map/all_to_all | solution.py:419
  85.3 4.7 %add_convert_fusion.1 = bf16[512,2048]{1,0:T(8,128)(2,1)} fusion(bf16[512,2048]{1,0:T(8,128)(2,1)} %collective-permute-done.17, bf16[512,2048]{1,0:T(8,128)(2,1)} %share.6), kind=kLoop, calls=%fused_computation.32 | loop fusion | flops 4194304 | bytes 6291456 | tf_op jit(solution)/shard_map/convert_element_type | solution.py:416
  90.2 5.0 %scores.9 = (f32[16,128]{1,0:T(8,128)S(1)}, s32[1,1]{1,0:T(1,128)}, s32[128,1]{1,0:T(8,128)S(1)}) custom-call(s32[1]{0:T(128)} %bitcast.1.me_ref.refs_0_, s32[1,1]{1,0:T(1,128)} %get-tuple-element.233.refs_1_, bf16[128,2176]{1,0:T(8,128)(2,1)} %collective-permute-done.13.refs_2_, bf16[1024,2048]{1,0:T(8,128)(2,1)S(1)} %bitcast.37), custom_call_target="tpu_custom_call" | custom-call | tf_op jit(solution)/shard_map/scores/pallas_call | solution.py:91
  95.2 1.5 collective-permute-start.18
  96.7 2.1 %collective-permute-done.18 = f32[16,128]{1,0:T(8,128)S(1)} collective-permute-done((f32[16,128]{1,0:T(8,128)S(1)}, f32[16,128]{1,0:T(8,128)S(1)}, u32[]{:S(2)}, u32[]{:S(2)}) %collective-permute-start.18) | collective-permute-done | bytes 8224 | tf_op jit(solution)/shard_map/ppermute | solution.py:400
  101.5 2.9 %deltas.8 = bf16[128,2048]{1,0:T(8,128)(2,1)} custom-call(s32[128,1]{1,0:T(8,128)S(1)} %get-tuple-element.253.refs_0_, f32[16,128]{1,0:T(8,128)S(1)} %add.159.refs_1_, bf16[1024,2048]{1,0:T(8,128)(2,1)S(1)} %bitcast.33), custom_call_target="tpu_custom_call" | custom-call | tf_op jit(solution)/shard_map/deltas/pallas_call | solution.py:167
  104.4 1.9 %collective-permute-start.20 = (bf16[128,2048]{1,0:T(8,128)(2,1)}, bf16[128,2048]{1,0:T(8,128)(2,1)}, u32[]{:S(2)}, u32[]{:S(2)}) collective-permute-start(bf16[128,2048]{1,0:T(8,128)(2,1)} %deltas.8), channel_id=1, source_target_pairs={{0,4},{4,0},{8,12},{12,8},{1,5},{5,1},{9,13},{13,9},{2,6},{6,2},{1... | collective-permute-start | bytes 1572872 | tf_op jit(solution)/shard_map/ppermute | solution.py:400
  106.3 8.2 %all-to-all-done.refs_0_ = bf16[4,72,2048]{2,1,0:T(8,128)(2,1)S(1)} async-done(((bf16[4,72,2048]{2,1,0:T(8,128)(2,1)}), bf16[4,72,2048]{2,1,0:T(8,128)(2,1)S(1)}, u32[]{:S(2)}, u32[]{:S(2)}) %all-to-all-start) | async-done | bytes 1179680 | tf_op jit(solution)/shard_map/all_to_all | solution.py:419
  116.2 6.7 %deltas.9.refs_3_ = bf16[512,2048]{1,0:T(8,128)(2,1)} custom-call(s32[512,1]{1,0:T(8,128)S(1)} %copy-done.2, f32[64,128]{1,0:T(8,128)S(1)} %copy-done.3, bf16[1024,2048]{1,0:T(8,128)(2,1)} %bitcast.30), custom_call_target="tpu_custom_call" | custom-call | tf_op jit(solution)/shard_map/deltas/pallas_call | solution.py:167
  122.9 5.7 %place.2.refs_3_ = f32[512,2048]{1,0:T(8,128)} custom-call(s32[1]{0:T(128)} %bitcast.1.me_ref.refs_0_, s32[512,1]{1,0:T(8,128)S(1)} %get-tuple-element.280.row_ref, s32[6,256]{1,0:T(8,128)S(1)} %get-tuple-element.220.codes_ref, bf16[4,72,2048]{2,1,0:T(8,128)(2,1)S(1)} %all-to-all-done.refs_0_, bf16[512,2048]{1,0:T(8,128)(2,1)S(1)} %copy-done, ...), custom_call_target="tpu_custom_call" | custom-call | tf_op jit(solution)/shard_map/place/pallas_call | solution.py:201
  129.8 2.0 %collective-permute-start.21 = (bf16[64,2048]{1,0:T(8,128)(2,1)S(1)}, bf16[64,2048]{1,0:T(8,128)(2,1)S(1)}, u32[]{:S(2)}, u32[]{:S(2)}) collective-permute-start(bf16[64,2048]{1,0:T(8,128)(2,1)S(1)} %get-tuple-element.311), channel_id=1, source_target_pairs={{0,8},{4,12},{8,0},{12,4},{1,9},{5,13},{9,1},{13,5},{2,10},{6,14},... | collective-permute-start | bytes 786440 | tf_op jit(solution)/shard_map/ppermute | solution.py:400
  131.8 2.4 %collective-permute-start.22 = (bf16[64,2048]{1,0:T(8,128)(2,1)S(1)}, bf16[64,2048]{1,0:T(8,128)(2,1)S(1)}, u32[]{:S(2)}, u32[]{:S(2)}) collective-permute-start(bf16[64,2048]{1,0:T(8,128)(2,1)S(1)} %get-tuple-element.310), channel_id=1, source_target_pairs={{0,12},{4,8},{8,4},{12,0},{1,13},{5,9},{9,5},{13,1},{2,14},{6,10},... | collective-permute-start | bytes 786440 | tf_op jit(solution)/shard_map/ppermute | solution.py:400
  134.3 1.5 collective-permute-start.25
  135.8 2.2 %collective-permute-done.25 = s32[1,1]{1,0:T(1,128)} collective-permute-done((s32[1,1]{1,0:T(1,128)}, s32[1,1]{1,0:T(1,128)}, u32[]{:S(2)}, u32[]{:S(2)}) %collective-permute-start.25) | collective-permute-done | bytes 36 | tf_op jit(solution)/shard_map/ppermute | solution.py:400
  139.3 11.7 %collective-permute-done.21.refs_0_ = bf16[64,2048]{1,0:T(8,128)(2,1)S(1)} collective-permute-done((bf16[64,2048]{1,0:T(8,128)(2,1)S(1)}, bf16[64,2048]{1,0:T(8,128)(2,1)S(1)}, u32[]{:S(2)}, u32[]{:S(2)}) %collective-permute-start.21) | collective-permute-done | bytes 262176 | tf_op jit(solution)/shard_map/ppermute | solution.py:400
  151.0 5.9 %place.3 = bf16[512,2048]{1,0:T(8,128)(2,1)} custom-call(s32[1]{0:T(128)} %bitcast.1.me_ref.refs_0_, s32[512,1]{1,0:T(8,128)S(1)} %get-tuple-element.280.row_ref, s32[6,256]{1,0:T(8,128)S(1)} %get-tuple-element.220.codes_ref, bf16[64,2048]{1,0:T(8,128)(2,1)S(1)} %collective-permute-done.21.refs_0_, bf16[64,2048]{1,0:T(8,128)(2,1)S(1)} %collective-permute-done.22.refs_1_, ...), custom_call_target="tpu_custom_call" | custom-call | tf_op jit(solution)/shard_map/place/pallas_call | solution.py:201
  (64 shorter events, 10.1 us)
Async XLA Ops:
  2.2 10.2 %copy-start.10 = (bf16[4,128,2048]{2,1,0:T(8,128)(2,1)S(1)}, bf16[4,128,2048]{2,1,0:T(8,128)(2,1)}, u32[]{:S(2)}) copy-start(bf16[4,128,2048]{2,1,0:T(8,128)(2,1)} %param.9) | copy-start | bytes 6291460
  6.8 51.0 %collective-permute-start.10 = (bf16[208,2176]{1,0:T(8,128)(2,1)}, bf16[208,2176]{1,0:T(8,128)(2,1)S(1)}, u32[]{:S(2)}, u32[]{:S(2)}) collective-permute-start(bf16[208,2176]{1,0:T(8,128)(2,1)} %get-tuple-element.224), channel_id=1, source_target_pairs={{0,4},{4,0},{8,12},{12,8},{1,5},{5,1},{9,13},{13,9},{2,6},{6,2},{1... | collective-permute-start | bytes 2715656 | tf_op jit(solution)/shard_map/ppermute | solution.py:400
  9.8 46.3 %collective-permute-start.8 = (bf16[136,2176]{1,0:T(8,128)(2,1)}, bf16[136,2176]{1,0:T(8,128)(2,1)S(1)}, u32[]{:S(2)}, u32[]{:S(2)}) collective-permute-start(bf16[136,2176]{1,0:T(8,128)(2,1)} %get-tuple-element.222), channel_id=1, source_target_pairs={{0,8},{4,12},{8,0},{12,4},{1,9},{5,13},{9,1},{13,5},{2,10},{6,14},... | collective-permute-start | bytes 1775624 | tf_op jit(solution)/shard_map/ppermute | solution.py:400
  12.4 45.4 %collective-permute-start.9 = (bf16[136,2176]{1,0:T(8,128)(2,1)S(1)}, bf16[136,2176]{1,0:T(8,128)(2,1)S(1)}, u32[]{:S(2)}, u32[]{:S(2)}) collective-permute-start(bf16[136,2176]{1,0:T(8,128)(2,1)S(1)} %get-tuple-element.223), channel_id=1, source_target_pairs={{0,12},{4,8},{8,4},{12,0},{1,13},{5,9},{9,5},{13,1},{2,14},{6,10},... | collective-permute-start | bytes 1775624 | tf_op jit(solution)/shard_map/ppermute | solution.py:400
  18.1 12.8 %copy-start.1 = (s32[512,1]{1,0:T(8,128)}, s32[512,1]{1,0:T(8,128)S(1)}, u32[]{:S(2)}) copy-start(s32[512,1]{1,0:T(8,128)S(1)} %get-tuple-element.261.refs_0_) | copy-start | bytes 6148
  18.1 3.9 %collective-permute-start.11 = (f32[64,128]{1,0:T(8,128)S(1)}, f32[64,128]{1,0:T(8,128)S(1)}, u32[]{:S(2)}, u32[]{:S(2)}) collective-permute-start(f32[64,128]{1,0:T(8,128)S(1)} %get-tuple-element.229), channel_id=1, source_target_pairs={{0,2},{1,3},{2,0},{3,1},{4,6},{5,7},{6,4},{7,5},{8,10},{9,11},{10,... | collective-permute-start | bytes 98312 | tf_op jit(solution)/shard_map/ppermute | solution.py:400
  22.0 33.5 %collective-permute-start.12 = (f32[64,128]{1,0:T(8,128)S(1)}, f32[64,128]{1,0:T(8,128)S(1)}, u32[]{:S(2)}, u32[]{:S(2)}) collective-permute-start(f32[64,128]{1,0:T(8,128)S(1)} %add.153), channel_id=1, source_target_pairs={{0,1},{1,0},{2,3},{3,2},{4,5},{5,4},{6,7},{7,6},{8,9},{9,8},{10,11... | collective-permute-start | bytes 98312 | tf_op jit(solution)/shard_map/ppermute | solution.py:400
  22.0 8.9 %copy-start.11 = (bf16[4,128,2048]{2,1,0:T(8,128)(2,1)S(1)}, bf16[4,128,2048]{2,1,0:T(8,128)(2,1)}, u32[]{:S(2)}) copy-start(bf16[4,128,2048]{2,1,0:T(8,128)(2,1)} %param.9) | copy-start | bytes 6291460
  47.2 10.5 %copy-start.8 = (bf16[64,16,2048]{2,1,0:T(8,128)(2,1)S(1)}, bf16[64,16,2048]{2,1,0:T(8,128)(2,1)}, u32[]{:S(2)}) copy-start(bf16[64,16,2048]{2,1,0:T(8,128)(2,1)} %param.11) | copy-start | bytes 12582916
  57.8 18.6 %copy-start.5 = (bf16[64,16,2048]{2,1,0:T(8,128)(2,1)S(1)}, bf16[64,16,2048]{2,1,0:T(8,128)(2,1)}, u32[]{:S(2)}) copy-start(bf16[64,16,2048]{2,1,0:T(8,128)(2,1)} %param.12) | copy-start | bytes 12582916
  64.4 20.9 %collective-permute-start.17 = (bf16[512,2048]{1,0:T(8,128)(2,1)}, bf16[512,2048]{1,0:T(8,128)(2,1)}, u32[]{:S(2)}, u32[]{:S(2)}) collective-permute-start(bf16[512,2048]{1,0:T(8,128)(2,1)} %share.7), channel_id=1, source_target_pairs={{0,1},{1,0},{2,3},{3,2},{4,5},{5,4},{6,7},{7,6},{8,9},{9,8},{10,11... | collective-permute-start | bytes 6291464 | tf_op jit(solution)/shard_map/ppermute | solution.py:400
  64.4 25.7 %collective-permute-start.16 = (bf16[512,2048]{1,0:T(8,128)(2,1)}, bf16[512,2048]{1,0:T(8,128)(2,1)S(1)}, u32[]{:S(2)}, u32[]{:S(2)}) collective-permute-start(bf16[512,2048]{1,0:T(8,128)(2,1)} %share.5), channel_id=1, source_target_pairs={{0,1},{1,0},{2,3},{3,2},{4,5},{5,4},{6,7},{7,6},{8,9},{9,8},{10,11... | collective-permute-start | bytes 6291464 | tf_op jit(solution)/shard_map/ppermute | solution.py:400
  64.9 3.9 %collective-permute-start.14 = (f32[60,128]{1,0:T(8,128)S(1)}, f32[60,128]{1,0:T(8,128)S(1)}, u32[]{:S(2)}, u32[]{:S(2)}) collective-permute-start(f32[60,128]{1,0:T(8,128)S(1)} %get-tuple-element.243), channel_id=1, source_target_pairs={{0,2},{1,3},{2,0},{3,1},{4,6},{5,7},{6,4},{7,5},{8,10},{9,11},{10,... | collective-permute-start | bytes 92168 | tf_op jit(solution)/shard_map/ppermute | solution.py:400
  68.8 7.5 %collective-permute-start.15 = (f32[60,128]{1,0:T(8,128)S(1)}, f32[60,128]{1,0:T(8,128)S(1)}, u32[]{:S(2)}, u32[]{:S(2)}) collective-permute-start(f32[60,128]{1,0:T(8,128)S(1)} %add.155), channel_id=1, source_target_pairs={{0,1},{1,0},{2,3},{3,2},{4,5},{5,4},{6,7},{7,6},{8,9},{9,8},{10,11... | collective-permute-start | bytes 92168 | tf_op jit(solution)/shard_map/ppermute | solution.py:400
  69.7 20.4 %collective-permute-start.13 = (bf16[128,2176]{1,0:T(8,128)(2,1)}, bf16[128,2176]{1,0:T(8,128)(2,1)}, u32[]{:S(2)}, u32[]{:S(2)}) collective-permute-start(bf16[128,2176]{1,0:T(8,128)(2,1)} %pad_maximum_fusion), channel_id=1, source_target_pairs={{0,4},{4,0},{8,12},{12,8},{1,5},{5,1},{9,13},{13,9},{2,6},{6,2},{1... | collective-permute-start | bytes 1671176 | tf_op jit(solution)/shard_map/ppermute | solution.py:400
  81.4 33.1 %all-to-all-start = ((bf16[4,72,2048]{2,1,0:T(8,128)(2,1)}), bf16[4,72,2048]{2,1,0:T(8,128)(2,1)S(1)}, u32[]{:S(2)}, u32[]{:S(2)}) async-start(bf16[4,72,2048]{2,1,0:T(8,128)(2,1)} %get-tuple-element.247), calls=%async_computation | async-start | bytes 2359296 | tf_op jit(solution)/shard_map/all_to_all | solution.py:419
  85.3 4.9 %copy-start.9 = (bf16[64,16,2048]{2,1,0:T(8,128)(2,1)S(1)}, bf16[64,16,2048]{2,1,0:T(8,128)(2,1)}, u32[]{:S(2)}) copy-start(bf16[64,16,2048]{2,1,0:T(8,128)(2,1)} %param.11) | copy-start | bytes 12582916
  90.2 11.3 %copy-start.6 = (bf16[64,16,2048]{2,1,0:T(8,128)(2,1)S(1)}, bf16[64,16,2048]{2,1,0:T(8,128)(2,1)}, u32[]{:S(2)}) copy-start(bf16[64,16,2048]{2,1,0:T(8,128)(2,1)} %param.12) | copy-start | bytes 12582916
  95.2 3.7 %collective-permute-start.18 = (f32[16,128]{1,0:T(8,128)S(1)}, f32[16,128]{1,0:T(8,128)S(1)}, u32[]{:S(2)}, u32[]{:S(2)}) collective-permute-start(f32[16,128]{1,0:T(8,128)S(1)} %get-tuple-element.254), channel_id=1, source_target_pairs={{0,2},{1,3},{2,0},{3,1},{4,6},{5,7},{6,4},{7,5},{8,10},{9,11},{10,... | collective-permute-start | bytes 24584 | tf_op jit(solution)/shard_map/ppermute | solution.py:400
  98.8 1.2 collective-permute-start.19
  100.0 51.0 %collective-permute-start.24 = (bf16[512,2048]{1,0:T(8,128)(2,1)}, bf16[512,2048]{1,0:T(8,128)(2,1)}, u32[]{:S(2)}, u32[]{:S(2)}) collective-permute-start(bf16[512,2048]{1,0:T(8,128)(2,1)} %add_convert_fusion.1), channel_id=1, source_target_pairs={{0,2},{1,3},{2,0},{3,1},{4,6},{5,7},{6,4},{7,5},{8,10},{9,11},{10,... | collective-permute-start | bytes 6291464 | tf_op jit(solution)/shard_map/ppermute | solution.py:400
  104.4 24.3 %collective-permute-start.20 = (bf16[128,2048]{1,0:T(8,128)(2,1)}, bf16[128,2048]{1,0:T(8,128)(2,1)}, u32[]{:S(2)}, u32[]{:S(2)}) collective-permute-start(bf16[128,2048]{1,0:T(8,128)(2,1)} %deltas.8), channel_id=1, source_target_pairs={{0,4},{4,0},{8,12},{12,8},{1,5},{5,1},{9,13},{13,9},{2,6},{6,2},{1... | collective-permute-start | bytes 1572872 | tf_op jit(solution)/shard_map/ppermute | solution.py:400
  114.5 24.7 %collective-permute-start.23 = (bf16[136,2048]{1,0:T(8,128)(2,1)}, bf16[136,2048]{1,0:T(8,128)(2,1)}, u32[]{:S(2)}, u32[]{:S(2)}) collective-permute-start(bf16[136,2048]{1,0:T(8,128)(2,1)} %get-tuple-element.269), channel_id=1, source_target_pairs={{0,4},{4,0},{8,12},{12,8},{1,5},{5,1},{9,13},{13,9},{2,6},{6,2},{1... | collective-permute-start | bytes 1671176 | tf_op jit(solution)/shard_map/ppermute | solution.py:400
  114.5 1.0 copy-start.2
  116.2 6.7 %copy-start = (bf16[512,2048]{1,0:T(8,128)(2,1)S(1)}, bf16[512,2048]{1,0:T(8,128)(2,1)}, u32[]{:S(2)}) copy-start(bf16[512,2048]{1,0:T(8,128)(2,1)} %share.4.refs_1_) | copy-start | bytes 6291460
  122.9 5.7 %copy-start.15 = (bf16[64,2048]{1,0:T(8,128)(2,1)S(1)}, bf16[64,2048]{1,0:T(8,128)(2,1)}, u32[]{:S(2)}) copy-start(bf16[64,2048]{1,0:T(8,128)(2,1)} %get-tuple-element.266) | copy-start | bytes 786436
  122.9 5.7 %copy-start.16 = (bf16[64,2048]{1,0:T(8,128)(2,1)S(1)}, bf16[64,2048]{1,0:T(8,128)(2,1)}, u32[]{:S(2)}) copy-start(bf16[64,2048]{1,0:T(8,128)(2,1)} %get-tuple-element.268) | copy-start | bytes 786436
  129.8 21.2 %collective-permute-start.21 = (bf16[64,2048]{1,0:T(8,128)(2,1)S(1)}, bf16[64,2048]{1,0:T(8,128)(2,1)S(1)}, u32[]{:S(2)}, u32[]{:S(2)}) collective-permute-start(bf16[64,2048]{1,0:T(8,128)(2,1)S(1)} %get-tuple-element.311), channel_id=1, source_target_pairs={{0,8},{4,12},{8,0},{12,4},{1,9},{5,13},{9,1},{13,5},{2,10},{6,14},... | collective-permute-start | bytes 786440 | tf_op jit(solution)/shard_map/ppermute | solution.py:400
  131.8 19.2 %collective-permute-start.22 = (bf16[64,2048]{1,0:T(8,128)(2,1)S(1)}, bf16[64,2048]{1,0:T(8,128)(2,1)S(1)}, u32[]{:S(2)}, u32[]{:S(2)}) collective-permute-start(bf16[64,2048]{1,0:T(8,128)(2,1)S(1)} %get-tuple-element.310), channel_id=1, source_target_pairs={{0,12},{4,8},{8,4},{12,0},{1,13},{5,9},{9,5},{13,1},{2,14},{6,10},... | collective-permute-start | bytes 786440 | tf_op jit(solution)/shard_map/ppermute | solution.py:400
  134.3 3.7 %collective-permute-start.25 = (s32[1,1]{1,0:T(1,128)}, s32[1,1]{1,0:T(1,128)}, u32[]{:S(2)}, u32[]{:S(2)}) collective-permute-start(s32[1,1]{1,0:T(1,128)} %get-tuple-element.233.refs_1_), channel_id=1, source_target_pairs={{0,16},{16,0},{1,17},{17,1},{2,18},{18,2},{3,19},{19,3},{4,20},{20... | collective-permute-start | bytes 20 | tf_op jit(solution)/shard_map/ppermute | solution.py:400
  139.2 17.7 %copy-start.14 = (bf16[512,128]{1,0:T(8,128)(2,1)S(1)}, bf16[512,128]{1,0:T(8,128)(2,1)}, u32[]{:S(2)}) copy-start(bf16[512,128]{1,0:T(8,128)(2,1)} %get-tuple-element.413) | copy-start | bytes 393220
  139.2 17.7 %copy-start.17 = (s32[2,32]{1,0:T(2,128)S(1)}, s32[2,32]{1,0:T(2,128)}, u32[]{:S(2)}) copy-start(s32[2,32]{1,0:T(2,128)} %get-tuple-element.411) | copy-start | bytes 772
  (2 other events, 1.4 us)
